TPU v7x, 128 devices: a whole 4x4x4 slice. The times are simulated.
128 devices in a mesh: seq: 32 (over z, y, core), chan: 4 (over x).
Axes of the slice: x: 4, y: 4, z: 4, core: 2. Of those that a mesh axis runs over, the one named last changes fastest.
Arguments:
- gate_in: bfloat16 [8192, 8192], P('seq', 'chan'), may hold values from -6 to 6
- key_in: bfloat16 [8192, 8192], P('seq', 'chan'), may hold values from -6 to 6
- value_in: bfloat16 [8192, 8192], P('seq', 'chan'), may hold values from -6 to 6
- conv_out: bfloat16 [8192, 8192], P('seq', 'chan'), may hold values from -6 to 6
- cotangent: bfloat16 [8192, 8192], P('seq', 'chan'), may hold values from -6 to 6
- long_filter: float32 [8192, 8192], P('seq', 'chan'), may hold values from -1.05 to 1.05
- key_taps: float32 [3, 8192], P(None, 'chan'), may hold values from -3 to 3
- value_taps: float32 [3, 8192], P(None, 'chan'), may hold values from -3 to 3
Outputs:
- gate_grad: bfloat16 [8192, 8192], P('seq', 'chan')
- key_grad: bfloat16 [8192, 8192], P('seq', 'chan')
- value_grad: bfloat16 [8192, 8192], P('seq', 'chan')
- filter_grad: float32 [8192, 8192], P('seq', 'chan')
- key_taps_grad: float32 [3, 8192], P(None, 'chan')
- value_taps_grad: float32 [3, 8192], P(None, 'chan')
All inputs are finite; a program needn't handle non-finite values.
Results may differ from a plain program's by a relative error of at most 0.0065.
Values may be sent and summed in bfloat16 or wider, within the bound.
No kernel may reach another device: no remote copies, remote signals or barrier semaphores. Data moves between devices by JAX's collectives and lax.ppermute only.
A program may use at most 192 MiB of HBM per device.

v0:
```python
import math

import jax
import jax.numpy as jnp
from jax import lax
from jax.sharding import PartitionSpec as P


def split_sizes(length):
    total = 2 * length
    factor = 1
    for candidate in range(1, length + 1):
        if length % candidate == 0 and candidate * candidate <= total:
            factor = candidate
    return (factor, total // factor)


def phase_table(first, second, modulus):
    left = jnp.arange(first, dtype=jnp.int32)[:, None]
    right = jnp.arange(second, dtype=jnp.int32)[None, :]
    angle = (left * right % modulus).astype(jnp.float32) * (2.0 * math.pi / modulus)
    return (jnp.cos(angle), jnp.sin(angle))


def contract(form, left, right):
    return jnp.einsum(form, left, right, precision=lax.Precision.HIGHEST)


def forward_spectrum(signal, size_a, size_b):
    chans = signal.shape[0]
    half = size_b // 2
    cos_b, sin_b = phase_table(size_b, half, size_b)
    cos_w, sin_w = phase_table(size_b, size_a, size_a * size_b)
    cos_a, sin_a = phase_table(size_a, size_a, size_a)
    blocks = signal.reshape(chans, half, size_a)
    real_y = contract("kb,cba->cka", cos_b, blocks)
    imag_y = -contract("kb,cba->cka", sin_b, blocks)
    real_t = real_y * cos_w + imag_y * sin_w
    imag_t = imag_y * cos_w - real_y * sin_w
    real_x = contract("ckn,jn->ckj", real_t, cos_a) + contract("ckn,jn->ckj", imag_t, sin_a)
    imag_x = contract("ckn,jn->ckj", imag_t, cos_a) - contract("ckn,jn->ckj", real_t, sin_a)
    return (real_x, imag_x)


def inverse_real(real_x, imag_x, size_a, size_b):
    chans = real_x.shape[0]
    half = size_b // 2
    cos_b, sin_b = phase_table(size_b, half, size_b)
    cos_w, sin_w = phase_table(size_b, size_a, size_a * size_b)
    cos_a, sin_a = phase_table(size_a, size_a, size_a)
    real_z = contract("ckj,nj->ckn", real_x, cos_a) - contract("ckj,nj->ckn", imag_x, sin_a)
    imag_z = contract("ckj,nj->ckn", real_x, sin_a) + contract("ckj,nj->ckn", imag_x, cos_a)
    real_u = real_z * cos_w - imag_z * sin_w
    imag_u = real_z * sin_w + imag_z * cos_w
    result = contract("kb,cka->cba", cos_b, real_u) - contract("kb,cka->cba", sin_b, imag_u)
    return result.reshape(chans, half * size_a) / (size_a * size_b)


def long_backward(grad_cols, mixed_cols, filter_cols):
    chans, length = filter_cols.shape
    size_a, size_b = split_sizes(length)
    signals = jnp.concatenate(
        [grad_cols.astype(jnp.float32), mixed_cols.astype(jnp.float32), filter_cols], 0
    )
    real_s, imag_s = forward_spectrum(signals, size_a, size_b)
    real_g, imag_g = (real_s[:chans], imag_s[:chans])
    real_m, imag_m = (real_s[chans : 2 * chans], imag_s[chans : 2 * chans])
    real_f, imag_f = (real_s[2 * chans :], imag_s[2 * chans :])
    real_out = jnp.concatenate(
        [real_f * real_g + imag_f * imag_g, real_g * real_m + imag_g * imag_m], 0
    )
    imag_out = jnp.concatenate(
        [real_f * imag_g - imag_f * real_g, imag_g * real_m - real_g * imag_m], 0
    )
    both = inverse_real(real_out, imag_out, size_a, size_b)
    return (both[:chans], both[chans:])


def causal_mix(padded, taps, axis, count):
    width = taps.shape[0]
    total = 0.0
    for offset in range(width):
        start = width - 1 - offset
        total = total + taps[offset] * lax.slice_in_dim(padded, start, start + count, axis=axis)
    return total


def reverse_mix(padded, taps, axis, count):
    width = taps.shape[0]
    total = 0.0
    for offset in range(width):
        total = total + taps[offset] * lax.slice_in_dim(padded, offset, offset + count, axis=axis)
    return total


def taps_terms(grad, padded, width, axis, count):
    terms = []
    for offset in range(width):
        start = width - 1 - offset
        terms.append(
            jnp.sum(grad * lax.slice_in_dim(padded, start, start + count, axis=axis), axis=axis)
        )
    return jnp.stack(terms, axis=0)


def clip_factor(grad_h):
    count = grad_h.shape[0] * grad_h.shape[1] * lax.axis_size("seq") * lax.axis_size("chan")
    total = lax.psum(jnp.sum(grad_h * grad_h), ("seq", "chan"))
    return jnp.minimum(1.0, 1.0 / jnp.sqrt(total / count + 1e-06))


def shards(gate_in, key_in, value_in, conv_out, cotangent, long_filter, key_taps, value_taps):
    width = key_taps.shape[0]
    cot_f = cotangent.astype(jnp.float32)
    grad_mix = (cot_f * gate_in.astype(jnp.float32)).astype(jnp.bfloat16)
    gate_grad = (cot_f * conv_out.astype(jnp.float32)).astype(jnp.bfloat16)
    filter_cols = lax.all_to_all(long_filter, "seq", split_axis=1, concat_axis=0, tiled=True).T
    grad_c, key_c, value_c = (
        lax.all_to_all(grad_mix, "seq", split_axis=1, concat_axis=0, tiled=True),
        lax.all_to_all(key_in, "seq", split_axis=1, concat_axis=0, tiled=True),
        lax.all_to_all(value_in, "seq", split_axis=1, concat_axis=0, tiled=True),
    )
    grad_c, key_c, value_c = (grad_c.T, key_c.T, value_c.T)
    chans, length = key_c.shape
    start = lax.axis_index("seq") * chans
    key_part = lax.dynamic_slice_in_dim(key_taps, start, chans, 1)[:, :, None]
    value_part = lax.dynamic_slice_in_dim(value_taps, start, chans, 1)[:, :, None]
    key_pad = jnp.pad(key_c.astype(jnp.float32), ((0, 0), (width - 1, 0)))
    value_pad = jnp.pad(value_c.astype(jnp.float32), ((0, 0), (width - 1, 0)))
    key_short = causal_mix(key_pad, key_part, 1, length)
    value_short = causal_mix(value_pad, value_part, 1, length)
    mixed = (key_short * value_short).astype(jnp.bfloat16)
    grad_z, grad_h = long_backward(grad_c, mixed, filter_cols)
    grad_key_short = grad_z * value_short
    grad_value_short = grad_z * key_short
    key_after = jnp.pad(grad_key_short, ((0, 0), (0, width - 1)))
    value_after = jnp.pad(grad_value_short, ((0, 0), (0, width - 1)))
    key_cols = reverse_mix(key_after, key_part, 1, length).astype(jnp.bfloat16)
    value_cols = reverse_mix(value_after, value_part, 1, length).astype(jnp.bfloat16)
    key_terms = taps_terms(grad_key_short, key_pad, width, 1, length)
    value_terms = taps_terms(grad_value_short, value_pad, width, 1, length)
    key_grad, value_grad = (
        lax.all_to_all(key_cols.T, "seq", split_axis=0, concat_axis=1, tiled=True),
        lax.all_to_all(value_cols.T, "seq", split_axis=0, concat_axis=1, tiled=True),
    )
    key_taps_grad, value_taps_grad = (
        lax.all_gather(key_terms, "seq", axis=1, tiled=True),
        lax.all_gather(value_terms, "seq", axis=1, tiled=True),
    )
    scale = clip_factor(grad_h)
    filter_grad = lax.all_to_all((grad_h * scale).T, "seq", split_axis=0, concat_axis=1, tiled=True)
    return (gate_grad, key_grad, value_grad, filter_grad, key_taps_grad, value_taps_grad)


def solution(mesh):
    return jax.shard_map(
        shards,
        mesh=mesh,
        in_specs=(
            P("seq", "chan"),
            P("seq", "chan"),
            P("seq", "chan"),
            P("seq", "chan"),
            P("seq", "chan"),
            P("seq", "chan"),
            P(None, "chan"),
            P(None, "chan"),
        ),
        out_specs=(
            P("seq", "chan"),
            P("seq", "chan"),
            P("seq", "chan"),
            P("seq", "chan"),
            P(None, "chan"),
            P(None, "chan"),
        ),
        check_vma=False,
    )
```

profile of v0, /device:TPU:0, one launch (start us, length us, event | category | flops | bytes accessed | tf_op | source)
XLA Modules:
  0.0 540.1 jit_solution(6094465058913384012)
XLA Ops:
  3.1 8.4 %all-to-all-start.1 = ((bf16[256,32,64]{0,2,1:T(8,128)(2,1)}), bf16[256,32,64]{0,2,1:T(8,128)(2,1)S(1)}, u32[]{:S(2)}, u32[]{:S(2)}) async-start(bf16[256,32,64]{0,2,1:T(8,128)(2,1)} %bitcast.4), calls=%async_computation.1 | async-start | bytes 2097152 | tf_op jit(solution)/shard_map/all_to_all | solution.py:120
  12.8 16.0 %all-to-all-done.1 = bf16[256,32,64]{0,2,1:T(8,128)(2,1)S(1)} async-done(((bf16[256,32,64]{0,2,1:T(8,128)(2,1)}), bf16[256,32,64]{0,2,1:T(8,128)(2,1)S(1)}, u32[]{:S(2)}, u32[]{:S(2)}) %all-to-all-start.1) | async-done | bytes 1048608 | tf_op jit(solution)/shard_map/all_to_all | solution.py:120
  58.3 13.8 %all-to-all-done = bf16[256,32,64]{0,2,1:T(8,128)(2,1)} async-done(((bf16[256,32,64]{0,2,1:T(8,128)(2,1)}), bf16[256,32,64]{0,2,1:T(8,128)(2,1)}, u32[]{:S(2)}, u32[]{:S(2)}) %all-to-all-start) | async-done | bytes 1048608 | tf_op jit(solution)/shard_map/all_to_all | solution.py:119
  72.1 5.3 all-to-all-start.3
  80.6 5.2 fusion.32
  85.7 21.1 %all-to-all-done.3 = f32[256,32,64]{0,2,1:T(8,128)} async-done(((f32[256,32,64]{0,2,1:T(8,128)}), f32[256,32,64]{0,2,1:T(8,128)}, u32[]{:S(2)}, u32[]{:S(2)}) %all-to-all-start.3) | async-done | bytes 2097184 | tf_op jit(solution)/shard_map/all_to_all | solution.py:117
  113.5 21.1 %fusion.56 = f32[192,128,128]{2,1,0:T(8,128)S(1)} fusion(f32[192,64,128]{2,1,0:T(8,128)S(1)} %bitcast.152), kind=kOutput, calls=%fused_computation.101 | convolution fusion | flops 2416033792 | bytes 18874368 | tf_op jit(solution)/shard_map/kb,cba->cka/dot_general | solution.py:26
  134.6 22.2 %fusion.59 = f32[192,128,128]{2,1,0:T(8,128)S(1)} fusion(f32[192,64,128]{2,1,0:T(8,128)} %bitcast.153), kind=kOutput, calls=%fused_computation.104 | convolution fusion | flops 2416033792 | bytes 18874368 | tf_op jit(solution)/shard_map/kb,cba->cka/dot_general | solution.py:26
  156.8 23.5 %fusion.22 = f32[192,128,128]{2,1,0:T(8,128)} fusion(f32[192,128,128]{2,1,0:T(8,128)S(1)} %fusion.59, f32[192,128,128]{2,1,0:T(8,128)S(1)} %fusion.56, f32[128,128]{0,1:T(8,128)S(1)} %copy.81, f32[128,128]{0,1:T(8,128)S(1)} %copy.80), kind=kOutput, calls=%fused_computation.36 | convolution fusion | flops 4844650496 | bytes 37879808 | tf_op jit(solution)/shard_map/ckn,jn->ckj/dot_general | solution.py:26
  180.4 23.2 %fusion.26 = f32[192,128,128]{2,1,0:T(8,128)} fusion(f32[192,128,128]{2,1,0:T(8,128)S(1)} %fusion.59, f32[192,128,128]{2,1,0:T(8,128)S(1)} %fusion.56, f32[128,128]{0,1:T(8,128)S(1)} %copy.81, f32[128,128]{0,1:T(8,128)S(1)} %copy.80), kind=kOutput, calls=%fused_computation.37 | convolution fusion | flops 4844650496 | bytes 37879808 | tf_op jit(solution)/shard_map/ckn,jn->ckj/dot_general | solution.py:26
  203.5 26.5 %convolution_subtract_fusion = f32[192,128,128]{2,1,0:T(8,128)} fusion(f32[192,128,128]{2,1,0:T(8,128)} %fusion.22, f32[192,128,128]{2,1,0:T(8,128)} %copy-done, f32[192,128,128]{2,1,0:T(8,128)S(1)} %fusion.56, f32[128,128]{0,1:T(8,128)S(1)} %copy.81, f32[128,128]{0,1:T(8,128)S(1)} %copy.80), kind=kOutput, calls=%fused_computation.21 | convolution fusion | flops 4847796224 | bytes 50462720 | tf_op jit(solution)/shard_map/ckn,jn->ckj/dot_general | solution.py:26
  230.0 26.1 %convolution_add_fusion = f32[192,128,128]{2,1,0:T(8,128)} fusion(f32[192,128,128]{2,1,0:T(8,128)} %fusion.26, f32[192,128,128]{2,1,0:T(8,128)} %copy-done, f32[192,128,128]{2,1,0:T(8,128)S(1)} %fusion.56, f32[128,128]{0,1:T(8,128)S(1)} %copy.81, f32[128,128]{0,1:T(8,128)S(1)} %copy.80), kind=kOutput, calls=%fused_computation.22 | convolution fusion | flops 4847796224 | bytes 50462720 | tf_op jit(solution)/shard_map/ckn,jn->ckj/dot_general | solution.py:26
  256.1 15.5 %multiply_subtract_fusion.1 = (f32[64,128,128]{2,1,0:T(8,128)}, f32[64,128,128]{2,1,0:T(8,128)}, f32[64,128,128]{2,1,0:T(8,128)S(1)}, f32[64,128,128]{2,1,0:T(8,128)}) fusion(f32[192,128,128]{2,1,0:T(8,128)} %convolution_subtract_fusion, f32[192,128,128]{2,1,0:T(8,128)} %convolution_add_fusion), kind=kLoop, calls=%fused_computation.29 | loop fusion | flops 12582912 | bytes 41943040 | tf_op jit(solution)/shard_map/sub | solution.py:73
  271.7 10.2 %fusion.10 = f32[128,128,128]{2,1,0:T(8,128)S(1)} fusion(f32[64,128,128]{2,1,0:T(8,128)} %get-tuple-element.36, f32[64,128,128]{2,1,0:T(8,128)} %get-tuple-element.35), kind=kOutput, calls=%fused_computation.16 | convolution fusion | flops 3223552000 | bytes 16777216 | tf_op jit(solution)/shard_map/ckj,nj->ckn/dot_general | solution.py:26
  281.9 9.3 %fusion.11 = f32[128,128,128]{2,1,0:T(8,128)} fusion(f32[64,128,128]{2,1,0:T(8,128)S(1)} %copy-done.4, f32[64,128,128]{2,1,0:T(8,128)S(1)} %copy-done.3), kind=kOutput, calls=%fused_computation.17 | convolution fusion | flops 3223552000 | bytes 16777216 | tf_op jit(solution)/shard_map/ckj,nj->ckn/dot_general | solution.py:26
  291.3 9.4 %fusion.12 = f32[128,128,128]{2,1,0:T(8,128)} fusion(f32[64,128,128]{2,1,0:T(8,128)S(1)} %get-tuple-element.37, f32[64,128,128]{2,1,0:T(8,128)S(1)} %copy-done.2), kind=kOutput, calls=%fused_computation.18 | convolution fusion | flops 3223552000 | bytes 16777216 | tf_op jit(solution)/shard_map/ckj,nj->ckn/dot_general | solution.py:26
  300.7 9.3 %fusion.13 = f32[128,128,128]{2,1,0:T(8,128)} fusion(f32[64,128,128]{2,1,0:T(8,128)S(1)} %get-tuple-element.37, f32[64,128,128]{2,1,0:T(8,128)S(1)} %copy-done.2), kind=kOutput, calls=%fused_computation.19 | convolution fusion | flops 3223552000 | bytes 16777216 | tf_op jit(solution)/shard_map/ckj,nj->ckn/dot_general | solution.py:26
  310.0 12.9 %fusion.2 = f32[128,128,64]{1,2,0:T(8,128)} fusion(f32[128,128]{1,0:T(8,128)S(1)} %get-tuple-element.55, f32[128,128]{1,0:T(8,128)S(1)} %get-tuple-element.56, f32[128,128,128]{2,1,0:T(8,128)} %fusion.12, f32[128,128,128]{2,1,0:T(8,128)S(1)} %fusion.10, f32[128,128,128]{2,1,0:T(8,128)} %fusion.13, f32[128,128,128]{2,1,0:T(8,128)} %fusion.11), kind=kOutput, calls=%fused_computation.8 | convolution fusion | flops 1621213184 | bytes 37879808 | tf_op jit(solution)/shard_map/kb,cka->cba/dot_general | solution.py:26
  322.9 14.4 %multiply_bitcast_fusion = f32[128,64,128]{2,1,0:T(8,128)} fusion(f32[128,128,64]{1,2,0:T(8,128)} %fusion.2, f32[128,128]{1,0:T(8,128)S(1)} %get-tuple-element.55, f32[128,128]{1,0:T(8,128)S(1)} %get-tuple-element.56, f32[128,128,128]{2,1,0:T(8,128)} %fusion.12, f32[128,128,128]{2,1,0:T(8,128)S(1)} %fusion.10, f32[128,128,128]{2,1,0:T(8,128)} %fusion.13, ...), kind=kOutput, calls=%fused_computation.23 | convolution fusion | flops 1623310336 | bytes 42074112 | tf_op jit(solution)/shard_map/kb,cka->cba/dot_general | solution.py:26
  340.1 63.4 %psum.7 = f32[]{:T(128)} all-reduce(f32[]{:T(128)} %multiply_reduce_fusion.6), channel_id=1, replica_groups=mesh['seq'=32,'chan'=4] {'seq','chan'}, use_global_device_ids=true, to_apply=%region_1.2 | all-reduce | flops 1 | bytes 8 | tf_op jit(solution)/shard_map/psum | solution.py:108
  423.1 15.0 %all-to-all-done.5 = bf16[32,256,64]{1,2,0:T(8,128)(2,1)} async-done(((bf16[32,256,64]{1,2,0:T(8,128)(2,1)}), bf16[32,256,64]{1,2,0:T(8,128)(2,1)}, u32[]{:S(2)}, u32[]{:S(2)}) %all-to-all-start.5) | async-done | bytes 1048608 | tf_op jit(solution)/shard_map/all_to_all | solution.py:144
  445.5 14.5 %all-to-all-done.4 = bf16[32,256,64]{1,2,0:T(8,128)(2,1)} async-done(((bf16[32,256,64]{1,2,0:T(8,128)(2,1)}), bf16[32,256,64]{1,2,0:T(8,128)(2,1)}, u32[]{:S(2)}, u32[]{:S(2)}) %all-to-all-start.4) | async-done | bytes 1048608 | tf_op jit(solution)/shard_map/all_to_all | solution.py:143
  465.8 42.5 %all-gather = f32[32,64,3]{1,2,0:T(4,128)S(1)} all-gather(f32[1,64,3]{1,2,0:T(4,128)S(1)} %maximum_bitcast_fusion.1), channel_id=1, replica_groups=mesh['seq'=32,'chan'=4] {'seq'}, dimensions={0}, use_global_device_ids=true | all-gather | bytes 25344 | tf_op jit(solution)/shard_map/all_gather | solution.py:147
  509.1 23.7 %all-gather.1 = f32[32,64,3]{1,2,0:T(4,128)S(1)} all-gather(f32[1,64,3]{1,2,0:T(4,128)S(1)} %maximum_bitcast_fusion.2), channel_id=1, replica_groups=mesh['seq'=32,'chan'=4] {'seq'}, dimensions={0}, use_global_device_ids=true | all-gather | bytes 25344 | tf_op jit(solution)/shard_map/all_gather | solution.py:148
  (84 shorter events, 85.4 us)
Async XLA Ops:
  0.6 10.9 %copy-start.16 = (bf16[256,2048]{1,0:T(8,128)(2,1)S(1)}, bf16[256,2048]{1,0:T(8,128)(2,1)}, u32[]{:S(2)}) copy-start(bf16[256,2048]{1,0:T(8,128)(2,1)} %param.10) | copy-start | bytes 3145732
  0.6 32.6 %copy-start.17 = (bf16[256,2048]{1,0:T(8,128)(2,1)S(1)}, bf16[256,2048]{1,0:T(8,128)(2,1)}, u32[]{:S(2)}) copy-start(bf16[256,2048]{1,0:T(8,128)(2,1)} %param.8) | copy-start | bytes 3145732
  3.1 25.8 %all-to-all-start.1 = ((bf16[256,32,64]{0,2,1:T(8,128)(2,1)}), bf16[256,32,64]{0,2,1:T(8,128)(2,1)S(1)}, u32[]{:S(2)}, u32[]{:S(2)}) async-start(bf16[256,32,64]{0,2,1:T(8,128)(2,1)} %bitcast.4), calls=%async_computation.1 | async-start | bytes 2097152 | tf_op jit(solution)/shard_map/all_to_all | solution.py:120
  28.8 21.3 %all-to-all-start.2 = ((bf16[256,32,64]{0,2,1:T(8,128)(2,1)}), bf16[256,32,64]{0,2,1:T(8,128)(2,1)S(1)}, u32[]{:S(2)}, u32[]{:S(2)}) async-start(bf16[256,32,64]{0,2,1:T(8,128)(2,1)} %bitcast.10), calls=%async_computation.2 | async-start | bytes 2097152 | tf_op jit(solution)/shard_map/all_to_all | solution.py:121
  50.1 4.7 copy-start.14
  50.1 22.0 %all-to-all-start = ((bf16[256,32,64]{0,2,1:T(8,128)(2,1)}), bf16[256,32,64]{0,2,1:T(8,128)(2,1)}, u32[]{:S(2)}, u32[]{:S(2)}) async-start(bf16[256,32,64]{0,2,1:T(8,128)(2,1)} %bitcast.167), calls=%async_computation | async-start | bytes 2097152 | tf_op jit(solution)/shard_map/all_to_all | solution.py:119
  56.3 24.3 %copy-start.5 = (f32[32,8,8,256]{3,2,0,1:T(8,128)}, f32[32,8,8,256]{3,2,0,1:T(8,128)S(1)}, u32[]{:S(2)}) copy-start(f32[32,8,8,256]{3,2,0,1:T(8,128)S(1)} %copy.103) | copy-start | bytes 6291460
  72.1 34.7 %all-to-all-start.3 = ((f32[256,32,64]{0,2,1:T(8,128)}), f32[256,32,64]{0,2,1:T(8,128)}, u32[]{:S(2)}, u32[]{:S(2)}) async-start(f32[256,32,64]{0,2,1:T(8,128)} %bitcast.160), calls=%async_computation.3 | async-start | bytes 4194304 | tf_op jit(solution)/shard_map/all_to_all | solution.py:117
  77.4 3.2 copy-start.7
  85.7 23.0 %copy-start.12 = (f32[32,8,8,256]{3,2,0,1:T(8,128)S(1)}, f32[32,8,8,256]{3,2,0,1:T(8,128)}, u32[]{:S(2)}) copy-start(f32[32,8,8,256]{3,2,0,1:T(8,128)} %copy.102) | copy-start | bytes 6291460
  106.8 2.2 copy-start.13
  110.8 2.7 copy-start.1
  156.8 23.5 %copy-start = (f32[192,128,128]{2,1,0:T(8,128)}, f32[192,128,128]{2,1,0:T(8,128)S(1)}, u32[]{:S(2)}) copy-start(f32[192,128,128]{2,1,0:T(8,128)S(1)} %fusion.59) | copy-start | bytes 37748740
  271.7 10.2 %copy-start.3 = (f32[64,128,128]{2,1,0:T(8,128)S(1)}, f32[64,128,128]{2,1,0:T(8,128)}, u32[]{:S(2)}) copy-start(f32[64,128,128]{2,1,0:T(8,128)} %get-tuple-element.35) | copy-start | bytes 12582916
  271.7 10.2 %copy-start.4 = (f32[64,128,128]{2,1,0:T(8,128)S(1)}, f32[64,128,128]{2,1,0:T(8,128)}, u32[]{:S(2)}) copy-start(f32[64,128,128]{2,1,0:T(8,128)} %get-tuple-element.36) | copy-start | bytes 12582916
  281.9 9.4 %copy-start.2 = (f32[64,128,128]{2,1,0:T(8,128)S(1)}, f32[64,128,128]{2,1,0:T(8,128)}, u32[]{:S(2)}) copy-start(f32[64,128,128]{2,1,0:T(8,128)} %get-tuple-element.38) | copy-start | bytes 12582916
  404.2 4.4 copy-start.6
  404.2 4.4 copy-start.8
  404.2 4.4 copy-start.9
  404.2 5.5 %copy-start.10 = (f32[64,8192]{1,0:T(8,128)S(1)}, f32[64,8192]{1,0:T(8,128)}, u32[]{:S(2)}) copy-start(f32[64,8192]{1,0:T(8,128)} %get-tuple-element.34) | copy-start | bytes 6291460
  416.1 22.0 %all-to-all-start.5 = ((bf16[32,256,64]{1,2,0:T(8,128)(2,1)}), bf16[32,256,64]{1,2,0:T(8,128)(2,1)}, u32[]{:S(2)}, u32[]{:S(2)}) async-start(bf16[32,256,64]{1,2,0:T(8,128)(2,1)} %bitcast.169), calls=%async_computation.5 | async-start | bytes 2097152 | tf_op jit(solution)/shard_map/all_to_all | solution.py:144
  422.0 20.8 %copy-start.11 = (f32[64,64,128]{2,1,0:T(8,128)S(1)}, f32[64,64,128]{2,1,0:T(8,128)}, u32[]{:S(2)}) copy-start(f32[64,64,128]{2,1,0:T(8,128)} %get-tuple-element.39) | copy-start | bytes 6291460
  438.1 22.0 %all-to-all-start.4 = ((bf16[32,256,64]{1,2,0:T(8,128)(2,1)}), bf16[32,256,64]{1,2,0:T(8,128)(2,1)}, u32[]{:S(2)}, u32[]{:S(2)}) async-start(bf16[32,256,64]{1,2,0:T(8,128)(2,1)} %bitcast.168), calls=%async_computation.4 | async-start | bytes 2097152 | tf_op jit(solution)/shard_map/all_to_all | solution.py:143
  460.1 78.0 %all-to-all-start.6 = ((f32[32,256,64]{1,2,0:T(8,128)}), f32[32,256,64]{1,2,0:T(8,128)S(1)}, u32[]{:S(2)}, u32[]{:S(2)}) async-start(f32[32,256,64]{1,2,0:T(8,128)} %bitcast.149), calls=%async_computation.6 | async-start | bytes 4194304 | tf_op jit(solution)/shard_map/all_to_all | solution.py:151
  (1 other events, 1.2 us)
where the time goes:
time: 546 us; the launch traced here: 540 us
  matrix products  208 us (38%)
  blocking collectives  130 us (24%)
  waiting for transfers between devices  84.4 us (15%)
  other arithmetic  40.6 us (7%)
  local copies, waits for them, and re-layouts  39.2 us (7%)
  starting transfers between devices  36 us (7%)
    dot_general x12, matrix products, contract(): return jnp.einsum(form, left, right, precision=lax.Precision.HIGHEST)  208 us
    psum x1, blocking collectives, clip_factor(): total = lax.psum(jnp.sum(grad_h * grad_h), ('seq', 'chan'))  63.4 us
    all_gather x1, blocking collectives, shards(): lax.all_gather(key_terms, 'seq', axis=1, tiled=True)  42.5 us
    unnamed x50, local copies, waits for them, and re-layouts  29.1 us
    all_gather x1, blocking collectives, shards(): lax.all_gather(value_terms, 'seq', axis=1, tiled=True)  23.7 us
    all_to_all x1, waiting for transfers between devices, shards(): lax.all_to_all(long_filter, 'seq', split_axis=1, concat_axis=0, tiled=True)  21.1 us
    all_to_all x1, waiting for transfers between devices, shards(): lax.all_to_all(key_in, 'seq', split_axis=1, concat_axis=0, tiled=True)  16 us
    sub x1, other arithmetic, long_backward(): real_f * imag_g - imag_f * real_g  15.5 us
  transfers between devices with their start and end apart: 7, of which 6 were waited for; matrix products, arithmetic and copies ran while one was open for 7% of the time, Pallas kernels for 0%

commit v1 on v0

v1 whole, which is shorter than its diff:
```python
import functools
import math

import jax
import jax.numpy as jnp
import numpy as np
from jax import lax
from jax.experimental import pallas as pl
from jax.experimental.pallas import tpu as pltpu
from jax.sharding import PartitionSpec as P

BF = jnp.bfloat16
F32 = jnp.float32
HALF = 64
MIB = 1 << 20


def transform_tables(parts, rows):
    length = parts * rows
    mid = rows // 2
    p = np.arange(parts)
    k = np.arange(parts)
    step = math.pi / (2 * length)
    angle = ((rows * p[None, :] * (4 * k[:, None] + 1)) % (4 * length)) * step
    first = np.stack([np.cos(angle), -np.sin(angle)], 1)
    forward = np.einsum("kcp,rs->kcrps", first, np.eye(8)).reshape(parts * 16, parts * 8)
    backward = forward.T / length
    angle = ((np.arange(rows)[None, :] * (4 * k[:, None] + 1)) % (4 * length)) * step
    factors = np.stack([np.cos(angle), np.sin(angle)], 1).astype(np.float32)
    r, j = np.arange(mid)[:, None], np.arange(mid)[None, :]
    second = []
    for odd in (0, 1):
        turn = (((2 * j + odd) * r) % rows) * (2 * math.pi / rows)
        cos, sin = np.cos(turn), np.sin(turn)
        second.append(np.block([[cos, -sin], [sin, cos]]))
    as_bf = lambda x: x.astype(np.float32).astype(jnp.bfloat16)
    second = np.stack(second)
    return as_bf(forward), as_bf(second), as_bf(second.transpose(0, 2, 1)), as_bf(backward), factors


def low_lanes(shape):
    return (lax.broadcasted_iota(jnp.int32, shape, len(shape) - 1) % 128) < HALF


def swap_halves(x):
    return pltpu.roll(x, HALF, axis=x.ndim - 1)


def spectral_kernel(recv, m1, w, wi, m2, factors, gz_out, gh_out, y, u, acc):
    parts, chans, rows = recv.shape
    chans //= 3
    mid = rows // 2
    group = 16

    @pl.loop(0, 3 * chans // 16, unroll=2)
    def _(i):
        base = pl.multiple_of(16 * i, 16)
        x = recv[:, pl.ds(base, 16), :].astype(F32)
        out = []
        for q in range(2):
            xq = x[:, 8 * q : 8 * q + 8, :].reshape(parts * 8, rows).astype(BF)
            out.append(jnp.dot(m1[...], xq, preferred_element_type=F32))
        for k in range(parts):
            c, s = factors[k, 0:1, :], factors[k, 1:2, :]
            sums, gaps = [], []
            for q in range(2):
                re, im = out[q][16 * k : 16 * k + 8], out[q][16 * k + 8 : 16 * k + 16]
                turned = (re * c + im * s, im * c - re * s)
                sums.append(jnp.concatenate([t[:, :mid] + t[:, mid:] for t in turned], axis=1))
                gaps.append(jnp.concatenate([t[:, :mid] - t[:, mid:] for t in turned], axis=1))
            y[0, k, pl.ds(base, 16), :] = jnp.concatenate(sums, axis=0).astype(BF)
            y[1, k, pl.ds(base, 16), :] = jnp.concatenate(gaps, axis=0).astype(BF)

    @pl.loop(0, parts // group)
    def _(kk):
        backs = []
        for odd in range(2):
            lines = y[odd, pl.ds(group * kk, group)].reshape(group * 3 * chans, rows)
            spec = jnp.dot(lines, w[odd], preferred_element_type=F32)
            products = []
            for n in range(group):
                at = 3 * chans * n
                grad = spec[at + 2 * chans : at + 3 * chans]
                gr, gi = grad[:, :mid], grad[:, mid:]
                for h in range(2):
                    part = spec[at + h * chans : at + (h + 1) * chans]
                    sr, si = part[:, :mid], part[:, mid:]
                    products.append(jnp.concatenate([sr * gr + si * gi, sr * gi - si * gr], axis=1))
            product = jnp.concatenate(products, axis=0).astype(BF)
            backs.append(jnp.dot(product, wi[odd], preferred_element_type=F32))
        for h, back in enumerate((backs[0] + backs[1], backs[0] - backs[1])):
            cols = slice(mid * h, mid * h + mid)
            for n in range(group):
                k = group * kk + n
                c, s = factors[k, 0:1, cols], factors[k, 1:2, cols]
                lines = back[2 * chans * n : 2 * chans * (n + 1)]
                re, im = lines[:, :mid], lines[:, mid:]
                u[2 * k, :, cols] = (re * c - im * s).astype(BF)
                u[2 * k + 1, :, cols] = (im * c + re * s).astype(BF)

    acc[...] = jnp.zeros_like(acc)

    def backward(base):
        piece = u[:, pl.ds(base, 16), :].astype(F32)
        outs = []
        for q in range(2):
            v = piece[:, 8 * q : 8 * q + 8, :].reshape(parts * 16, rows).astype(BF)
            out = jnp.dot(m2[...], v, preferred_element_type=F32)
            outs.append(out.reshape(parts, 8, rows))
        return jnp.concatenate(outs, axis=1)

    @pl.loop(0, chans // 16, unroll=2)
    def _(i):
        base = pl.multiple_of(16 * i, 16)
        grad = backward(base)
        for h in range(2):
            gz_out[:, pl.ds(chans * h + base, 16), :] = grad[:, :, mid * h : mid * h + mid].astype(BF)

    @pl.loop(0, chans // 16, unroll=2)
    def _(i):
        base = pl.multiple_of(16 * i, 16)
        grad = backward(chans + base)
        for h in range(2):
            gh_out[:, pl.ds(chans * h + base, 16), :] = grad[:, :, mid * h : mid * h + mid].astype(BF)
        acc[...] += jnp.sum((grad * grad).reshape(parts * 2, 8, rows), axis=0)

    total = jnp.sum(jnp.sum(acc[...], axis=0, keepdims=True), axis=1, keepdims=True)
    coarse = total.astype(BF).astype(F32)
    fine = (total - coarse).astype(BF).astype(F32)
    row = lax.broadcasted_iota(jnp.int32, (16, 128), 0)
    sums = jnp.where(row == 2, coarse, jnp.where(row == 3, fine, 0.0))
    lane = lax.broadcasted_iota(jnp.int32, (16, mid), 1)
    pick = jnp.where((lane == lax.broadcasted_iota(jnp.int32, (16, mid), 0)) & (lane < 2), 1.0, 0.0).astype(BF)
    firsts = gz_out[:, :chans, :].reshape(parts * chans, mid)
    edges = lax.dot_general(pick, firsts, (((1,), (1,)), ((), ())), preferred_element_type=F32)
    for p in range(parts):
        after = jnp.zeros((16, 128), F32)
        if p + 1 < parts:
            at = (p + 1) // 2 * 128
            after = edges[:, at : at + 128]
            if (p + 1) % 2:
                after = swap_halves(after)
        gz_out[p, 2 * chans : 2 * chans + 16, :] = jnp.where(row < 2, after, sums).astype(BF)


def spectral(recv, parts, rows):
    tables = transform_tables(parts, rows)
    chans = recv.shape[1] // 3
    mid = rows // 2
    vmem = pl.BlockSpec(memory_space=pltpu.VMEM)
    flops = 2 * parts * parts * 16 * 8 * rows * chans // 8 * 5 + 2 * parts * rows * rows * chans * 10
    return pl.pallas_call(
        spectral_kernel,
        out_shape=(
            jax.ShapeDtypeStruct((parts, 2 * chans + 16, mid), BF),
            jax.ShapeDtypeStruct((parts, 2 * chans, mid), BF),
        ),
        in_specs=[vmem] * 6,
        out_specs=(vmem, vmem),
        scratch_shapes=[
            pltpu.VMEM((2, parts, 3 * chans, rows), BF),
            pltpu.VMEM((2 * parts, 2 * chans, rows), BF),
            pltpu.VMEM((8, rows), F32),
        ],
        compiler_params=pltpu.CompilerParams(vmem_limit_bytes=60 * MIB),
        cost_estimate=pl.CostEstimate(flops=flops, bytes_accessed=7 * MIB, transcendentals=0),
        name="spectral",
    )(recv, *[jnp.asarray(x) for x in tables])


def row_index(x):
    return lax.broadcasted_iota(jnp.int32, x.shape, 0)


def delayed(x, before):
    row = row_index(x)
    one = jnp.where(row == 0, before[1:2], pltpu.roll(x, 1, axis=0))
    two = jnp.where(row == 0, before[0:1], jnp.where(row == 1, before[1:2], pltpu.roll(x, 2, axis=0)))
    return one, two


def prepare_kernel(cot, gate, key, value, filt, key_taps, value_taps, before, send):
    rows, lanes = cot.shape
    mid = rows // 2
    grad = cot[...].astype(F32) * gate[...].astype(F32)
    kf, vf = key[...].astype(F32), value[...].astype(F32)
    edge = before[...].astype(F32)
    k1, k2 = delayed(kf, edge[0:2])
    v1, v2 = delayed(vf, edge[2:4])
    kt, vt = key_taps[...], value_taps[...]
    key_short = kt[0:1] * kf + kt[1:2] * k1 + kt[2:3] * k2
    value_short = vt[0:1] * vf + vt[1:2] * v1 + vt[2:3] * v2
    mixed = key_short * value_short
    for j in range(lanes // 128):
        cols = slice(128 * j, 128 * j + 128)
        for n, x in enumerate((filt[:, cols], mixed[:, cols], grad[:, cols])):
            x = x.astype(BF)
            turned = jnp.concatenate([x[:mid].T, x[mid:].T], axis=1)
            send[2 * j, HALF * n : HALF * n + HALF, :] = turned[:HALF]
            send[2 * j + 1, HALF * n : HALF * n + HALF, :] = turned[HALF:]


def column_call(kernel, name, ins, outs, lanes, columns):
    def spec(shape):
        if len(shape) == 3:
            return pl.BlockSpec((shape[0] * lanes // columns,) + shape[1:], lambda i: (i, 0, 0))
        return pl.BlockSpec((shape[0], lanes), lambda i: (0, i))

    size = sum(math.prod(a.shape) * a.dtype.itemsize for a in list(ins) + list(outs))
    return pl.pallas_call(
        kernel,
        grid=(columns // lanes,),
        in_specs=[spec(a.shape) for a in ins],
        out_specs=[spec(a.shape) for a in outs],
        out_shape=outs,
        compiler_params=pltpu.CompilerParams(vmem_limit_bytes=60 * MIB),
        cost_estimate=pl.CostEstimate(flops=size, bytes_accessed=size, transcendentals=0),
        name=name,
    )(*ins)


def gate_kernel(cot, conv, out):
    out[...] = (cot[...].astype(F32) * conv[...].astype(F32)).astype(BF)


def unpack(first, second):
    pairs = [jnp.concatenate([x[at : at + HALF] for x in (first, second)], axis=0) for at in (0, HALF)]
    return jnp.concatenate([pair.T for pair in pairs], axis=0).astype(F32)


def finish_kernel(grads, key, value, key_taps, value_taps, before, after, key_out, value_out, taps_out):
    rows, lanes = key.shape
    pieces, edges = [], []
    for j in range(lanes // 128):
        first, second = grads[2 * j], grads[2 * j + 1]
        pieces.append(unpack(first, second))
        edge = [x[2 * HALF : 2 * HALF + 16].astype(F32) for x in (first, second)]
        edges.append(jnp.where(low_lanes((16, 128)), edge[0], swap_halves(edge[1])))
    gz = jnp.concatenate(pieces, axis=1)
    edge = jnp.concatenate(edges, axis=1)
    next0, next1 = edge[0:1], edge[1:2]
    kf, vf = key[...].astype(F32), value[...].astype(F32)
    prev, post = before[...].astype(F32), after[...].astype(F32)
    k1, k2 = delayed(kf, prev[0:2])
    v1, v2 = delayed(vf, prev[2:4])
    kt, vt = key_taps[...], value_taps[...]
    row = row_index(kf)

    def short(taps, x0, x1, x2):
        return taps[0:1] * x0 + taps[1:2] * x1 + taps[2:3] * x2

    def beyond(taps, x, edge):
        last, prior = x[rows - 1 : rows], x[rows - 2 : rows - 1]
        return short(taps, edge[0:1], last, prior), short(taps, edge[1:2], edge[0:1], last)

    def backward(taps, grad, grad0, grad1):
        one = jnp.where(row == rows - 1, grad0, pltpu.roll(grad, rows - 1, axis=0))
        two = jnp.where(row == rows - 2, grad0, jnp.where(row == rows - 1, grad1, pltpu.roll(grad, rows - 2, axis=0)))
        return short(taps, grad, one, two)

    key_short, value_short = short(kt, kf, k1, k2), short(vt, vf, v1, v2)
    key_a, key_b = beyond(kt, kf, post[0:2])
    value_a, value_b = beyond(vt, vf, post[2:4])
    grad_key, grad_value = gz * value_short, gz * key_short
    key_out[...] = backward(kt, grad_key, next0 * value_a, next1 * value_b).astype(BF)
    value_out[...] = backward(vt, grad_value, next0 * key_a, next1 * key_b).astype(BF)
    sums = [jnp.sum(grad_key * x, axis=0, keepdims=True) for x in (kf, k1, k2)]
    sums += [jnp.sum(grad_value * x, axis=0, keepdims=True) for x in (vf, v1, v2)]
    taps_out[...] = jnp.concatenate(sums + [jnp.zeros((2, lanes), F32)], axis=0)


def clip_kernel(grads, scale, out):
    factor = scale[0:1, 0:1]
    for j in range(out.shape[1] // 128):
        out[:, 128 * j : 128 * j + 128] = unpack(grads[2 * j], grads[2 * j + 1]) * factor


def clip(grads, scale, rows, columns, lanes):
    per = grads.shape[0] * lanes // columns
    return pl.pallas_call(
        clip_kernel,
        grid=(columns // lanes,),
        in_specs=[
            pl.BlockSpec((per,) + grads.shape[1:], lambda i: (i, 0, 0)),
            pl.BlockSpec((1, 1), lambda i: (0, 0)),
        ],
        out_specs=pl.BlockSpec((rows, lanes), lambda i: (0, i)),
        out_shape=jax.ShapeDtypeStruct((rows, columns), F32),
        compiler_params=pltpu.CompilerParams(vmem_limit_bytes=60 * MIB),
        cost_estimate=pl.CostEstimate(flops=rows * columns * 4, bytes_accessed=rows * columns * 6, transcendentals=0),
        name="clip",
    )(grads, scale)


def tree_sum(x, axis, size):
    step = 1
    while step < size:
        x = x + lax.ppermute(x, axis, [(i, i ^ step) for i in range(size)])
        step *= 2
    return x


def shards(gate_in, key_in, value_in, conv_out, cotangent, long_filter, key_taps, value_taps, *, parts, others):
    rows, columns = key_in.shape
    shape = jax.ShapeDtypeStruct
    tails = jnp.concatenate([key_in[-2:], value_in[-2:]], axis=0)
    heads = jnp.concatenate([key_in[:2], value_in[:2]], axis=0)
    before = lax.ppermute(tails, "seq", [(i, i + 1) for i in range(parts - 1)])
    after = lax.ppermute(heads, "seq", [(i + 1, i) for i in range(parts - 1)])
    before, after = lax.optimization_barrier((before, after))
    (send,) = column_call(
        prepare_kernel,
        "prepare",
        (cotangent, gate_in, key_in, value_in, long_filter, key_taps, value_taps, before),
        (shape((parts, 3 * HALF, rows), BF),),
        1024,
        columns,
    )
    recv = lax.all_to_all(send, "seq", 0, 0)
    (gate_grad,) = column_call(gate_kernel, "gate", (cotangent, conv_out), (shape((rows, columns), BF),), 1024, columns)
    recv, gate_grad = lax.optimization_barrier((recv, gate_grad))
    gz_send, gh_send = spectral(recv, parts, rows)
    gz_recv = lax.all_to_all(gz_send, "seq", 0, 0)
    gz_recv, gh_send = lax.optimization_barrier((gz_recv, gh_send))
    gh_recv = lax.all_to_all(gh_send, "seq", 0, 0)
    squares = jnp.sum(gz_recv[:, 2 * HALF + 2 : 2 * HALF + 4, 0].astype(F32)).reshape(1, 1)
    total = tree_sum(squares, "chan", others)
    count = rows * columns * parts * others
    scale = jnp.minimum(1.0, 1.0 / jnp.sqrt(total / count + 1e-6))
    key_grad, value_grad, taps = column_call(
        finish_kernel,
        "finish",
        (gz_recv, key_in, value_in, key_taps, value_taps, before, after),
        (shape((rows, columns), BF), shape((rows, columns), BF), shape((8, columns), F32)),
        512,
        columns,
    )
    taps = tree_sum(taps, "seq", parts)
    filter_grad = clip(gh_recv, scale, rows, columns, 1024)
    return (gate_grad, key_grad, value_grad, filter_grad, taps[0:3], taps[3:6])


def solution(mesh):
    blocks, vectors = P("seq", "chan"), P(None, "chan")
    return jax.shard_map(
        functools.partial(shards, parts=mesh.shape["seq"], others=mesh.shape["chan"]),
        mesh=mesh,
        in_specs=(blocks,) * 6 + (vectors,) * 2,
        out_specs=(blocks,) * 4 + (vectors,) * 2,
        check_vma=False,
    )
```

time: 546 us -> 155 us (0.28)
  matrix products: 208 us -> 0 us
  blocking collectives: 130 us -> 23.7 us
  other arithmetic: 40.6 us -> 2.42 us
  local copies, waits for them, and re-layouts: 39.2 us -> 4.72 us
  Pallas kernels: 0 us -> 29.9 us
  waiting for transfers between devices: 84.4 us -> 54.8 us
    dot_general x12 -> x0, matrix products: 208 us -> none  [contract(): return jnp.einsum(form, left, right, precision=lax.Precision.HIGHEST)]
    all_gather x2 -> x0, blocking collectives: 66.3 us -> none  [the longest x1 42.5 us: shards(): lax.all_gather(key_terms, 'seq', axis=1, tiled=True)]
    psum x1 -> x0, blocking collectives: 63.4 us -> none  [clip_factor(): total = lax.psum(jnp.sum(grad_h * grad_h), ('seq', 'chan'))]
    all_to_all x7 -> x2, waiting for transfers between devices: 84.4 us -> 39.3 us  [the longest x1 39.3 us: shards(): recv = lax.all_to_all(send, 'seq', 0, 0)]
    pallas_call x0 -> x5, Pallas kernels: none -> 29.9 us  [the longest x3 14.4 us: column_call(): pl.pallas_call(kernel, grid=(columns // lanes,), in_specs=[spec(a.shape)...]
    unnamed x50 -> x8, local copies, waits for them, and re-layouts: 29.1 us -> 3.24 us
    all_to_all x0 -> x1, blocking collectives: none -> 23.7 us  [shards(): gz_recv = lax.all_to_all(gz_send, 'seq', 0, 0)]
    all_to_all x7 -> x2, starting transfers between devices: 36 us -> 15.9 us  [the longest x1 12 us: shards(): recv = lax.all_to_all(send, 'seq', 0, 0)]
  transfers between devices with their start and end apart: 7 -> 11, of which waited for: 6 -> 8; matrix products, arithmetic and copies ran while one was open for 7% -> 2% of each run, Pallas kernels for 0% -> 6%
where the time goes in v1:
time: 155 us; the launch traced here: 154 us
  waiting for transfers between devices  54.8 us (35%)
  starting transfers between devices  35.6 us (23%)
  Pallas kernels  29.9 us (19%)
  blocking collectives  23.7 us (15%)
  local copies, waits for them, and re-layouts  4.72 us (3%)
  between operations  2.81 us (2%)
  other arithmetic  2.42 us (2%)
    all_to_all x1, waiting for transfers between devices, shards(): recv = lax.all_to_all(send, 'seq', 0, 0)  39.3 us
    all_to_all x1, blocking collectives, shards(): gz_recv = lax.all_to_all(gz_send, 'seq', 0, 0)  23.7 us
    ppermute x7, starting transfers between devices, tree_sum(): x = x + lax.ppermute(x, axis, [(i, i ^ step) for i in range(size)])  15.4 us
    ppermute x7, waiting for transfers between devices, tree_sum(): x = x + lax.ppermute(x, axis, [(i, i ^ step) for i in range(size)])  14.6 us
    pallas_call x3, Pallas kernels, column_call(): pl.pallas_call(kernel, grid=(columns // lanes,), in_specs=[spec(a.shape)...  14.4 us
    pallas_call x1, Pallas kernels, spectral(): pl.pallas_call(spectral_kernel, out_shape=(jax.ShapeDtypeStruct((parts, 2...  13 us
    all_to_all x1, starting transfers between devices, shards(): recv = lax.all_to_all(send, 'seq', 0, 0)  12 us
    all_to_all x1, starting transfers between devices, shards(): gh_recv = lax.all_to_all(gh_send, 'seq', 0, 0)  3.93 us
  transfers between devices with their start and end apart: 11, of which 8 were waited for; matrix products, arithmetic and copies ran while one was open for 2% of the time, Pallas kernels for 6%

profile of v1, /device:TPU:0, one launch (start us, length us, event | category | flops | bytes accessed | tf_op | source)
XLA Modules:
  0.0 153.9 jit_solution(10067122256325042304)
XLA Ops:
  1.5 1.3 collective-permute-start.1
  2.8 3.0 %collective-permute-start = (bf16[4,2048]{1,0:T(4,128)(2,1)S(1)}, bf16[4,2048]{1,0:T(4,128)(2,1)S(1)}, u32[]{:S(2)}, u32[]{:S(2)}) collective-permute-start(bf16[4,2048]{1,0:T(4,128)(2,1)S(1)} %pad_maximum_fusion), channel_id=1, source_target_pairs={{0,4},{4,8},{8,12},{12,16},{16,20},{20,24},{24,28},{28,32},{32,36}... | collective-permute-start | bytes 49160 | tf_op jit(solution)/shard_map/ppermute | solution.py:308
  7.3 5.3 %prepare.1 = bf16[32,192,256]{2,1,0:T(8,128)(2,1)} custom-call(bf16[256,2048]{1,0:T(8,128)(2,1)} %cot.3, bf16[256,2048]{1,0:T(8,128)(2,1)} %gate.2, bf16[256,2048]{1,0:T(8,128)(2,1)} %key.3, bf16[256,2048]{1,0:T(8,128)(2,1)} %value.3, f32[256,2048]{1,0:T(8,128)} %filt.1, f32[3,2048]{1,0:T(4,128)} %key_taps.3, f32[3,2048]{1,0:T(4,128)} %value_taps.3, ...), custom_call_target="tpu_custom_call" | custom-call | flops 9502720 | bytes 9502720 | tf_op jit(solution)/shard_map/prepare/pallas_call | solution.py:210
  12.6 12.0 %all-to-all-start = ((bf16[32,192,256]{2,1,0:T(8,128)(2,1)}), bf16[32,192,256]{2,1,0:T(8,128)(2,1)S(1)}, u32[]{:S(2)}, u32[]{:S(2)}) async-start(bf16[32,192,256]{2,1,0:T(8,128)(2,1)} %prepare.1), calls=%async_computation | async-start | bytes 6291456 | tf_op jit(solution)/shard_map/all_to_all | solution.py:319
  24.6 2.4 %gate.3 = bf16[256,2048]{1,0:T(8,128)(2,1)} custom-call(bf16[256,2048]{1,0:T(8,128)(2,1)} %cot.3, bf16[256,2048]{1,0:T(8,128)(2,1)} %conv.1), custom_call_target="tpu_custom_call" | custom-call | flops 3145728 | bytes 3145728 | tf_op jit(solution)/shard_map/gate/pallas_call | solution.py:210
  27.1 39.3 %all-to-all-done.recv = bf16[32,192,256]{2,1,0:T(8,128)(2,1)S(1)} async-done(((bf16[32,192,256]{2,1,0:T(8,128)(2,1)}), bf16[32,192,256]{2,1,0:T(8,128)(2,1)S(1)}, u32[]{:S(2)}, u32[]{:S(2)}) %all-to-all-start) | async-done | bytes 3145760 | tf_op jit(solution)/shard_map/all_to_all | solution.py:319
  66.4 1.6 %copy-done.1 = bf16[32,192,256]{2,1,0:T(8,128)(2,1)} copy-done((bf16[32,192,256]{2,1,0:T(8,128)(2,1)}, bf16[32,192,256]{2,1,0:T(8,128)(2,1)S(1)}, u32[]{:S(2)}) %copy-start.1) | copy-done | bytes 3145752
  68.1 13.0 %spectral.1 = (bf16[32,144,128]{2,1,0:T(8,128)(2,1)}, bf16[32,128,128]{2,1,0:T(8,128)(2,1)}) custom-call(bf16[32,192,256]{2,1,0:T(8,128)(2,1)} %copy-done.1, bf16[512,256]{1,0:T(8,128)(2,1)} %constant.19.clone.m1, bf16[2,256,256]{2,1,0:T(8,128)(2,1)} %constant.20.clone.w, bf16[2,256,256]{2,1,0:T(8,128)(2,1)} %constant.21.clone.wi, ...), custom_call_target="tpu_custom_call" | custom-call | flops 5368709120 | bytes 7340032 | tf_op jit(solution)/shard_map/spectral/pallas_call | solution.py:152
  81.0 23.7 %all_to_all.15.grads = bf16[32,144,128]{2,1,0:T(8,128)(2,1)} all-to-all(bf16[32,144,128]{2,1,0:T(8,128)(2,1)} %get-tuple-element.20), channel_id=1, replica_groups=mesh['seq'=32,'chan'=4] {'seq'}, dimensions={0} | all-to-all | bytes 2359296 | tf_op jit(solution)/shard_map/all_to_all | solution.py:323
  104.7 3.9 %all-to-all-start.2 = ((bf16[32,128,128]{2,1,0:T(8,128)(2,1)}), bf16[32,128,128]{2,1,0:T(8,128)(2,1)S(1)}, u32[]{:S(2)}, u32[]{:S(2)}) async-start(bf16[32,128,128]{2,1,0:T(8,128)(2,1)} %get-tuple-element.26), calls=%async_computation.2 | async-start | bytes 2097152 | tf_op jit(solution)/shard_map/all_to_all | solution.py:325
  108.7 6.6 %finish.1 = (bf16[256,2048]{1,0:T(8,128)(2,1)}, bf16[256,2048]{1,0:T(8,128)(2,1)}, f32[8,2048]{1,0:T(8,128)}) custom-call(bf16[32,144,128]{2,1,0:T(8,128)(2,1)} %all_to_all.15.grads, bf16[256,2048]{1,0:T(8,128)(2,1)} %key.3, bf16[256,2048]{1,0:T(8,128)(2,1)} %value.3, f32[3,2048]{1,0:T(4,128)} %key_taps.3, f32[3,2048]{1,0:T(4,128)} %value_taps.3, ...), custom_call_target="tpu_custom_call" | custom-call | flops 5521408 | bytes 5521408 | tf_op jit(solution)/shard_map/finish/pallas_call | solution.py:210
  115.5 1.3 collective-permute-done.4
  117.6 1.8 %collective-permute-start.5 = (f32[8,2048]{1,0:T(8,128)S(1)}, f32[8,2048]{1,0:T(8,128)S(1)}, u32[]{:S(2)}, u32[]{:S(2)}) collective-permute-start(f32[8,2048]{1,0:T(8,128)S(1)} %add.27), channel_id=1, source_target_pairs={{0,8},{4,12},{8,0},{12,4},{16,24},{20,28},{24,16},{28,20},{32,40},... | collective-permute-start | bytes 196616 | tf_op jit(solution)/shard_map/ppermute | solution.py:298
  119.4 4.7 %collective-permute-done.5 = f32[8,2048]{1,0:T(8,128)S(1)} collective-permute-done((f32[8,2048]{1,0:T(8,128)S(1)}, f32[8,2048]{1,0:T(8,128)S(1)}, u32[]{:S(2)}, u32[]{:S(2)}) %collective-permute-start.5) | collective-permute-done | bytes 65568 | tf_op jit(solution)/shard_map/ppermute | solution.py:298
  124.1 2.8 %collective-permute-start.6 = (f32[8,2048]{1,0:T(8,128)S(1)}, f32[8,2048]{1,0:T(8,128)S(1)}, u32[]{:S(2)}, u32[]{:S(2)}) collective-permute-start(f32[8,2048]{1,0:T(8,128)S(1)} %add.28), channel_id=1, source_target_pairs={{0,16},{4,20},{8,24},{12,28},{16,0},{20,4},{24,8},{28,12},{32,48},... | collective-permute-start | bytes 196616 | tf_op jit(solution)/shard_map/ppermute | solution.py:298
  126.9 3.1 %collective-permute-done.6 = f32[8,2048]{1,0:T(8,128)S(1)} collective-permute-done((f32[8,2048]{1,0:T(8,128)S(1)}, f32[8,2048]{1,0:T(8,128)S(1)}, u32[]{:S(2)}, u32[]{:S(2)}) %collective-permute-start.6) | collective-permute-done | bytes 65568 | tf_op jit(solution)/shard_map/ppermute | solution.py:298
  129.9 1.6 %collective-permute-start.7 = (f32[8,2048]{1,0:T(8,128)S(1)}, f32[8,2048]{1,0:T(8,128)S(1)}, u32[]{:S(2)}, u32[]{:S(2)}) collective-permute-start(f32[8,2048]{1,0:T(8,128)S(1)} %add.29), channel_id=1, source_target_pairs={{0,32},{4,36},{8,40},{12,44},{16,48},{20,52},{24,56},{28,60},{32,0... | collective-permute-start | bytes 196616 | tf_op jit(solution)/shard_map/ppermute | solution.py:298
  131.5 2.7 %collective-permute-done.7 = f32[8,2048]{1,0:T(8,128)S(1)} collective-permute-done((f32[8,2048]{1,0:T(8,128)S(1)}, f32[8,2048]{1,0:T(8,128)S(1)}, u32[]{:S(2)}, u32[]{:S(2)}) %collective-permute-start.7) | collective-permute-done | bytes 65568 | tf_op jit(solution)/shard_map/ppermute | solution.py:298
  134.3 3.2 %collective-permute-start.8 = (f32[8,2048]{1,0:T(8,128)S(1)}, f32[8,2048]{1,0:T(8,128)S(1)}, u32[]{:S(2)}, u32[]{:S(2)}) collective-permute-start(f32[8,2048]{1,0:T(8,128)S(1)} %add.30), channel_id=1, source_target_pairs={{0,64},{4,68},{8,72},{12,76},{16,80},{20,84},{24,88},{28,92},{32,9... | collective-permute-start | bytes 196616 | tf_op jit(solution)/shard_map/ppermute | solution.py:298
  137.5 1.5 convert_reduce_fusion
  138.9 1.5 collective-permute-start.2
  140.4 2.1 %collective-permute-done.2 = f32[1,1]{1,0:T(1,128)} collective-permute-done((f32[1,1]{1,0:T(1,128)}, f32[1,1]{1,0:T(1,128)}, u32[]{:S(2)}, u32[]{:S(2)}) %collective-permute-start.2) | collective-permute-done | bytes 36 | tf_op jit(solution)/shard_map/ppermute | solution.py:298
  143.9 4.4 %collective-permute-start.3 = (f32[1,1]{1,0:T(1,128)}, f32[1,1]{1,0:T(1,128)}, u32[]{:S(2)}, u32[]{:S(2)}) collective-permute-start(f32[1,1]{1,0:T(1,128)} %add.24), channel_id=1, source_target_pairs={{0,2},{1,3},{2,0},{3,1},{4,6},{5,7},{6,4},{7,5},{8,10},{9,11},{10,... | collective-permute-start | bytes 20 | tf_op jit(solution)/shard_map/ppermute | solution.py:298
  151.4 2.6 %clip.1 = f32[256,2048]{1,0:T(8,128)} custom-call(bf16[32,128,128]{2,1,0:T(8,128)(2,1)} %copy-done, f32[1,1]{1,0:T(1,128)S(6)} %min.3.scale), custom_call_target="tpu_custom_call" | custom-call | flops 2097152 | bytes 3145728 | tf_op jit(solution)/shard_map/clip/pallas_call | solution.py:280
  (22 shorter events, 5.7 us)
Async XLA Ops:
  1.5 4.4 %collective-permute-start.1 = (bf16[4,2048]{1,0:T(4,128)(2,1)S(1)}, bf16[4,2048]{1,0:T(4,128)(2,1)S(1)}, u32[]{:S(2)}, u32[]{:S(2)}) collective-permute-start(bf16[4,2048]{1,0:T(4,128)(2,1)S(1)} %pad_maximum_fusion.1), channel_id=1, source_target_pairs={{4,0},{8,4},{12,8},{16,12},{20,16},{24,20},{28,24},{32,28},{36,32}... | collective-permute-start | bytes 49160 | tf_op jit(solution)/shard_map/ppermute | solution.py:309
  2.8 3.9 %collective-permute-start = (bf16[4,2048]{1,0:T(4,128)(2,1)S(1)}, bf16[4,2048]{1,0:T(4,128)(2,1)S(1)}, u32[]{:S(2)}, u32[]{:S(2)}) collective-permute-start(bf16[4,2048]{1,0:T(4,128)(2,1)S(1)} %pad_maximum_fusion), channel_id=1, source_target_pairs={{0,4},{4,8},{8,12},{12,16},{16,20},{20,24},{24,28},{28,32},{32,36}... | collective-permute-start | bytes 49160 | tf_op jit(solution)/shard_map/ppermute | solution.py:308
  5.9 6.7 %copy-start.3 = (bf16[4,2048]{1,0:T(4,128)(2,1)}, bf16[4,2048]{1,0:T(4,128)(2,1)S(1)}, u32[]{:S(2)}) copy-start(bf16[4,2048]{1,0:T(4,128)(2,1)S(1)} %collective-permute-done.1.after) | copy-start | bytes 49156
  6.7 0.6 copy-start.2
  12.6 53.8 %all-to-all-start = ((bf16[32,192,256]{2,1,0:T(8,128)(2,1)}), bf16[32,192,256]{2,1,0:T(8,128)(2,1)S(1)}, u32[]{:S(2)}, u32[]{:S(2)}) async-start(bf16[32,192,256]{2,1,0:T(8,128)(2,1)} %prepare.1), calls=%async_computation | async-start | bytes 6291456 | tf_op jit(solution)/shard_map/all_to_all | solution.py:319
  66.4 1.6 %copy-start.1 = (bf16[32,192,256]{2,1,0:T(8,128)(2,1)}, bf16[32,192,256]{2,1,0:T(8,128)(2,1)S(1)}, u32[]{:S(2)}) copy-start(bf16[32,192,256]{2,1,0:T(8,128)(2,1)S(1)} %all-to-all-done.recv) | copy-start | bytes 9437188
  104.7 45.7 %all-to-all-start.2 = ((bf16[32,128,128]{2,1,0:T(8,128)(2,1)}), bf16[32,128,128]{2,1,0:T(8,128)(2,1)S(1)}, u32[]{:S(2)}, u32[]{:S(2)}) async-start(bf16[32,128,128]{2,1,0:T(8,128)(2,1)} %get-tuple-element.26), calls=%async_computation.2 | async-start | bytes 2097152 | tf_op jit(solution)/shard_map/all_to_all | solution.py:325
  115.3 1.5 collective-permute-start.4
  117.6 6.5 %collective-permute-start.5 = (f32[8,2048]{1,0:T(8,128)S(1)}, f32[8,2048]{1,0:T(8,128)S(1)}, u32[]{:S(2)}, u32[]{:S(2)}) collective-permute-start(f32[8,2048]{1,0:T(8,128)S(1)} %add.27), channel_id=1, source_target_pairs={{0,8},{4,12},{8,0},{12,4},{16,24},{20,28},{24,16},{28,20},{32,40},... | collective-permute-start | bytes 196616 | tf_op jit(solution)/shard_map/ppermute | solution.py:298
  124.1 5.8 %collective-permute-start.6 = (f32[8,2048]{1,0:T(8,128)S(1)}, f32[8,2048]{1,0:T(8,128)S(1)}, u32[]{:S(2)}, u32[]{:S(2)}) collective-permute-start(f32[8,2048]{1,0:T(8,128)S(1)} %add.28), channel_id=1, source_target_pairs={{0,16},{4,20},{8,24},{12,28},{16,0},{20,4},{24,8},{28,12},{32,48},... | collective-permute-start | bytes 196616 | tf_op jit(solution)/shard_map/ppermute | solution.py:298
  129.9 4.3 %collective-permute-start.7 = (f32[8,2048]{1,0:T(8,128)S(1)}, f32[8,2048]{1,0:T(8,128)S(1)}, u32[]{:S(2)}, u32[]{:S(2)}) collective-permute-start(f32[8,2048]{1,0:T(8,128)S(1)} %add.29), channel_id=1, source_target_pairs={{0,32},{4,36},{8,40},{12,44},{16,48},{20,52},{24,56},{28,60},{32,0... | collective-permute-start | bytes 196616 | tf_op jit(solution)/shard_map/ppermute | solution.py:298
  134.3 15.4 %collective-permute-start.8 = (f32[8,2048]{1,0:T(8,128)S(1)}, f32[8,2048]{1,0:T(8,128)S(1)}, u32[]{:S(2)}, u32[]{:S(2)}) collective-permute-start(f32[8,2048]{1,0:T(8,128)S(1)} %add.30), channel_id=1, source_target_pairs={{0,64},{4,68},{8,72},{12,76},{16,80},{20,84},{24,88},{28,92},{32,9... | collective-permute-start | bytes 196616 | tf_op jit(solution)/shard_map/ppermute | solution.py:298
  138.9 3.6 %collective-permute-start.2 = (f32[1,1]{1,0:T(1,128)}, f32[1,1]{1,0:T(1,128)}, u32[]{:S(2)}, u32[]{:S(2)}) collective-permute-start(f32[1,1]{1,0:T(1,128)} %bitcast), channel_id=1, source_target_pairs={{0,1},{1,0},{2,3},{3,2},{4,5},{5,4},{6,7},{7,6},{8,9},{9,8},{10,11... | collective-permute-start | bytes 20 | tf_op jit(solution)/shard_map/ppermute | solution.py:298
  143.9 5.1 %collective-permute-start.3 = (f32[1,1]{1,0:T(1,128)}, f32[1,1]{1,0:T(1,128)}, u32[]{:S(2)}, u32[]{:S(2)}) collective-permute-start(f32[1,1]{1,0:T(1,128)} %add.24), channel_id=1, source_target_pairs={{0,2},{1,3},{2,0},{3,1},{4,6},{5,7},{6,4},{7,5},{8,10},{9,11},{10,... | collective-permute-start | bytes 20 | tf_op jit(solution)/shard_map/ppermute | solution.py:298
  150.4 1.0 copy-start

commit v2 on v1

v2 whole, which is shorter than its diff:
```python
import functools
import math

import jax
import jax.numpy as jnp
import numpy as np
from jax import lax
from jax.experimental import pallas as pl
from jax.experimental.pallas import tpu as pltpu
from jax.sharding import PartitionSpec as P

BF = jnp.bfloat16
F32 = jnp.float32
HALF = 64
MIB = 1 << 20
SPECTRAL_LIMIT = 62
LATE_LIMIT = 24


def transform_tables(parts, rows):
    length = parts * rows
    mid = rows // 2
    p = np.arange(parts)
    k = np.arange(parts)
    step = math.pi / (2 * length)
    angle = ((rows * p[None, :] * (4 * k[:, None] + 1)) % (4 * length)) * step
    first = np.stack([np.cos(angle), -np.sin(angle)], 1)
    forward = np.einsum("kcp,rs->kcrps", first, np.eye(8)).reshape(parts * 16, parts * 8)
    backward = forward.T / length
    angle = ((np.arange(rows)[None, :] * (4 * k[:, None] + 1)) % (4 * length)) * step
    factors = np.stack([np.cos(angle), np.sin(angle)], 1).astype(np.float32)
    r, j = np.arange(mid)[:, None], np.arange(mid)[None, :]
    second = []
    for odd in (0, 1):
        turn = (((2 * j + odd) * r) % rows) * (2 * math.pi / rows)
        cos, sin = np.cos(turn), np.sin(turn)
        second.append(np.block([[cos, -sin], [sin, cos]]))
    as_bf = lambda x: x.astype(np.float32).astype(jnp.bfloat16)
    second = np.stack(second)
    return as_bf(forward), as_bf(second), as_bf(second.transpose(0, 2, 1)), as_bf(backward), factors


def low_lanes(shape):
    return (lax.broadcasted_iota(jnp.int32, shape, len(shape) - 1) % 128) < HALF


def swap_halves(x):
    return pltpu.roll(x, HALF, axis=x.ndim - 1)


def spectral_kernel(recv, m1, w, wi, m2, factors, gz_out, gh_out, x_v, gz_v, gh_v, y, u, acc, in_sems, out_sems):
    parts, chans, rows = recv.shape
    chans //= 3
    mid = rows // 2
    group = 16
    pieces = 3 * chans // 32

    def fetch(i):
        at = pl.ds(32 * i, 32)
        return pltpu.make_async_copy(recv.at[:, at, :], x_v.at[:, at, :], in_sems.at[i])

    for i in range(pieces):
        fetch(i).start()

    def forward(base):
        x = x_v[:, pl.ds(base, 16), :].astype(F32)
        out = []
        for q in range(2):
            xq = x[:, 8 * q : 8 * q + 8, :].reshape(parts * 8, rows).astype(BF)
            out.append(jnp.dot(m1[...], xq, preferred_element_type=F32))
        for k in range(parts):
            c, s = factors[k, 0:1, :], factors[k, 1:2, :]
            sums, gaps = [], []
            for q in range(2):
                re, im = out[q][16 * k : 16 * k + 8], out[q][16 * k + 8 : 16 * k + 16]
                turned = (re * c + im * s, im * c - re * s)
                sums.append(jnp.concatenate([t[:, :mid] + t[:, mid:] for t in turned], axis=1))
                gaps.append(jnp.concatenate([t[:, :mid] - t[:, mid:] for t in turned], axis=1))
            y[0, k, pl.ds(base, 16), :] = jnp.concatenate(sums, axis=0).astype(BF)
            y[1, k, pl.ds(base, 16), :] = jnp.concatenate(gaps, axis=0).astype(BF)

    @pl.loop(0, pieces)
    def _(i):
        fetch(i).wait()
        for q in range(2):
            forward(pl.multiple_of(32 * i + 16 * q, 16))

    @pl.loop(0, parts // group)
    def _(kk):
        backs = []
        for odd in range(2):
            lines = y[odd, pl.ds(group * kk, group)].reshape(group * 3 * chans, rows)
            spec = jnp.dot(lines, w[odd], preferred_element_type=F32)
            products = []
            for n in range(group):
                at = 3 * chans * n
                grad = spec[at + 2 * chans : at + 3 * chans]
                gr, gi = grad[:, :mid], grad[:, mid:]
                for h in range(2):
                    part = spec[at + h * chans : at + (h + 1) * chans]
                    sr, si = part[:, :mid], part[:, mid:]
                    products.append(jnp.concatenate([sr * gr + si * gi, sr * gi - si * gr], axis=1))
            product = jnp.concatenate(products, axis=0).astype(BF)
            backs.append(jnp.dot(product, wi[odd], preferred_element_type=F32))
        for h, back in enumerate((backs[0] + backs[1], backs[0] - backs[1])):
            cols = slice(mid * h, mid * h + mid)
            for n in range(group):
                k = group * kk + n
                c, s = factors[k, 0:1, cols], factors[k, 1:2, cols]
                lines = back[2 * chans * n : 2 * chans * (n + 1)]
                re, im = lines[:, :mid], lines[:, mid:]
                u[2 * k, :, cols] = (re * c - im * s).astype(BF)
                u[2 * k + 1, :, cols] = (im * c + re * s).astype(BF)

    acc[...] = jnp.zeros_like(acc)

    def backward(base):
        piece = u[:, pl.ds(base, 16), :].astype(F32)
        outs = []
        for q in range(2):
            v = piece[:, 8 * q : 8 * q + 8, :].reshape(parts * 16, rows).astype(BF)
            out = jnp.dot(m2[...], v, preferred_element_type=F32)
            outs.append(out.reshape(parts, 8, rows))
        return jnp.concatenate(outs, axis=1)

    tiles = chans // 16

    def store(target, scratch, first, row):
        at = pl.ds(pl.multiple_of(row, 16), 16)
        return pltpu.make_async_copy(scratch.at[:, at, :], target.at[:, at, :], out_sems.at[first])

    @pl.loop(0, tiles // 2)
    def _(i):
        for q in range(2):
            base = pl.multiple_of(32 * i + 16 * q, 16)
            grad = backward(chans + base)
            for h in range(2):
                gh_v[:, pl.ds(chans * h + base, 16), :] = grad[:, :, mid * h : mid * h + mid].astype(BF)
                store(gh_out, gh_v, tiles * h + 2 * i + q, chans * h + base).start()
            acc[...] += jnp.sum((grad * grad).reshape(parts * 2, 8, rows), axis=0)

    @pl.loop(0, tiles // 2)
    def _(i):
        for q in range(2):
            base = pl.multiple_of(32 * i + 16 * q, 16)
            grad = backward(base)
            for h in range(2):
                gz_v[:, pl.ds(chans * h + base, 16), :] = grad[:, :, mid * h : mid * h + mid].astype(BF)
                store(gz_out, gz_v, 2 * tiles + tiles * h + 2 * i + q, chans * h + base).start()

    total = jnp.sum(jnp.sum(acc[...], axis=0, keepdims=True), axis=1, keepdims=True)
    coarse = total.astype(BF).astype(F32)
    fine = (total - coarse).astype(BF).astype(F32)
    row = lax.broadcasted_iota(jnp.int32, (16, 128), 0)
    sums = jnp.where(row == 2, coarse, jnp.where(row == 3, fine, 0.0))
    lane = lax.broadcasted_iota(jnp.int32, (16, mid), 1)
    pick = jnp.where((lane == lax.broadcasted_iota(jnp.int32, (16, mid), 0)) & (lane < 2), 1.0, 0.0).astype(BF)
    firsts = gz_v[:, :chans, :].reshape(parts * chans, mid)
    edges = lax.dot_general(pick, firsts, (((1,), (1,)), ((), ())), preferred_element_type=F32)
    for p in range(parts):
        after = jnp.zeros((16, 128), F32)
        if p + 1 < parts:
            at = (p + 1) // 2 * 128
            after = edges[:, at : at + 128]
            if (p + 1) % 2:
                after = swap_halves(after)
        gz_v[p, 2 * chans : 2 * chans + 16, :] = jnp.where(row < 2, after, sums).astype(BF)
    store(gz_out, gz_v, 4 * tiles, 2 * chans).start()
    for n in range(2 * tiles):
        store(gh_out, gh_v, n, 16 * n).wait()
        store(gz_out, gz_v, 2 * tiles + n, 16 * n).wait()
    store(gz_out, gz_v, 4 * tiles, 2 * chans).wait()


def spectral(recv, parts, rows):
    tables = transform_tables(parts, rows)
    chans = recv.shape[1] // 3
    mid = rows // 2
    vmem = pl.BlockSpec(memory_space=pltpu.VMEM)
    anywhere = pl.BlockSpec(memory_space=pl.ANY)
    flops = 2 * parts * parts * 16 * 8 * rows * chans // 8 * 5 + 2 * parts * rows * rows * chans * 10
    return pl.pallas_call(
        spectral_kernel,
        out_shape=(
            jax.ShapeDtypeStruct((parts, 2 * chans + 16, mid), BF),
            jax.ShapeDtypeStruct((parts, 2 * chans, mid), BF),
        ),
        in_specs=[anywhere] + [vmem] * 5,
        out_specs=(anywhere, anywhere),
        scratch_shapes=[
            pltpu.VMEM(recv.shape, BF),
            pltpu.VMEM((parts, 2 * chans + 16, mid), BF),
            pltpu.VMEM((parts, 2 * chans, mid), BF),
            pltpu.VMEM((2, parts, 3 * chans, rows), BF),
            pltpu.VMEM((2 * parts, 2 * chans, rows), BF),
            pltpu.VMEM((8, rows), F32),
            pltpu.SemaphoreType.DMA((3 * chans // 32,)),
            pltpu.SemaphoreType.DMA((4 * (chans // 16) + 1,)),
        ],
        compiler_params=pltpu.CompilerParams(vmem_limit_bytes=SPECTRAL_LIMIT * MIB),
        cost_estimate=pl.CostEstimate(flops=flops, bytes_accessed=7 * MIB, transcendentals=0),
        name="spectral",
    )(recv, *[jnp.asarray(x) for x in tables])


def row_index(x):
    return lax.broadcasted_iota(jnp.int32, x.shape, 0)


def with_top(x, rows):
    top = x[:8]
    for n, line in enumerate(rows):
        top = jnp.where(row_index(top) == n, line, top)
    return jnp.concatenate([top, x[8:]], axis=0)


def with_bottom(x, rows):
    end = x.shape[0]
    bottom = x[end - 8 :]
    for n, line in enumerate(rows):
        bottom = jnp.where(row_index(bottom) == 8 - len(rows) + n, line, bottom)
    return jnp.concatenate([x[: end - 8], bottom], axis=0)


def delayed(x, before):
    first, second = before[0:1], before[1:2]
    one = with_top(pltpu.roll(x, 1, axis=0), [second])
    two = with_top(pltpu.roll(x, 2, axis=0), [first, second])
    return one, two


def stream(body, name, ins, smalls, outs, parts_of, chunks, limit, alias=None):
    def size(shape):
        return (shape[0] // chunks,) + tuple(shape[1:]) if len(shape) == 3 else (shape[0], shape[1] // chunks)

    def window(ref, c, rows=None):
        if len(ref.shape) == 2:
            per = ref.shape[1] // chunks
            return ref.at[:, pl.ds(pl.multiple_of(c * per, 128), per)]
        per = ref.shape[0] // chunks
        at = ref.at[pl.ds(c * per, per)]
        return at if rows is None else ref.at[pl.ds(c * per, per), pl.ds(rows[0], rows[1]), :]

    extra = [] if alias is None else [alias]
    n_in, n_small, n_out, n_part = len(ins), len(smalls), len(outs), len(parts_of)

    def kernel(*refs):
        refs = list(refs)
        take = lambda n: [refs.pop(0) for _ in range(n)]
        in_refs, small_refs, _, out_refs = take(n_in), take(n_small), take(len(extra)), take(n_out)
        in_v, small_v, out_v = take(n_in), take(n_small), take(n_part)
        in_sems, small_sems, out_sems = refs

        def fetch(n, c):
            return pltpu.make_async_copy(window(in_refs[n], c), in_v[n].at[c], in_sems.at[n, c])

        def store(n, c):
            index, rows = parts_of[n]
            return pltpu.make_async_copy(out_v[n].at[c], window(out_refs[index], c, rows), out_sems.at[n, c])

        smalls_in = [pltpu.make_async_copy(small_refs[n], small_v[n], small_sems.at[n]) for n in range(n_small)]
        for copy in smalls_in:
            copy.start()
        for c in range(chunks):
            for n in range(n_in):
                fetch(n, c).start()
        for copy in smalls_in:
            copy.wait()

        @pl.loop(0, chunks)
        def _(c):
            for n in range(n_in):
                fetch(n, c).wait()
            body(c, [v.at[c] for v in in_v], small_v, [v.at[c] for v in out_v])
            for n in range(n_part):
                store(n, c).start()

        for c in range(chunks):
            for n in range(n_part):
                store(n, c).wait()

    scratch = [pltpu.VMEM((chunks,) + size(a.shape), a.dtype) for a in ins]
    scratch += [pltpu.VMEM(a.shape, a.dtype) for a in smalls]
    for index, rows in parts_of:
        shape = size(outs[index].shape)
        if rows is not None:
            shape = (shape[0], rows[1], shape[2])
        scratch.append(pltpu.VMEM((chunks,) + shape, outs[index].dtype))
    scratch += [pltpu.SemaphoreType.DMA((n_in, chunks)), pltpu.SemaphoreType.DMA((max(n_small, 1),)), pltpu.SemaphoreType.DMA((n_part, chunks))]
    total = sum(math.prod(a.shape) * a.dtype.itemsize for a in list(ins) + list(outs))
    anywhere = pl.BlockSpec(memory_space=pl.ANY)
    return pl.pallas_call(
        kernel,
        in_specs=[anywhere] * (n_in + n_small + len(extra)),
        out_specs=[anywhere] * n_out,
        out_shape=outs,
        scratch_shapes=scratch,
        input_output_aliases={} if alias is None else {n_in + n_small: 0},
        compiler_params=pltpu.CompilerParams(vmem_limit_bytes=limit * MIB),
        cost_estimate=pl.CostEstimate(flops=total, bytes_accessed=total, transcendentals=0),
        name=name,
    )(*ins, *smalls, *extra)


def columns_of(ref, c, lanes):
    return ref[:, pl.ds(pl.multiple_of(c * lanes, 128), lanes)]


def short(taps, x0, x1, x2):
    return taps[0:1] * x0 + taps[1:2] * x1 + taps[2:3] * x2


def turn_out(x, out):
    rows, lanes = x.shape
    mid = rows // 2
    x = x.astype(BF)
    for j in range(lanes // 128):
        cols = slice(128 * j, 128 * j + 128)
        turned = jnp.concatenate([x[:mid, cols].T, x[mid:, cols].T], axis=1)
        out[2 * j] = turned[:HALF]
        out[2 * j + 1] = turned[HALF:]


def known_body(c, ins, smalls, outs):
    cot, gate, filt = ins
    turn_out(filt[...], outs[0])
    turn_out(cot[...].astype(F32) * gate[...].astype(F32), outs[1])


def mixed_body(c, ins, smalls, outs):
    kf, vf = (x[...].astype(F32) for x in ins)
    kt, vt, before = (columns_of(x, c, kf.shape[1]).astype(F32) for x in smalls)
    key_short = short(kt, kf, *delayed(kf, before[0:2]))
    value_short = short(vt, vf, *delayed(vf, before[2:4]))
    turn_out(key_short * value_short, outs[0])


def gate_body(c, ins, smalls, outs):
    cot, conv = ins
    outs[0][...] = (cot[...].astype(F32) * conv[...].astype(F32)).astype(BF)


def turn_in(blocks):
    tiles = []
    for j in range(blocks.shape[0] // 2):
        pair = (blocks[2 * j], blocks[2 * j + 1])
        halves = [jnp.concatenate([x[at : at + HALF] for x in pair], axis=0).T for at in (0, HALF)]
        tiles.append(jnp.concatenate(halves, axis=0))
    return jnp.concatenate(tiles, axis=1).astype(F32)


def taps_body(c, ins, smalls, outs):
    grads, key, value = ins
    gz = turn_in(grads)
    kf, vf = key[...].astype(F32), value[...].astype(F32)
    kt, vt, before = (columns_of(x, c, kf.shape[1]).astype(F32) for x in smalls)
    ks, vs = (kf,) + delayed(kf, before[0:2]), (vf,) + delayed(vf, before[2:4])
    grad_key, grad_value = gz * short(vt, *vs), gz * short(kt, *ks)
    sums = [jnp.sum(grad_key * x, axis=0, keepdims=True) for x in ks]
    sums += [jnp.sum(grad_value * x, axis=0, keepdims=True) for x in vs]
    outs[0][...] = jnp.concatenate(sums + [jnp.zeros((2, kf.shape[1]), F32)], axis=0)


def inputs_body(c, ins, smalls, outs):
    grads, key, value = ins
    rows, lanes = key.shape
    gz = turn_in(grads)
    kf, vf = key[...].astype(F32), value[...].astype(F32)
    kt, vt, before, after = (columns_of(x, c, lanes).astype(F32) for x in smalls)
    edges = []
    for j in range(lanes // 128):
        edge = [grads[2 * j + n, 2 * HALF : 2 * HALF + 16, :].astype(F32) for n in range(2)]
        edges.append(jnp.where(low_lanes((16, 128)), edge[0], swap_halves(edge[1])))
    edge = jnp.concatenate(edges, axis=1)
    next0, next1 = edge[0:1], edge[1:2]

    def beyond(taps, x, edge):
        last, prior = x[rows - 1 : rows], x[rows - 2 : rows - 1]
        return short(taps, edge[0:1], last, prior), short(taps, edge[1:2], edge[0:1], last)

    def backward(taps, grad, grad0, grad1):
        one = with_bottom(pltpu.roll(grad, rows - 1, axis=0), [grad0])
        two = with_bottom(pltpu.roll(grad, rows - 2, axis=0), [grad0, grad1])
        return short(taps, grad, one, two)

    key_short, value_short = short(kt, kf, *delayed(kf, before[0:2])), short(vt, vf, *delayed(vf, before[2:4]))
    key_a, key_b = beyond(kt, kf, after[0:2])
    value_a, value_b = beyond(vt, vf, after[2:4])
    outs[0][...] = backward(kt, gz * value_short, next0 * value_a, next1 * value_b).astype(BF)
    outs[1][...] = backward(vt, gz * key_short, next0 * key_a, next1 * key_b).astype(BF)


def clip_body(c, ins, smalls, outs):
    outs[0][...] = turn_in(ins[0]) * smalls[0][0:1, 0:1]


def tree_step(x, axis, step):
    return x + lax.ppermute(x, axis, [(i, i ^ step) for i in range(lax.axis_size(axis))])


def shards(gate_in, key_in, value_in, conv_out, cotangent, long_filter, key_taps, value_taps, *, parts, others):
    rows, columns = key_in.shape
    shape = jax.ShapeDtypeStruct
    block = shape((rows, columns), BF)
    send_shape = shape((parts, 3 * HALF, rows), BF)
    tails = jnp.concatenate([key_in[-2:], value_in[-2:]], axis=0)
    heads = jnp.concatenate([key_in[:2], value_in[:2]], axis=0)
    before = lax.ppermute(tails, "seq", [(i, i + 1) for i in range(parts - 1)])
    (known,) = stream(
        known_body,
        "known",
        (cotangent, gate_in, long_filter),
        (),
        (send_shape,),
        ((0, (0, HALF)), (0, (2 * HALF, HALF))),
        4,
        60,
    )
    (send,) = stream(
        mixed_body,
        "mixed",
        (key_in, value_in),
        (key_taps, value_taps, before),
        (send_shape,),
        ((0, (HALF, HALF)),),
        4,
        60,
        alias=known,
    )
    recv = lax.all_to_all(send, "seq", 0, 0)
    send, heads = lax.optimization_barrier((send, heads))
    after = lax.ppermute(heads, "seq", [(i + 1, i) for i in range(parts - 1)])
    (gate_grad,) = stream(gate_body, "gate", (cotangent, conv_out), (), (block,), ((0, None),), 4, 16)
    recv, gate_grad, after = lax.optimization_barrier((recv, gate_grad, after))
    gz_send, gh_send = spectral(recv, parts, rows)
    gz_recv = lax.all_to_all(gz_send, "seq", 0, 0)
    gz_recv, gh_send = lax.optimization_barrier((gz_recv, gh_send))
    gh_recv = lax.all_to_all(gh_send, "seq", 0, 0)
    (taps,) = stream(
        taps_body,
        "taps",
        (gz_recv, key_in, value_in),
        (key_taps, value_taps, before),
        (shape((8, columns), F32),),
        ((0, None),),
        4,
        LATE_LIMIT,
    )
    late, taps = lax.optimization_barrier((gz_recv, taps))
    key_grad, value_grad = stream(
        inputs_body,
        "inputs",
        (late, key_in, value_in),
        (key_taps, value_taps, before, after),
        (block, block),
        ((0, None), (1, None)),
        4,
        LATE_LIMIT,
    )
    total = jnp.sum(late[:, 2 * HALF + 2 : 2 * HALF + 4, :].astype(F32), axis=(0, 1))
    total = jnp.broadcast_to(total[None], (8, total.shape[0]))
    step, other, turns = 1, 1, 0
    while 2 * step < parts:
        if turns % 2 == 1 and other < others:
            taps, total = lax.optimization_barrier((taps, total))
            total = tree_step(total, "chan", other)
            other *= 2
        taps = tree_step(taps, "seq", step)
        step *= 2
        turns += 1
        if turns == 2:
            taps, key_grad, value_grad = lax.optimization_barrier((taps, key_grad, value_grad))
    while other < others:
        total = tree_step(total, "chan", other)
        other *= 2
    count = rows * columns * parts * others
    scale = jnp.minimum(1.0, 1.0 / jnp.sqrt(total / count + 1e-6))
    taps, gh_recv = lax.optimization_barrier((taps, gh_recv))
    taps = tree_step(taps, "seq", parts // 2)
    (filter_grad,) = stream(
        clip_body, "clip", (gh_recv,), (scale,), (shape((rows, columns), F32),), ((0, None),), 4, LATE_LIMIT
    )
    return (gate_grad, key_grad, value_grad, filter_grad, taps[0:3], taps[3:6])


def solution(mesh):
    blocks, vectors = P("seq", "chan"), P(None, "chan")
    return jax.shard_map(
        functools.partial(shards, parts=mesh.shape["seq"], others=mesh.shape["chan"]),
        mesh=mesh,
        in_specs=(blocks,) * 6 + (vectors,) * 2,
        out_specs=(blocks,) * 4 + (vectors,) * 2,
        check_vma=False,
    )
```

time: 155 us -> 137 us (0.88)
  waiting for transfers between devices: 54.8 us -> 46.8 us
  starting transfers between devices: 35.6 us -> 31.2 us
  local copies, waits for them, and re-layouts: 4.72 us -> 2.13 us
  Pallas kernels: 29.9 us -> 32.2 us
  other arithmetic: 2.42 us -> 0.16 us
  between operations: 2.81 us -> 0.91 us
    ppermute x7, waiting for transfers between devices: 14.6 us -> 7.61 us  [tree_step(): lax.ppermute(x, axis, [(i, i ^ step) for i in range(lax.axis_size(axis))])]
    unnamed x8 -> x16, local copies, waits for them, and re-layouts: 3.24 us -> 0.64 us
    pallas_call x4 -> x6, Pallas kernels: 16.9 us -> 19.3 us  [stream(): pl.pallas_call(kernel, in_specs=[anywhere] * (n_in + n_small + len(extra)...]
    ppermute x7, starting transfers between devices: 15.4 us -> 13.6 us  [tree_step(): lax.ppermute(x, axis, [(i, i ^ step) for i in range(lax.axis_size(axis))])]
    ppermute x1, starting transfers between devices: 3.03 us -> 1.29 us  [shards(): before = lax.ppermute(tails, 'seq', [(i, i + 1) for i in range(parts - 1)])]
    all_to_all x1, starting transfers between devices: 12 us -> 10.3 us  [shards(): recv = lax.all_to_all(send, 'seq', 0, 0)]
  transfers between devices with their start and end apart: 11 -> 11, of which waited for: 8 -> 6; matrix products, arithmetic and copies ran while one was open for 2% -> 0% of each run, Pallas kernels for 6% -> 11%
where the time goes in v2:
time: 137 us; the launch traced here: 136 us
  waiting for transfers between devices  46.8 us (34%)
  Pallas kernels  32.2 us (24%)
  starting transfers between devices  31.2 us (23%)
  blocking collectives  23.1 us (17%)
  local copies, waits for them, and re-layouts  2.13 us (2%)
    all_to_all x1, waiting for transfers between devices, shards(): recv = lax.all_to_all(send, 'seq', 0, 0)  38.7 us
    all_to_all x1, blocking collectives, shards(): gz_recv = lax.all_to_all(gz_send, 'seq', 0, 0)  23.1 us
    pallas_call x6, Pallas kernels, stream(): pl.pallas_call(kernel, in_specs=[anywhere] * (n_in + n_small + len(extra)...  19.3 us
    ppermute x7, starting transfers between devices, tree_step(): lax.ppermute(x, axis, [(i, i ^ step) for i in range(lax.axis_size(axis))])  13.6 us
    pallas_call x1, Pallas kernels, spectral(): pl.pallas_call(spectral_kernel, out_shape=(jax.ShapeDtypeStruct((parts, 2...  12.9 us
    all_to_all x1, starting transfers between devices, shards(): recv = lax.all_to_all(send, 'seq', 0, 0)  10.3 us
    ppermute x7, waiting for transfers between devices, tree_step(): lax.ppermute(x, axis, [(i, i ^ step) for i in range(lax.axis_size(axis))])  7.61 us
    all_to_all x1, starting transfers between devices, shards(): gh_recv = lax.all_to_all(gh_send, 'seq', 0, 0)  4.66 us
  transfers between devices with their start and end apart: 11, of which 6 were waited for; matrix products, arithmetic and copies ran while one was open for 0% of the time, Pallas kernels for 11%

profile of v2, /device:TPU:0, one launch (start us, length us, event | category | flops | bytes accessed | tf_op | source)
XLA Modules:
  0.0 136.5 jit_solution(12771322383870134748)
XLA Ops:
  0.6 0.8 fusion
  1.5 1.3 collective-permute-start
  2.8 3.3 %known.1.refs_5_ = bf16[32,192,256]{2,1,0:T(8,128)(2,1)} custom-call(bf16[256,2048]{1,0:T(8,128)(2,1)} %refs_0_.5, bf16[256,2048]{1,0:T(8,128)(2,1)} %refs_1_.5, f32[256,2048]{1,0:T(8,128)} %refs_2_.4), custom_call_target="tpu_custom_call" | custom-call | flops 7340032 | bytes 7340032 | tf_op jit(solution)/shard_map/known/pallas_call | solution.py:292
  6.7 3.9 %mixed.1 = bf16[32,192,256]{2,1,0:T(8,128)(2,1)} custom-call(bf16[256,2048]{1,0:T(8,128)(2,1)} %refs_1_.9, bf16[256,2048]{1,0:T(8,128)(2,1)} %refs_2_.7, f32[3,2048]{1,0:T(4,128)} %refs_3_.5, f32[3,2048]{1,0:T(4,128)} %refs_4_.3, bf16[4,2048]{1,0:T(4,128)(2,1)} %copy-done.6, bf16[32,192,256]{2,1,0:T(8,128)(2,1)} %known.1.refs_5_), custom_call_target="tpu_custom_call", output_to_operand_aliasing={{}: (5, {})} | custom-call | flops 5242880 | bytes 5242880 | tf_op jit(solution)/shard_map/mixed/pallas_call | solution.py:292
  10.7 10.3 %all-to-all-start = ((bf16[32,192,256]{2,1,0:T(8,128)(2,1)}), bf16[32,192,256]{2,1,0:T(8,128)(2,1)}, u32[]{:S(2)}, u32[]{:S(2)}) async-start(bf16[32,192,256]{2,1,0:T(8,128)(2,1)} %mixed.1), calls=%async_computation | async-start | bytes 6291456 | tf_op jit(solution)/shard_map/all_to_all | solution.py:430
  21.0 1.3 collective-permute-start.1
  22.4 1.3 gate.1
  24.1 38.7 %all-to-all-done.recv = bf16[32,192,256]{2,1,0:T(8,128)(2,1)} async-done(((bf16[32,192,256]{2,1,0:T(8,128)(2,1)}), bf16[32,192,256]{2,1,0:T(8,128)(2,1)}, u32[]{:S(2)}, u32[]{:S(2)}) %all-to-all-start) | async-done | bytes 3145760 | tf_op jit(solution)/shard_map/all_to_all | solution.py:430
  62.9 12.9 %spectral.1 = (bf16[32,144,128]{2,1,0:T(8,128)(2,1)}, bf16[32,128,128]{2,1,0:T(8,128)(2,1)}) custom-call(bf16[32,192,256]{2,1,0:T(8,128)(2,1)} %all-to-all-done.recv, bf16[512,256]{1,0:T(8,128)(2,1)} %constant.19.clone.m1, bf16[2,256,256]{2,1,0:T(8,128)(2,1)} %constant.20.clone.w, bf16[2,256,256]{2,1,0:T(8,128)(2,1)} %constant.21.clone.wi, ...), custom_call_target="tpu_custom_call" | custom-call | flops 5368709120 | bytes 7340032 | tf_op jit(solution)/shard_map/spectral/pallas_call | solution.py:182
  75.8 23.1 %all_to_all.15.refs_0_ = bf16[32,144,128]{2,1,0:T(8,128)(2,1)S(1)} all-to-all(bf16[32,144,128]{2,1,0:T(8,128)(2,1)} %get-tuple-element.30), channel_id=1, replica_groups=mesh['seq'=32,'chan'=4] {'seq'}, dimensions={0} | all-to-all | bytes 2359296 | tf_op jit(solution)/shard_map/all_to_all | solution.py:436
  98.9 4.7 %all-to-all-start.2 = ((bf16[32,128,128]{2,1,0:T(8,128)(2,1)}), bf16[32,128,128]{2,1,0:T(8,128)(2,1)}, u32[]{:S(2)}, u32[]{:S(2)}) async-start(bf16[32,128,128]{2,1,0:T(8,128)(2,1)} %get-tuple-element.44), calls=%async_computation.2 | async-start | bytes 2097152 | tf_op jit(solution)/shard_map/all_to_all | solution.py:438
  103.7 3.5 %taps.1 = f32[8,2048]{1,0:T(8,128)S(1)} custom-call(bf16[32,144,128]{2,1,0:T(8,128)(2,1)S(1)} %all_to_all.15.refs_0_, bf16[256,2048]{1,0:T(8,128)(2,1)S(1)} %copy-done, bf16[256,2048]{1,0:T(8,128)(2,1)S(1)} %copy-done.1, f32[3,2048]{1,0:T(4,128)S(1)} %copy-done.4, f32[3,2048]{1,0:T(4,128)S(1)} %copy-done.5, bf16[4,2048]{1,0:T(4,128)(2,1)S(1)} %copy-done.7), custom_call_target="tpu_custom_call" | custom-call | flops 3342336 | bytes 3342336 | tf_op jit(solution)/shard_map/taps/pallas_call | solution.py:292
  107.4 1.1 collective-permute-done.2
  108.5 1.7 %collective-permute-start.3 = (f32[8,2048]{1,0:T(8,128)S(1)}, f32[8,2048]{1,0:T(8,128)S(1)}, u32[]{:S(2)}, u32[]{:S(2)}) collective-permute-start(f32[8,2048]{1,0:T(8,128)S(1)} %add.27), channel_id=1, source_target_pairs={{0,8},{4,12},{8,0},{12,4},{16,24},{20,28},{24,16},{28,20},{32,40},... | collective-permute-start | bytes 196616 | tf_op jit(solution)/shard_map/ppermute | solution.py:398
  110.2 4.8 %inputs.1 = (bf16[256,2048]{1,0:T(8,128)(2,1)}, bf16[256,2048]{1,0:T(8,128)(2,1)}) custom-call(bf16[32,144,128]{2,1,0:T(8,128)(2,1)S(1)} %all_to_all.15.refs_0_, bf16[256,2048]{1,0:T(8,128)(2,1)S(1)} %copy-done, bf16[256,2048]{1,0:T(8,128)(2,1)S(1)} %copy-done.1, f32[3,2048]{1,0:T(4,128)S(1)} %copy-done.4, f32[3,2048]{1,0:T(4,128)S(1)} %copy-done.5, ...), custom_call_target="tpu_custom_call" | custom-call | flops 5373952 | bytes 5373952 | tf_op jit(solution)/shard_map/inputs/pallas_call | solution.py:292
  115.0 3.9 %collective-permute-done.3 = f32[8,2048]{1,0:T(8,128)S(1)} collective-permute-done((f32[8,2048]{1,0:T(8,128)S(1)}, f32[8,2048]{1,0:T(8,128)S(1)}, u32[]{:S(2)}, u32[]{:S(2)}) %collective-permute-start.3) | collective-permute-done | bytes 65568 | tf_op jit(solution)/shard_map/ppermute | solution.py:398
  118.9 2.8 %collective-permute-start.4 = (f32[8,2048]{1,0:T(8,128)S(1)}, f32[8,2048]{1,0:T(8,128)S(1)}, u32[]{:S(2)}, u32[]{:S(2)}) collective-permute-start(f32[8,2048]{1,0:T(8,128)S(1)} %add.28), channel_id=1, source_target_pairs={{0,16},{4,20},{8,24},{12,28},{16,0},{20,4},{24,8},{28,12},{32,48},... | collective-permute-start | bytes 196616 | tf_op jit(solution)/shard_map/ppermute | solution.py:398
  121.7 1.5 %collective-permute-start.5 = (f32[8,128]{1,0:T(8,128)S(1)}, f32[8,128]{1,0:T(8,128)S(1)}, u32[]{:S(2)}, u32[]{:S(2)}) collective-permute-start(f32[8,128]{1,0:T(8,128)S(1)} %broadcast_in_dim.2), channel_id=1, source_target_pairs={{0,1},{1,0},{2,3},{3,2},{4,5},{5,4},{6,7},{7,6},{8,9},{9,8},{10,11... | collective-permute-start | bytes 12296 | tf_op jit(solution)/shard_map/ppermute | solution.py:398
  123.2 2.1 %collective-permute-done.5 = f32[8,128]{1,0:T(8,128)S(1)} collective-permute-done((f32[8,128]{1,0:T(8,128)S(1)}, f32[8,128]{1,0:T(8,128)S(1)}, u32[]{:S(2)}, u32[]{:S(2)}) %collective-permute-start.5) | collective-permute-done | bytes 4128 | tf_op jit(solution)/shard_map/ppermute | solution.py:398
  125.3 1.6 %collective-permute-start.6 = (f32[8,2048]{1,0:T(8,128)S(1)}, f32[8,2048]{1,0:T(8,128)S(1)}, u32[]{:S(2)}, u32[]{:S(2)}) collective-permute-start(f32[8,2048]{1,0:T(8,128)S(1)} %add.29), channel_id=1, source_target_pairs={{0,32},{4,36},{8,40},{12,44},{16,48},{20,52},{24,56},{28,60},{32,0... | collective-permute-start | bytes 196616 | tf_op jit(solution)/shard_map/ppermute | solution.py:398
  126.9 3.0 %collective-permute-start.7 = (f32[8,128]{1,0:T(8,128)S(1)}, f32[8,128]{1,0:T(8,128)S(1)}, u32[]{:S(2)}, u32[]{:S(2)}) collective-permute-start(f32[8,128]{1,0:T(8,128)S(1)} %add.30), channel_id=1, source_target_pairs={{0,2},{1,3},{2,0},{3,1},{4,6},{5,7},{6,4},{7,5},{8,10},{9,11},{10,... | collective-permute-start | bytes 12296 | tf_op jit(solution)/shard_map/ppermute | solution.py:398
  130.0 2.9 %collective-permute-start.8 = (f32[8,2048]{1,0:T(8,128)S(1)}, f32[8,2048]{1,0:T(8,128)S(1)}, u32[]{:S(2)}, u32[]{:S(2)}) collective-permute-start(f32[8,2048]{1,0:T(8,128)S(1)} %add.31), channel_id=1, source_target_pairs={{0,64},{4,68},{8,72},{12,76},{16,80},{20,84},{24,88},{28,92},{32,9... | collective-permute-start | bytes 196616 | tf_op jit(solution)/shard_map/ppermute | solution.py:398
  132.8 2.5 %clip.1 = f32[256,2048]{1,0:T(8,128)} custom-call(bf16[32,128,128]{2,1,0:T(8,128)(2,1)} %all-to-all-done.2.refs_0_, f32[8,128]{1,0:T(8,128)S(1)} %rsqrt_minimum_fusion.refs_1_), custom_call_target="tpu_custom_call" | custom-call | flops 3145728 | bytes 3145728 | tf_op jit(solution)/shard_map/clip/pallas_call | solution.py:292
  135.8 0.6 fusion.2
  (35 shorter events, 1.9 us)
Async XLA Ops:
  1.5 4.6 %collective-permute-start = (bf16[4,2048]{1,0:T(4,128)(2,1)S(1)}, bf16[4,2048]{1,0:T(4,128)(2,1)S(1)}, u32[]{:S(2)}, u32[]{:S(2)}) collective-permute-start(bf16[4,2048]{1,0:T(4,128)(2,1)S(1)} %pad_maximum_fusion), channel_id=1, source_target_pairs={{0,4},{4,8},{8,12},{12,16},{16,20},{20,24},{24,28},{28,32},{32,36}... | collective-permute-start | bytes 49160 | tf_op jit(solution)/shard_map/ppermute | solution.py:408
  6.1 0.6 copy-start.6
  10.7 11.7 %copy-start.2 = (bf16[256,2048]{1,0:T(8,128)(2,1)S(1)}, bf16[256,2048]{1,0:T(8,128)(2,1)}, u32[]{:S(2)}) copy-start(bf16[256,2048]{1,0:T(8,128)(2,1)} %refs_0_.5) | copy-start | bytes 3145732
  10.7 11.7 %copy-start.3 = (bf16[256,2048]{1,0:T(8,128)(2,1)S(1)}, bf16[256,2048]{1,0:T(8,128)(2,1)}, u32[]{:S(2)}) copy-start(bf16[256,2048]{1,0:T(8,128)(2,1)} %refs_1_.7) | copy-start | bytes 3145732
  10.7 52.2 %all-to-all-start = ((bf16[32,192,256]{2,1,0:T(8,128)(2,1)}), bf16[32,192,256]{2,1,0:T(8,128)(2,1)}, u32[]{:S(2)}, u32[]{:S(2)}) async-start(bf16[32,192,256]{2,1,0:T(8,128)(2,1)} %mixed.1), calls=%async_computation | async-start | bytes 6291456 | tf_op jit(solution)/shard_map/all_to_all | solution.py:430
  21.0 3.1 %collective-permute-start.1 = (bf16[4,2048]{1,0:T(4,128)(2,1)S(1)}, bf16[4,2048]{1,0:T(4,128)(2,1)S(1)}, u32[]{:S(2)}, u32[]{:S(2)}) collective-permute-start(bf16[4,2048]{1,0:T(4,128)(2,1)S(1)} %pad_maximum_fusion.1), channel_id=1, source_target_pairs={{4,0},{8,4},{12,8},{16,12},{20,16},{24,20},{28,24},{32,28},{36,32}... | collective-permute-start | bytes 49160 | tf_op jit(solution)/shard_map/ppermute | solution.py:432
  75.8 27.8 %copy-start = (bf16[256,2048]{1,0:T(8,128)(2,1)S(1)}, bf16[256,2048]{1,0:T(8,128)(2,1)}, u32[]{:S(2)}) copy-start(bf16[256,2048]{1,0:T(8,128)(2,1)} %refs_1_.9) | copy-start | bytes 3145732
  75.8 27.8 %copy-start.1 = (bf16[256,2048]{1,0:T(8,128)(2,1)S(1)}, bf16[256,2048]{1,0:T(8,128)(2,1)}, u32[]{:S(2)}) copy-start(bf16[256,2048]{1,0:T(8,128)(2,1)} %refs_2_.7) | copy-start | bytes 3145732
  75.8 27.8 %copy-start.4 = (f32[3,2048]{1,0:T(4,128)S(1)}, f32[3,2048]{1,0:T(4,128)}, u32[]{:S(2)}) copy-start(f32[3,2048]{1,0:T(4,128)} %refs_3_.5) | copy-start | bytes 73732
  75.8 27.8 %copy-start.5 = (f32[3,2048]{1,0:T(4,128)S(1)}, f32[3,2048]{1,0:T(4,128)}, u32[]{:S(2)}) copy-start(f32[3,2048]{1,0:T(4,128)} %refs_4_.3) | copy-start | bytes 73732
  75.8 27.8 %copy-start.7 = (bf16[4,2048]{1,0:T(4,128)(2,1)S(1)}, bf16[4,2048]{1,0:T(4,128)(2,1)}, u32[]{:S(2)}) copy-start(bf16[4,2048]{1,0:T(4,128)(2,1)} %copy-done.6) | copy-start | bytes 49156
  98.9 31.0 %all-to-all-start.2 = ((bf16[32,128,128]{2,1,0:T(8,128)(2,1)}), bf16[32,128,128]{2,1,0:T(8,128)(2,1)}, u32[]{:S(2)}, u32[]{:S(2)}) async-start(bf16[32,128,128]{2,1,0:T(8,128)(2,1)} %get-tuple-element.44), calls=%async_computation.2 | async-start | bytes 2097152 | tf_op jit(solution)/shard_map/all_to_all | solution.py:438
  107.2 1.3 collective-permute-start.2
  108.5 10.4 %collective-permute-start.3 = (f32[8,2048]{1,0:T(8,128)S(1)}, f32[8,2048]{1,0:T(8,128)S(1)}, u32[]{:S(2)}, u32[]{:S(2)}) collective-permute-start(f32[8,2048]{1,0:T(8,128)S(1)} %add.27), channel_id=1, source_target_pairs={{0,8},{4,12},{8,0},{12,4},{16,24},{20,28},{24,16},{28,20},{32,40},... | collective-permute-start | bytes 196616 | tf_op jit(solution)/shard_map/ppermute | solution.py:398
  118.9 6.4 %collective-permute-start.4 = (f32[8,2048]{1,0:T(8,128)S(1)}, f32[8,2048]{1,0:T(8,128)S(1)}, u32[]{:S(2)}, u32[]{:S(2)}) collective-permute-start(f32[8,2048]{1,0:T(8,128)S(1)} %add.28), channel_id=1, source_target_pairs={{0,16},{4,20},{8,24},{12,28},{16,0},{20,4},{24,8},{28,12},{32,48},... | collective-permute-start | bytes 196616 | tf_op jit(solution)/shard_map/ppermute | solution.py:398
  121.7 3.6 %collective-permute-start.5 = (f32[8,128]{1,0:T(8,128)S(1)}, f32[8,128]{1,0:T(8,128)S(1)}, u32[]{:S(2)}, u32[]{:S(2)}) collective-permute-start(f32[8,128]{1,0:T(8,128)S(1)} %broadcast_in_dim.2), channel_id=1, source_target_pairs={{0,1},{1,0},{2,3},{3,2},{4,5},{5,4},{6,7},{7,6},{8,9},{9,8},{10,11... | collective-permute-start | bytes 12296 | tf_op jit(solution)/shard_map/ppermute | solution.py:398
  125.3 4.6 %collective-permute-start.6 = (f32[8,2048]{1,0:T(8,128)S(1)}, f32[8,2048]{1,0:T(8,128)S(1)}, u32[]{:S(2)}, u32[]{:S(2)}) collective-permute-start(f32[8,2048]{1,0:T(8,128)S(1)} %add.29), channel_id=1, source_target_pairs={{0,32},{4,36},{8,40},{12,44},{16,48},{20,52},{24,56},{28,60},{32,0... | collective-permute-start | bytes 196616 | tf_op jit(solution)/shard_map/ppermute | solution.py:398
  126.9 5.9 %collective-permute-start.7 = (f32[8,128]{1,0:T(8,128)S(1)}, f32[8,128]{1,0:T(8,128)S(1)}, u32[]{:S(2)}, u32[]{:S(2)}) collective-permute-start(f32[8,128]{1,0:T(8,128)S(1)} %add.30), channel_id=1, source_target_pairs={{0,2},{1,3},{2,0},{3,1},{4,6},{5,7},{6,4},{7,5},{8,10},{9,11},{10,... | collective-permute-start | bytes 12296 | tf_op jit(solution)/shard_map/ppermute | solution.py:398
  130.0 5.8 %collective-permute-start.8 = (f32[8,2048]{1,0:T(8,128)S(1)}, f32[8,2048]{1,0:T(8,128)S(1)}, u32[]{:S(2)}, u32[]{:S(2)}) collective-permute-start(f32[8,2048]{1,0:T(8,128)S(1)} %add.31), channel_id=1, source_target_pairs={{0,64},{4,68},{8,72},{12,76},{16,80},{20,84},{24,88},{28,92},{32,9... | collective-permute-start | bytes 196616 | tf_op jit(solution)/shard_map/ppermute | solution.py:398

commit v3 on v2

--- a/solution.py
+++ b/solution.py
@@ -13,7 +13,7 @@
 F32 = jnp.float32
 HALF = 64
 MIB = 1 << 20
-SPECTRAL_LIMIT = 62
+SPECTRAL_LIMIT = 60
 LATE_LIMIT = 24
 
 
@@ -48,22 +48,43 @@
     return pltpu.roll(x, HALF, axis=x.ndim - 1)
 
 
-def spectral_kernel(recv, m1, w, wi, m2, factors, gz_out, gh_out, x_v, gz_v, gh_v, y, u, acc, in_sems, out_sems):
-    parts, chans, rows = recv.shape
-    chans //= 3
-    mid = rows // 2
-    group = 16
-    pieces = 3 * chans // 32
-
-    def fetch(i):
-        at = pl.ds(32 * i, 32)
-        return pltpu.make_async_copy(recv.at[:, at, :], x_v.at[:, at, :], in_sems.at[i])
-
-    for i in range(pieces):
-        fetch(i).start()
+def spectral_kernel(recv, m1, w, wi, m2, factors, gz_out, gh_out, x_v, gz_v, gh_v, y, u, in_sems, out_sems):
+    parts, mid = recv.shape[0], recv.shape[2]
+    rows = 2 * mid
+    chans = (recv.shape[1] - 16) // 6
+    group = parts
+    pieces = 3
+
+    def fetch(row, count, n):
+        at = pl.ds(row, count)
+        return pltpu.make_async_copy(recv.at[:, at, :], x_v.at[:, at, :], in_sems.at[n])
+
+    def fetches(i):
+        return [fetch(pl.multiple_of(3 * chans * h + chans * i, 16), chans, 2 * i + h) for h in range(2)]
+
+    edges_in = fetch(6 * chans, 16, 2 * pieces)
+    mixed_in, others_in = fetches(1), fetches(2) + fetches(0)
+    for copy in [edges_in] + mixed_in + others_in:
+        copy.start()
+
+    for copy in [edges_in] + mixed_in:
+        copy.wait()
+    edges = x_v[:, 6 * chans : 6 * chans + 16, :].astype(F32)
+    edges = edges[:, :8] + edges[:, 8:]
+    ahead = jnp.concatenate([jnp.zeros((1, 8, 128), F32), edges[:-1]], axis=0)
+    shorts = edges + pltpu.roll(ahead, 4, axis=1)
+    starts = shorts * pltpu.roll(shorts, 6, axis=1)
+    lane = lax.broadcasted_iota(jnp.int32, (chans, mid), 1)
+    for p in range(parts):
+        if p % 16 == 0:
+            turned = starts[p : p + 16].reshape(128, 128).T[:chans]
+        here = pltpu.roll(turned, (128 - 8 * (p % 16)) % 128, axis=1)
+        old = x_v[p, chans : 2 * chans, :].astype(F32)
+        x_v[p, chans : 2 * chans, :] = jnp.where(lane < 2, here, old).astype(BF)
 
     def forward(base):
-        x = x_v[:, pl.ds(base, 16), :].astype(F32)
+        halves = [x_v[:, pl.ds(pl.multiple_of(3 * chans * h + base, 16), 16), :] for h in range(2)]
+        x = jnp.concatenate(halves, axis=2).astype(F32)
         out = []
         for q in range(2):
             xq = x[:, 8 * q : 8 * q + 8, :].reshape(parts * 8, rows).astype(BF)
@@ -79,11 +100,17 @@
             y[0, k, pl.ds(base, 16), :] = jnp.concatenate(sums, axis=0).astype(BF)
             y[1, k, pl.ds(base, 16), :] = jnp.concatenate(gaps, axis=0).astype(BF)
 
-    @pl.loop(0, pieces)
-    def _(i):
-        fetch(i).wait()
-        for q in range(2):
-            forward(pl.multiple_of(32 * i + 16 * q, 16))
+    @pl.loop(1, pieces + 1)
+    def _(n):
+        i = lax.rem(n, pieces)
+
+        @pl.when(i != 1)
+        def _():
+            for copy in fetches(i):
+                copy.wait()
+
+        for q in range(chans // 16):
+            forward(pl.multiple_of(chans * i + 16 * q, 16))
 
     @pl.loop(0, parts // group)
     def _(kk):
@@ -112,8 +139,6 @@
                 u[2 * k, :, cols] = (re * c - im * s).astype(BF)
                 u[2 * k + 1, :, cols] = (im * c + re * s).astype(BF)
 
-    acc[...] = jnp.zeros_like(acc)
-
     def backward(base):
         piece = u[:, pl.ds(base, 16), :].astype(F32)
         outs = []
@@ -126,42 +151,34 @@
     tiles = chans // 16
 
     def store(target, scratch, first, row):
-        at = pl.ds(pl.multiple_of(row, 16), 16)
+        at = pl.ds(row, 16)
         return pltpu.make_async_copy(scratch.at[:, at, :], target.at[:, at, :], out_sems.at[first])
 
-    @pl.loop(0, tiles // 2)
-    def _(i):
-        for q in range(2):
-            base = pl.multiple_of(32 * i + 16 * q, 16)
-            grad = backward(chans + base)
-            for h in range(2):
-                gh_v[:, pl.ds(chans * h + base, 16), :] = grad[:, :, mid * h : mid * h + mid].astype(BF)
-                store(gh_out, gh_v, tiles * h + 2 * i + q, chans * h + base).start()
-            acc[...] += jnp.sum((grad * grad).reshape(parts * 2, 8, rows), axis=0)
-
-    @pl.loop(0, tiles // 2)
-    def _(i):
-        for q in range(2):
-            base = pl.multiple_of(32 * i + 16 * q, 16)
-            grad = backward(base)
-            for h in range(2):
-                gz_v[:, pl.ds(chans * h + base, 16), :] = grad[:, :, mid * h : mid * h + mid].astype(BF)
-                store(gz_out, gz_v, 2 * tiles + tiles * h + 2 * i + q, chans * h + base).start()
-
-    total = jnp.sum(jnp.sum(acc[...], axis=0, keepdims=True), axis=1, keepdims=True)
+    squares = jnp.zeros((8, rows), F32)
+    for i in range(tiles):
+        grad = backward(chans + 16 * i)
+        for h in range(2):
+            row = chans * h + 16 * i
+            gh_v[:, row : row + 16, :] = grad[:, :, mid * h : mid * h + mid].astype(BF)
+            store(gh_out, gh_v, tiles * h + i, row).start()
+        squares += jnp.sum((grad * grad).reshape(parts * 2, 8, rows), axis=0)
+    for i in range(tiles):
+        grad = backward(16 * i)
+        for h in range(2):
+            row = chans * h + 16 * i
+            gz_v[:, row : row + 16, :] = grad[:, :, mid * h : mid * h + mid].astype(BF)
+            store(gz_out, gz_v, 2 * tiles + tiles * h + i, row).start()
+
+    total = jnp.sum(jnp.sum(squares, axis=0, keepdims=True), axis=1, keepdims=True)
     coarse = total.astype(BF).astype(F32)
     fine = (total - coarse).astype(BF).astype(F32)
     row = lax.broadcasted_iota(jnp.int32, (16, 128), 0)
     sums = jnp.where(row == 2, coarse, jnp.where(row == 3, fine, 0.0))
-    lane = lax.broadcasted_iota(jnp.int32, (16, mid), 1)
-    pick = jnp.where((lane == lax.broadcasted_iota(jnp.int32, (16, mid), 0)) & (lane < 2), 1.0, 0.0).astype(BF)
-    firsts = gz_v[:, :chans, :].reshape(parts * chans, mid)
-    edges = lax.dot_general(pick, firsts, (((1,), (1,)), ((), ())), preferred_element_type=F32)
     for p in range(parts):
         after = jnp.zeros((16, 128), F32)
         if p + 1 < parts:
-            at = (p + 1) // 2 * 128
-            after = edges[:, at : at + 128]
+            at = (p + 1) // 2 * 2
+            after = gz_v[at : at + 2, :chans, :].reshape(2 * chans, mid).T[:16].astype(F32)
             if (p + 1) % 2:
                 after = swap_halves(after)
         gz_v[p, 2 * chans : 2 * chans + 16, :] = jnp.where(row < 2, after, sums).astype(BF)
@@ -174,7 +191,7 @@
 
 def spectral(recv, parts, rows):
     tables = transform_tables(parts, rows)
-    chans = recv.shape[1] // 3
+    chans = (recv.shape[1] - 16) // 6
     mid = rows // 2
     vmem = pl.BlockSpec(memory_space=pltpu.VMEM)
     anywhere = pl.BlockSpec(memory_space=pl.ANY)
@@ -193,8 +210,7 @@
             pltpu.VMEM((parts, 2 * chans, mid), BF),
             pltpu.VMEM((2, parts, 3 * chans, rows), BF),
             pltpu.VMEM((2 * parts, 2 * chans, rows), BF),
-            pltpu.VMEM((8, rows), F32),
-            pltpu.SemaphoreType.DMA((3 * chans // 32,)),
+            pltpu.SemaphoreType.DMA((7,)),
             pltpu.SemaphoreType.DMA((4 * (chans // 16) + 1,)),
         ],
         compiler_params=pltpu.CompilerParams(vmem_limit_bytes=SPECTRAL_LIMIT * MIB),
@@ -229,7 +245,7 @@
     return one, two
 
 
-def stream(body, name, ins, smalls, outs, parts_of, chunks, limit, alias=None):
+def stream(body, name, ins, smalls, outs, parts_of, chunks, limit):
     def size(shape):
         return (shape[0] // chunks,) + tuple(shape[1:]) if len(shape) == 3 else (shape[0], shape[1] // chunks)
 
@@ -241,13 +257,12 @@
         at = ref.at[pl.ds(c * per, per)]
         return at if rows is None else ref.at[pl.ds(c * per, per), pl.ds(rows[0], rows[1]), :]
 
-    extra = [] if alias is None else [alias]
     n_in, n_small, n_out, n_part = len(ins), len(smalls), len(outs), len(parts_of)
 
     def kernel(*refs):
         refs = list(refs)
         take = lambda n: [refs.pop(0) for _ in range(n)]
-        in_refs, small_refs, _, out_refs = take(n_in), take(n_small), take(len(extra)), take(n_out)
+        in_refs, small_refs, out_refs = take(n_in), take(n_small), take(n_out)
         in_v, small_v, out_v = take(n_in), take(n_small), take(n_part)
         in_sems, small_sems, out_sems = refs
 
@@ -291,15 +306,14 @@
     anywhere = pl.BlockSpec(memory_space=pl.ANY)
     return pl.pallas_call(
         kernel,
-        in_specs=[anywhere] * (n_in + n_small + len(extra)),
+        in_specs=[anywhere] * (n_in + n_small),
         out_specs=[anywhere] * n_out,
         out_shape=outs,
         scratch_shapes=scratch,
-        input_output_aliases={} if alias is None else {n_in + n_small: 0},
         compiler_params=pltpu.CompilerParams(vmem_limit_bytes=limit * MIB),
         cost_estimate=pl.CostEstimate(flops=total, bytes_accessed=total, transcendentals=0),
         name=name,
-    )(*ins, *smalls, *extra)
+    )(*ins, *smalls)
 
 
 def columns_of(ref, c, lanes):
@@ -310,29 +324,36 @@
     return taps[0:1] * x0 + taps[1:2] * x1 + taps[2:3] * x2
 
 
-def turn_out(x, out):
-    rows, lanes = x.shape
+def pack_body(c, ins, smalls, outs):
+    cot, gate, filt, key, value = ins
+    out = outs[0]
+    rows, lanes = cot.shape
     mid = rows // 2
-    x = x.astype(BF)
+    kt, vt = (columns_of(x, c, lanes) for x in smalls)
+    none = jnp.zeros((2, lanes), F32)
+    edges, shorts = [[], []], []
+    for x, taps in ((key, kt), (value, vt)):
+        x = x[...].astype(F32)
+        shorts.append(short(taps, x, *delayed(x, none)))
+        last, prior = x[rows - 1 : rows], x[rows - 2 : rows - 1]
+        edges[0].append(shorts[-1][0:2])
+        edges[1] += [taps[1:2] * last + taps[2:3] * prior, taps[2:3] * last]
+    edge = jnp.concatenate(edges[0] + edges[1], axis=0)
+    coarse = edge.astype(BF).astype(F32)
+    edge = jnp.concatenate([coarse, edge - coarse], axis=0)
+    grad = cot[...].astype(F32) * gate[...].astype(F32)
+    for n, x in enumerate((filt[...], shorts[0] * shorts[1], grad)):
+        x = x.astype(BF)
+        for j in range(lanes // 128):
+            for h in range(2):
+                turned = x[mid * h : mid * h + mid, 128 * j : 128 * j + 128].T
+                at = 3 * HALF * h + HALF * n
+                out[2 * j, at : at + HALF] = turned[:HALF]
+                out[2 * j + 1, at : at + HALF] = turned[HALF:]
     for j in range(lanes // 128):
-        cols = slice(128 * j, 128 * j + 128)
-        turned = jnp.concatenate([x[:mid, cols].T, x[mid:, cols].T], axis=1)
-        out[2 * j] = turned[:HALF]
-        out[2 * j + 1] = turned[HALF:]
-
-
-def known_body(c, ins, smalls, outs):
-    cot, gate, filt = ins
-    turn_out(filt[...], outs[0])
-    turn_out(cot[...].astype(F32) * gate[...].astype(F32), outs[1])
-
-
-def mixed_body(c, ins, smalls, outs):
-    kf, vf = (x[...].astype(F32) for x in ins)
-    kt, vt, before = (columns_of(x, c, kf.shape[1]).astype(F32) for x in smalls)
-    key_short = short(kt, kf, *delayed(kf, before[0:2]))
-    value_short = short(vt, vf, *delayed(vf, before[2:4]))
-    turn_out(key_short * value_short, outs[0])
+        tile = edge[:, 128 * j : 128 * j + 128]
+        out[2 * j, 6 * HALF :] = tile.astype(BF)
+        out[2 * j + 1, 6 * HALF :] = swap_halves(tile).astype(BF)
 
 
 def gate_body(c, ins, smalls, outs):
@@ -398,40 +419,34 @@
     return x + lax.ppermute(x, axis, [(i, i ^ step) for i in range(lax.axis_size(axis))])
 
 
+def quarter_sum(x, axis):
+    size = lax.axis_size(axis)
+    one, two, three = (lax.ppermute(x, axis, [(i, (i + n * size // 4) % size) for i in range(size)]) for n in (1, 2, 3))
+    return (x + two) + (one + three)
+
+
 def shards(gate_in, key_in, value_in, conv_out, cotangent, long_filter, key_taps, value_taps, *, parts, others):
     rows, columns = key_in.shape
     shape = jax.ShapeDtypeStruct
     block = shape((rows, columns), BF)
-    send_shape = shape((parts, 3 * HALF, rows), BF)
     tails = jnp.concatenate([key_in[-2:], value_in[-2:]], axis=0)
     heads = jnp.concatenate([key_in[:2], value_in[:2]], axis=0)
-    before = lax.ppermute(tails, "seq", [(i, i + 1) for i in range(parts - 1)])
-    (known,) = stream(
-        known_body,
-        "known",
-        (cotangent, gate_in, long_filter),
-        (),
-        (send_shape,),
-        ((0, (0, HALF)), (0, (2 * HALF, HALF))),
+    (send,) = stream(
+        pack_body,
+        "pack",
+        (cotangent, gate_in, long_filter, key_in, value_in),
+        (key_taps, value_taps),
+        (shape((parts, 6 * HALF + 16, rows // 2), BF),),
+        ((0, None),),
         4,
         60,
     )
-    (send,) = stream(
-        mixed_body,
-        "mixed",
-        (key_in, value_in),
-        (key_taps, value_taps, before),
-        (send_shape,),
-        ((0, (HALF, HALF)),),
-        4,
-        60,
-        alias=known,
-    )
     recv = lax.all_to_all(send, "seq", 0, 0)
-    send, heads = lax.optimization_barrier((send, heads))
+    send, tails, heads = lax.optimization_barrier((send, tails, heads))
+    before = lax.ppermute(tails, "seq", [(i, i + 1) for i in range(parts - 1)])
     after = lax.ppermute(heads, "seq", [(i + 1, i) for i in range(parts - 1)])
     (gate_grad,) = stream(gate_body, "gate", (cotangent, conv_out), (), (block,), ((0, None),), 4, 16)
-    recv, gate_grad, after = lax.optimization_barrier((recv, gate_grad, after))
+    recv, gate_grad, before, after = lax.optimization_barrier((recv, gate_grad, before, after))
     gz_send, gh_send = spectral(recv, parts, rows)
     gz_recv = lax.all_to_all(gz_send, "seq", 0, 0)
     gz_recv, gh_send = lax.optimization_barrier((gz_recv, gh_send))
@@ -447,6 +462,10 @@
         LATE_LIMIT,
     )
     late, taps = lax.optimization_barrier((gz_recv, taps))
+    total = jnp.sum(late[:, 2 * HALF + 2 : 2 * HALF + 4, :].astype(F32), axis=(0, 1))
+    total = jnp.broadcast_to(total[None], (8, total.shape[0]))
+    taps = tree_step(taps, "seq", 1)
+    late, taps = lax.optimization_barrier((late, taps))
     key_grad, value_grad = stream(
         inputs_body,
         "inputs",
@@ -457,26 +476,15 @@
         4,
         LATE_LIMIT,
     )
-    total = jnp.sum(late[:, 2 * HALF + 2 : 2 * HALF + 4, :].astype(F32), axis=(0, 1))
-    total = jnp.broadcast_to(total[None], (8, total.shape[0]))
-    step, other, turns = 1, 1, 0
-    while 2 * step < parts:
-        if turns % 2 == 1 and other < others:
-            taps, total = lax.optimization_barrier((taps, total))
-            total = tree_step(total, "chan", other)
-            other *= 2
-        taps = tree_step(taps, "seq", step)
-        step *= 2
-        turns += 1
-        if turns == 2:
-            taps, key_grad, value_grad = lax.optimization_barrier((taps, key_grad, value_grad))
-    while other < others:
-        total = tree_step(total, "chan", other)
-        other *= 2
+    taps = quarter_sum(taps, "seq")
+    total = tree_step(total, "chan", 1)
+    taps, total, key_grad, value_grad = lax.optimization_barrier((taps, total, key_grad, value_grad))
+    total = tree_step(total, "chan", 3)
+    taps = tree_step(taps, "seq", 2)
     count = rows * columns * parts * others
     scale = jnp.minimum(1.0, 1.0 / jnp.sqrt(total / count + 1e-6))
     taps, gh_recv = lax.optimization_barrier((taps, gh_recv))
-    taps = tree_step(taps, "seq", parts // 2)
+    taps = tree_step(taps, "seq", 6)
     (filter_grad,) = stream(
         clip_body, "clip", (gh_recv,), (scale,), (shape((rows, columns), F32),), ((0, None),), 4, LATE_LIMIT
     )

time: 137 us -> 128 us (0.934)
  waiting for transfers between devices: 46.8 us -> 39.6 us
  Pallas kernels: 32.2 us -> 30.2 us
    ppermute x7 -> x5, waiting for transfers between devices: 7.61 us -> 0.76 us  [tree_step(): lax.ppermute(x, axis, [(i, i ^ step) for i in range(lax.axis_size(axis))])]
    ppermute x0 -> x3, starting transfers between devices: none -> 6.6 us  [quarter_sum(): lax.ppermute(x, axis, [(i, (i + n * size // 4) % size) for i in range(siz...]
    ppermute x7 -> x5, starting transfers between devices: 13.6 us -> 8.37 us  [tree_step(): lax.ppermute(x, axis, [(i, i ^ step) for i in range(lax.axis_size(axis))])]
    all_to_all x1, waiting for transfers between devices: 38.7 us -> 36.9 us  [shards(): recv = lax.all_to_all(send, 'seq', 0, 0)]
    ppermute x0 -> x3, waiting for transfers between devices: none -> 1.55 us  [quarter_sum(): lax.ppermute(x, axis, [(i, (i + n * size // 4) % size) for i in range(siz...]
    all_to_all x1, starting transfers between devices: 10.3 us -> 8.81 us  [shards(): recv = lax.all_to_all(send, 'seq', 0, 0)]
    pallas_call x6 -> x5, Pallas kernels: 19.3 us -> 18.1 us  [stream(): pl.pallas_call(kernel, in_specs=[anywhere] * (n_in + n_small), out_specs=...]
  transfers between devices with their start and end apart: 11 -> 12, of which waited for: 6 -> 5; matrix products, arithmetic and copies ran while one was open for 0% -> 0% of each run, Pallas kernels for 11% -> 9%
where the time goes in v3:
time: 128 us
  waiting for transfers between devices  39.6 us (31%)
  starting transfers between devices  31.9 us (25%)
  Pallas kernels  30.2 us (24%)
  blocking collectives  23 us (18%)
  local copies, waits for them, and re-layouts  1.93 us (2%)
    all_to_all x1, waiting for transfers between devices, shards(): recv = lax.all_to_all(send, 'seq', 0, 0)  36.9 us
    all_to_all x1, blocking collectives, shards(): gz_recv = lax.all_to_all(gz_send, 'seq', 0, 0)  23 us
    pallas_call x5, Pallas kernels, stream(): pl.pallas_call(kernel, in_specs=[anywhere] * (n_in + n_small), out_specs=...  18.1 us
    pallas_call x1, Pallas kernels, spectral(): pl.pallas_call(spectral_kernel, out_shape=(jax.ShapeDtypeStruct((parts, 2...  12 us
    all_to_all x1, starting transfers between devices, shards(): recv = lax.all_to_all(send, 'seq', 0, 0)  8.81 us
    ppermute x5, starting transfers between devices, tree_step(): lax.ppermute(x, axis, [(i, i ^ step) for i in range(lax.axis_size(axis))])  8.37 us
    ppermute x3, starting transfers between devices, quarter_sum(): lax.ppermute(x, axis, [(i, (i + n * size // 4) % size) for i in range(siz...  6.6 us
    all_to_all x1, starting transfers between devices, shards(): gh_recv = lax.all_to_all(gh_send, 'seq', 0, 0)  4.66 us
  transfers between devices with their start and end apart: 12, of which 5 were waited for; matrix products, arithmetic and copies ran while one was open for 0% of the time, Pallas kernels for 9%

profile of v3, /device:TPU:0, one launch (start us, length us, event | category | flops | bytes accessed | tf_op | source)
XLA Modules:
  0.0 127.5 jit_solution(12882176301562731904)
XLA Ops:
  0.6 6.1 %pack.1 = bf16[32,400,128]{2,1,0:T(8,128)(2,1)} custom-call(bf16[256,2048]{1,0:T(8,128)(2,1)} %refs_0_.3, bf16[256,2048]{1,0:T(8,128)(2,1)} %refs_1_.4, f32[256,2048]{1,0:T(8,128)} %refs_2_.3, bf16[256,2048]{1,0:T(8,128)(2,1)} %refs_1_.7, bf16[256,2048]{1,0:T(8,128)(2,1)} %refs_2_.5, f32[3,2048]{1,0:T(4,128)} %refs_3_.5, f32[3,2048]{1,0:T(4,128)} %refs_4_.5), custom_call_target="tpu_custom_call" | custom-call | flops 9568256 | bytes 9568256 | tf_op jit(solution)/shard_map/pack/pallas_call | solution.py:307
  6.7 8.8 %all-to-all-start = ((bf16[32,400,128]{2,1,0:T(8,128)(2,1)}), bf16[32,400,128]{2,1,0:T(8,128)(2,1)}, u32[]{:S(2)}, u32[]{:S(2)}) async-start(bf16[32,400,128]{2,1,0:T(8,128)(2,1)} %pack.1), calls=%async_computation | async-start | bytes 6553600 | tf_op jit(solution)/shard_map/all_to_all | solution.py:444
  15.7 2.1 %collective-permute-start = (bf16[4,2048]{1,0:T(4,128)(2,1)S(1)}, bf16[4,2048]{1,0:T(4,128)(2,1)S(1)}, u32[]{:S(2)}, u32[]{:S(2)}) collective-permute-start(bf16[4,2048]{1,0:T(4,128)(2,1)S(1)} %get-tuple-element.28), channel_id=1, source_target_pairs={{0,4},{4,8},{8,12},{12,16},{16,20},{20,24},{24,28},{28,32},{32,36}... | collective-permute-start | bytes 49160 | tf_op jit(solution)/shard_map/ppermute | solution.py:446
  17.8 1.3 %collective-permute-start.1 = (bf16[4,2048]{1,0:T(4,128)(2,1)S(1)}, bf16[4,2048]{1,0:T(4,128)(2,1)S(1)}, u32[]{:S(2)}, u32[]{:S(2)}) collective-permute-start(bf16[4,2048]{1,0:T(4,128)(2,1)S(1)} %get-tuple-element.29), channel_id=1, source_target_pairs={{4,0},{8,4},{12,8},{16,12},{20,16},{24,20},{28,24},{32,28},{36,32}... | collective-permute-start | bytes 49160 | tf_op jit(solution)/shard_map/ppermute | solution.py:447
  19.1 1.2 copy-done.3
  20.3 1.3 %gate.1 = bf16[256,2048]{1,0:T(8,128)(2,1)} custom-call(bf16[256,2048]{1,0:T(8,128)(2,1)S(1)} %copy-done.2, bf16[256,2048]{1,0:T(8,128)(2,1)S(1)} %copy-done.3), custom_call_target="tpu_custom_call" | custom-call | flops 3145728 | bytes 3145728 | tf_op jit(solution)/shard_map/gate/pallas_call | solution.py:307
  21.7 0.4 collective-permute-done.1.refs_6_
  22.0 36.9 %all-to-all-done.recv = bf16[32,400,128]{2,1,0:T(8,128)(2,1)} async-done(((bf16[32,400,128]{2,1,0:T(8,128)(2,1)}), bf16[32,400,128]{2,1,0:T(8,128)(2,1)}, u32[]{:S(2)}, u32[]{:S(2)}) %all-to-all-start) | async-done | bytes 3276832 | tf_op jit(solution)/shard_map/all_to_all | solution.py:444
  58.9 12.0 %spectral.1 = (bf16[32,144,128]{2,1,0:T(8,128)(2,1)}, bf16[32,128,128]{2,1,0:T(8,128)(2,1)}) custom-call(bf16[32,400,128]{2,1,0:T(8,128)(2,1)} %all-to-all-done.recv, bf16[512,256]{1,0:T(8,128)(2,1)} %constant.19.clone.m1, bf16[2,256,256]{2,1,0:T(8,128)(2,1)} %constant.20.clone.w, bf16[2,256,256]{2,1,0:T(8,128)(2,1)} %constant.21.clone.wi, ...), custom_call_target="tpu_custom_call" | custom-call | flops 5368709120 | bytes 7340032 | tf_op jit(solution)/shard_map/spectral/pallas_call | solution.py:199
  71.0 23.0 %all_to_all.15.refs_0_ = bf16[32,144,128]{2,1,0:T(8,128)(2,1)S(1)} all-to-all(bf16[32,144,128]{2,1,0:T(8,128)(2,1)} %get-tuple-element.32), channel_id=1, replica_groups=mesh['seq'=32,'chan'=4] {'seq'}, dimensions={0} | all-to-all | bytes 2359296 | tf_op jit(solution)/shard_map/all_to_all | solution.py:451
  94.0 4.7 %all-to-all-start.2 = ((bf16[32,128,128]{2,1,0:T(8,128)(2,1)}), bf16[32,128,128]{2,1,0:T(8,128)(2,1)}, u32[]{:S(2)}, u32[]{:S(2)}) async-start(bf16[32,128,128]{2,1,0:T(8,128)(2,1)} %get-tuple-element.46), calls=%async_computation.2 | async-start | bytes 2097152 | tf_op jit(solution)/shard_map/all_to_all | solution.py:453
  98.7 3.5 %taps.1 = f32[8,2048]{1,0:T(8,128)S(1)} custom-call(bf16[32,144,128]{2,1,0:T(8,128)(2,1)S(1)} %all_to_all.15.refs_0_, bf16[256,2048]{1,0:T(8,128)(2,1)S(1)} %copy-done, bf16[256,2048]{1,0:T(8,128)(2,1)S(1)} %copy-done.1, f32[3,2048]{1,0:T(4,128)S(1)} %copy-done.4, f32[3,2048]{1,0:T(4,128)S(1)} %copy-done.5, bf16[4,2048]{1,0:T(4,128)(2,1)S(1)} %collective-permute-done.refs_5_), custom_call_target="tpu_custom_call" | custom-call | flops 3342336 | bytes 3342336 | tf_op jit(solution)/shard_map/taps/pallas_call | solution.py:307
  102.4 1.6 %collective-permute-start.6 = (f32[8,128]{1,0:T(8,128)S(1)}, f32[8,128]{1,0:T(8,128)S(1)}, u32[]{:S(2)}, u32[]{:S(2)}) collective-permute-start(f32[8,128]{1,0:T(8,128)S(1)} %broadcast_in_dim.2), channel_id=1, source_target_pairs={{0,1},{1,0},{2,3},{3,2},{4,5},{5,4},{6,7},{7,6},{8,9},{9,8},{10,11... | collective-permute-start | bytes 12296 | tf_op jit(solution)/shard_map/ppermute | solution.py:419
  104.0 3.4 %collective-permute-start.3 = (f32[8,2048]{1,0:T(8,128)S(1)}, f32[8,2048]{1,0:T(8,128)S(1)}, u32[]{:S(2)}, u32[]{:S(2)}) collective-permute-start(f32[8,2048]{1,0:T(8,128)S(1)} %add.30), channel_id=1, source_target_pairs={{0,64},{4,68},{8,72},{12,76},{16,80},{20,84},{24,88},{28,92},{32,9... | collective-permute-start | bytes 196616 | tf_op jit(solution)/shard_map/ppermute | solution.py:424
  107.3 0.6 collective-permute-start.4
  108.0 2.6 %collective-permute-start.5 = (f32[8,2048]{1,0:T(8,128)S(1)}, f32[8,2048]{1,0:T(8,128)S(1)}, u32[]{:S(2)}, u32[]{:S(2)}) collective-permute-start(f32[8,2048]{1,0:T(8,128)S(1)} %add.30), channel_id=1, source_target_pairs={{0,96},{4,100},{8,104},{12,108},{16,112},{20,116},{24,120},{28,124... | collective-permute-start | bytes 196616 | tf_op jit(solution)/shard_map/ppermute | solution.py:424
  110.6 4.8 %inputs.1 = (bf16[256,2048]{1,0:T(8,128)(2,1)}, bf16[256,2048]{1,0:T(8,128)(2,1)}) custom-call(bf16[32,144,128]{2,1,0:T(8,128)(2,1)S(1)} %all_to_all.15.refs_0_, bf16[256,2048]{1,0:T(8,128)(2,1)S(1)} %copy-done, bf16[256,2048]{1,0:T(8,128)(2,1)S(1)} %copy-done.1, f32[3,2048]{1,0:T(4,128)S(1)} %copy-done.4, f32[3,2048]{1,0:T(4,128)S(1)} %copy-done.5, ...), custom_call_target="tpu_custom_call" | custom-call | flops 5373952 | bytes 5373952 | tf_op jit(solution)/shard_map/inputs/pallas_call | solution.py:307
  115.4 1.5 %collective-permute-done.4 = f32[8,2048]{1,0:T(8,128)S(1)} collective-permute-done((f32[8,2048]{1,0:T(8,128)S(1)}, f32[8,2048]{1,0:T(8,128)S(1)}, u32[]{:S(2)}, u32[]{:S(2)}) %collective-permute-start.4) | collective-permute-done | bytes 65568 | tf_op jit(solution)/shard_map/ppermute | solution.py:424
  117.0 1.4 %collective-permute-start.7 = (f32[8,2048]{1,0:T(8,128)S(1)}, f32[8,2048]{1,0:T(8,128)S(1)}, u32[]{:S(2)}, u32[]{:S(2)}) collective-permute-start(f32[8,2048]{1,0:T(8,128)S(1)} %add_add_fusion), channel_id=1, source_target_pairs={{0,8},{4,12},{8,0},{12,4},{16,24},{20,28},{24,16},{28,20},{32,40},... | collective-permute-start | bytes 196616 | tf_op jit(solution)/shard_map/ppermute | solution.py:419
  118.3 2.7 %collective-permute-start.8 = (f32[8,128]{1,0:T(8,128)S(1)}, f32[8,128]{1,0:T(8,128)S(1)}, u32[]{:S(2)}, u32[]{:S(2)}) collective-permute-start(f32[8,128]{1,0:T(8,128)S(1)} %broadcast_add_fusion), channel_id=1, source_target_pairs={{0,3},{1,2},{2,1},{3,0},{4,7},{5,6},{6,5},{7,4},{8,11},{9,10},{10,... | collective-permute-start | bytes 12296 | tf_op jit(solution)/shard_map/ppermute | solution.py:419
  121.3 2.6 %collective-permute-start.9 = (f32[8,2048]{1,0:T(8,128)S(1)}, f32[8,2048]{1,0:T(8,128)S(1)}, u32[]{:S(2)}, u32[]{:S(2)}) collective-permute-start(f32[8,2048]{1,0:T(8,128)S(1)} %add.35), channel_id=1, source_target_pairs={{0,24},{4,28},{8,16},{12,20},{16,8},{20,12},{24,0},{28,4},{32,56},... | collective-permute-start | bytes 196616 | tf_op jit(solution)/shard_map/ppermute | solution.py:419
  123.9 2.5 %clip.1 = f32[256,2048]{1,0:T(8,128)} custom-call(bf16[32,128,128]{2,1,0:T(8,128)(2,1)} %all-to-all-done.2.refs_0_, f32[8,128]{1,0:T(8,128)S(1)} %rsqrt_minimum_fusion.refs_1_), custom_call_target="tpu_custom_call" | custom-call | flops 3145728 | bytes 3145728 | tf_op jit(solution)/shard_map/clip/pallas_call | solution.py:307
  126.4 0.5 collective-permute-done.9
  126.9 0.6 fusion.2
  (31 shorter events, 0.7 us)
Async XLA Ops:
  6.7 8.9 %copy-start = (bf16[256,2048]{1,0:T(8,128)(2,1)S(1)}, bf16[256,2048]{1,0:T(8,128)(2,1)}, u32[]{:S(2)}) copy-start(bf16[256,2048]{1,0:T(8,128)(2,1)} %refs_1_.7) | copy-start | bytes 3145732
  6.7 8.9 %copy-start.1 = (bf16[256,2048]{1,0:T(8,128)(2,1)S(1)}, bf16[256,2048]{1,0:T(8,128)(2,1)}, u32[]{:S(2)}) copy-start(bf16[256,2048]{1,0:T(8,128)(2,1)} %refs_2_.5) | copy-start | bytes 3145732
  6.7 12.4 %copy-start.2 = (bf16[256,2048]{1,0:T(8,128)(2,1)S(1)}, bf16[256,2048]{1,0:T(8,128)(2,1)}, u32[]{:S(2)}) copy-start(bf16[256,2048]{1,0:T(8,128)(2,1)} %refs_0_.3) | copy-start | bytes 3145732
  6.7 52.2 %all-to-all-start = ((bf16[32,400,128]{2,1,0:T(8,128)(2,1)}), bf16[32,400,128]{2,1,0:T(8,128)(2,1)}, u32[]{:S(2)}, u32[]{:S(2)}) async-start(bf16[32,400,128]{2,1,0:T(8,128)(2,1)} %pack.1), calls=%async_computation | async-start | bytes 6553600 | tf_op jit(solution)/shard_map/all_to_all | solution.py:444
  15.7 6.0 %collective-permute-start = (bf16[4,2048]{1,0:T(4,128)(2,1)S(1)}, bf16[4,2048]{1,0:T(4,128)(2,1)S(1)}, u32[]{:S(2)}, u32[]{:S(2)}) collective-permute-start(bf16[4,2048]{1,0:T(4,128)(2,1)S(1)} %get-tuple-element.28), channel_id=1, source_target_pairs={{0,4},{4,8},{8,12},{12,16},{16,20},{20,24},{24,28},{28,32},{32,36}... | collective-permute-start | bytes 49160 | tf_op jit(solution)/shard_map/ppermute | solution.py:446
  17.8 4.2 %collective-permute-start.1 = (bf16[4,2048]{1,0:T(4,128)(2,1)S(1)}, bf16[4,2048]{1,0:T(4,128)(2,1)S(1)}, u32[]{:S(2)}, u32[]{:S(2)}) collective-permute-start(bf16[4,2048]{1,0:T(4,128)(2,1)S(1)} %get-tuple-element.29), channel_id=1, source_target_pairs={{4,0},{8,4},{12,8},{16,12},{20,16},{24,20},{28,24},{32,28},{36,32}... | collective-permute-start | bytes 49160 | tf_op jit(solution)/shard_map/ppermute | solution.py:447
  19.1 1.2 copy-start.3
  71.0 27.7 %copy-start.4 = (f32[3,2048]{1,0:T(4,128)S(1)}, f32[3,2048]{1,0:T(4,128)}, u32[]{:S(2)}) copy-start(f32[3,2048]{1,0:T(4,128)} %refs_3_.5) | copy-start | bytes 73732
  71.0 27.7 %copy-start.5 = (f32[3,2048]{1,0:T(4,128)S(1)}, f32[3,2048]{1,0:T(4,128)}, u32[]{:S(2)}) copy-start(f32[3,2048]{1,0:T(4,128)} %refs_4_.5) | copy-start | bytes 73732
  94.0 27.4 %all-to-all-start.2 = ((bf16[32,128,128]{2,1,0:T(8,128)(2,1)}), bf16[32,128,128]{2,1,0:T(8,128)(2,1)}, u32[]{:S(2)}, u32[]{:S(2)}) async-start(bf16[32,128,128]{2,1,0:T(8,128)(2,1)} %get-tuple-element.46), calls=%async_computation.2 | async-start | bytes 2097152 | tf_op jit(solution)/shard_map/all_to_all | solution.py:453
  102.2 1.8 %collective-permute-start.2 = (f32[8,2048]{1,0:T(8,128)S(1)}, f32[8,2048]{1,0:T(8,128)S(1)}, u32[]{:S(2)}, u32[]{:S(2)}) collective-permute-start(f32[8,2048]{1,0:T(8,128)S(1)} %taps.1), channel_id=1, source_target_pairs={{0,4},{4,0},{8,12},{12,8},{16,20},{20,16},{24,28},{28,24},{32,36},... | collective-permute-start | bytes 196616 | tf_op jit(solution)/shard_map/ppermute | solution.py:419
  102.4 8.2 %collective-permute-start.6 = (f32[8,128]{1,0:T(8,128)S(1)}, f32[8,128]{1,0:T(8,128)S(1)}, u32[]{:S(2)}, u32[]{:S(2)}) collective-permute-start(f32[8,128]{1,0:T(8,128)S(1)} %broadcast_in_dim.2), channel_id=1, source_target_pairs={{0,1},{1,0},{2,3},{3,2},{4,5},{5,4},{6,7},{7,6},{8,9},{9,8},{10,11... | collective-permute-start | bytes 12296 | tf_op jit(solution)/shard_map/ppermute | solution.py:419
  104.0 11.4 %collective-permute-start.3 = (f32[8,2048]{1,0:T(8,128)S(1)}, f32[8,2048]{1,0:T(8,128)S(1)}, u32[]{:S(2)}, u32[]{:S(2)}) collective-permute-start(f32[8,2048]{1,0:T(8,128)S(1)} %add.30), channel_id=1, source_target_pairs={{0,64},{4,68},{8,72},{12,76},{16,80},{20,84},{24,88},{28,92},{32,9... | collective-permute-start | bytes 196616 | tf_op jit(solution)/shard_map/ppermute | solution.py:424
  107.3 9.6 %collective-permute-start.4 = (f32[8,2048]{1,0:T(8,128)S(1)}, f32[8,2048]{1,0:T(8,128)S(1)}, u32[]{:S(2)}, u32[]{:S(2)}) collective-permute-start(f32[8,2048]{1,0:T(8,128)S(1)} %add.30), channel_id=1, source_target_pairs={{0,32},{4,36},{8,40},{12,44},{16,48},{20,52},{24,56},{28,60},{32,6... | collective-permute-start | bytes 196616 | tf_op jit(solution)/shard_map/ppermute | solution.py:424
  108.0 9.0 %collective-permute-start.5 = (f32[8,2048]{1,0:T(8,128)S(1)}, f32[8,2048]{1,0:T(8,128)S(1)}, u32[]{:S(2)}, u32[]{:S(2)}) collective-permute-start(f32[8,2048]{1,0:T(8,128)S(1)} %add.30), channel_id=1, source_target_pairs={{0,96},{4,100},{8,104},{12,108},{16,112},{20,116},{24,120},{28,124... | collective-permute-start | bytes 196616 | tf_op jit(solution)/shard_map/ppermute | solution.py:424
  117.0 4.3 %collective-permute-start.7 = (f32[8,2048]{1,0:T(8,128)S(1)}, f32[8,2048]{1,0:T(8,128)S(1)}, u32[]{:S(2)}, u32[]{:S(2)}) collective-permute-start(f32[8,2048]{1,0:T(8,128)S(1)} %add_add_fusion), channel_id=1, source_target_pairs={{0,8},{4,12},{8,0},{12,4},{16,24},{20,28},{24,16},{28,20},{32,40},... | collective-permute-start | bytes 196616 | tf_op jit(solution)/shard_map/ppermute | solution.py:419
  118.3 5.5 %collective-permute-start.8 = (f32[8,128]{1,0:T(8,128)S(1)}, f32[8,128]{1,0:T(8,128)S(1)}, u32[]{:S(2)}, u32[]{:S(2)}) collective-permute-start(f32[8,128]{1,0:T(8,128)S(1)} %broadcast_add_fusion), channel_id=1, source_target_pairs={{0,3},{1,2},{2,1},{3,0},{4,7},{5,6},{6,5},{7,4},{8,11},{9,10},{10,... | collective-permute-start | bytes 12296 | tf_op jit(solution)/shard_map/ppermute | solution.py:419
  121.3 5.6 %collective-permute-start.9 = (f32[8,2048]{1,0:T(8,128)S(1)}, f32[8,2048]{1,0:T(8,128)S(1)}, u32[]{:S(2)}, u32[]{:S(2)}) collective-permute-start(f32[8,2048]{1,0:T(8,128)S(1)} %add.35), channel_id=1, source_target_pairs={{0,24},{4,28},{8,16},{12,20},{16,8},{20,12},{24,0},{28,4},{32,56},... | collective-permute-start | bytes 196616 | tf_op jit(solution)/shard_map/ppermute | solution.py:419

commit v4 on v3

--- a/solution.py
+++ b/solution.py
@@ -48,7 +48,9 @@
     return pltpu.roll(x, HALF, axis=x.ndim - 1)
 
 
-def spectral_kernel(recv, m1, w, wi, m2, factors, gz_out, gh_out, x_v, gz_v, gh_v, y, u, in_sems, out_sems):
+def spectral_kernel(recv, *refs):
+    tables, (gz_out, gh_out), scratch = refs[:5], refs[5:7], refs[7:]
+    m1, w, wi, m2, factors, x_v, gz_v, gh_v, y, u, in_sems, table_sems, out_sems = scratch
     parts, mid = recv.shape[0], recv.shape[2]
     rows = 2 * mid
     chans = (recv.shape[1] - 16) // 6
@@ -64,7 +66,8 @@
 
     edges_in = fetch(6 * chans, 16, 2 * pieces)
     mixed_in, others_in = fetches(1), fetches(2) + fetches(0)
-    for copy in [edges_in] + mixed_in + others_in:
+    tables_in = [pltpu.make_async_copy(tables[n], scratch[n], table_sems.at[n]) for n in range(5)]
+    for copy in [edges_in] + mixed_in + [tables_in[0], tables_in[4]] + others_in + tables_in[1:4]:
         copy.start()
 
     for copy in [edges_in] + mixed_in:
@@ -100,6 +103,9 @@
             y[0, k, pl.ds(base, 16), :] = jnp.concatenate(sums, axis=0).astype(BF)
             y[1, k, pl.ds(base, 16), :] = jnp.concatenate(gaps, axis=0).astype(BF)
 
+    tables_in[0].wait()
+    tables_in[4].wait()
+
     @pl.loop(1, pieces + 1)
     def _(n):
         i = lax.rem(n, pieces)
@@ -111,6 +117,9 @@
 
         for q in range(chans // 16):
             forward(pl.multiple_of(chans * i + 16 * q, 16))
+
+    tables_in[1].wait()
+    tables_in[2].wait()
 
     @pl.loop(0, parts // group)
     def _(kk):
@@ -154,6 +163,7 @@
         at = pl.ds(row, 16)
         return pltpu.make_async_copy(scratch.at[:, at, :], target.at[:, at, :], out_sems.at[first])
 
+    tables_in[3].wait()
     squares = jnp.zeros((8, rows), F32)
     for i in range(tiles):
         grad = backward(chans + 16 * i)
@@ -193,7 +203,6 @@
     tables = transform_tables(parts, rows)
     chans = (recv.shape[1] - 16) // 6
     mid = rows // 2
-    vmem = pl.BlockSpec(memory_space=pltpu.VMEM)
     anywhere = pl.BlockSpec(memory_space=pl.ANY)
     flops = 2 * parts * parts * 16 * 8 * rows * chans // 8 * 5 + 2 * parts * rows * rows * chans * 10
     return pl.pallas_call(
@@ -202,15 +211,17 @@
             jax.ShapeDtypeStruct((parts, 2 * chans + 16, mid), BF),
             jax.ShapeDtypeStruct((parts, 2 * chans, mid), BF),
         ),
-        in_specs=[anywhere] + [vmem] * 5,
+        in_specs=[anywhere] * 6,
         out_specs=(anywhere, anywhere),
-        scratch_shapes=[
+        scratch_shapes=[pltpu.VMEM(x.shape, x.dtype) for x in tables]
+        + [
             pltpu.VMEM(recv.shape, BF),
             pltpu.VMEM((parts, 2 * chans + 16, mid), BF),
             pltpu.VMEM((parts, 2 * chans, mid), BF),
             pltpu.VMEM((2, parts, 3 * chans, rows), BF),
             pltpu.VMEM((2 * parts, 2 * chans, rows), BF),
             pltpu.SemaphoreType.DMA((7,)),
+            pltpu.SemaphoreType.DMA((len(tables),)),
             pltpu.SemaphoreType.DMA((4 * (chans // 16) + 1,)),
         ],
         compiler_params=pltpu.CompilerParams(vmem_limit_bytes=SPECTRAL_LIMIT * MIB),
@@ -278,7 +289,7 @@
             copy.start()
         for c in range(chunks):
             for n in range(n_in):
-                fetch(n, c).start()
+                fetch(n, c).start(priority=(n + c) % 2)
         for copy in smalls_in:
             copy.wait()
 

time: 128 us -> 127 us (level)
  Pallas kernels: 30.2 us -> 28.8 us
  transfers between devices with their start and end apart: 12 -> 12, of which waited for: 5 -> 5; matrix products, arithmetic and copies ran while one was open for 0% -> 0% of each run, Pallas kernels for 9% -> 10%
where the time goes in v4:
time: 127 us; the launch traced here: 126 us
  waiting for transfers between devices  39.5 us (31%)
  starting transfers between devices  31.9 us (25%)
  Pallas kernels  28.8 us (23%)
  blocking collectives  23 us (18%)
  local copies, waits for them, and re-layouts  1.93 us (2%)
    all_to_all x1, waiting for transfers between devices, shards(): recv = lax.all_to_all(send, 'seq', 0, 0)  36.9 us
    all_to_all x1, blocking collectives, shards(): gz_recv = lax.all_to_all(gz_send, 'seq', 0, 0)  23 us
    pallas_call x5, Pallas kernels, stream(): pl.pallas_call(kernel, in_specs=[anywhere] * (n_in + n_small), out_specs=...  17.6 us
    pallas_call x1, Pallas kernels, spectral(): pl.pallas_call(spectral_kernel, out_shape=(jax.ShapeDtypeStruct((parts, 2...  11.2 us
    all_to_all x1, starting transfers between devices, shards(): recv = lax.all_to_all(send, 'seq', 0, 0)  8.81 us
    ppermute x5, starting transfers between devices, tree_step(): lax.ppermute(x, axis, [(i, i ^ step) for i in range(lax.axis_size(axis))])  8.38 us
    ppermute x3, starting transfers between devices, quarter_sum(): lax.ppermute(x, axis, [(i, (i + n * size // 4) % size) for i in range(siz...  6.6 us
    all_to_all x1, starting transfers between devices, shards(): gh_recv = lax.all_to_all(gh_send, 'seq', 0, 0)  4.66 us
  transfers between devices with their start and end apart: 12, of which 5 were waited for; matrix products, arithmetic and copies ran while one was open for 0% of the time, Pallas kernels for 10%

profile of v4, /device:TPU:0, one launch (start us, length us, event | category | flops | bytes accessed | tf_op | source)
XLA Modules:
  0.0 126.1 jit_solution(12233404712670149161)
XLA Ops:
  0.6 5.5 %pack.1 = bf16[32,400,128]{2,1,0:T(8,128)(2,1)} custom-call(bf16[256,2048]{1,0:T(8,128)(2,1)} %refs_0_.4, bf16[256,2048]{1,0:T(8,128)(2,1)} %refs_1_.5, f32[256,2048]{1,0:T(8,128)} %refs_2_.4, bf16[256,2048]{1,0:T(8,128)(2,1)} %refs_1_.8, bf16[256,2048]{1,0:T(8,128)(2,1)} %refs_2_.6, f32[3,2048]{1,0:T(4,128)} %refs_3_.6, f32[3,2048]{1,0:T(4,128)} %refs_4_.6), custom_call_target="tpu_custom_call" | custom-call | flops 9568256 | bytes 9568256 | tf_op jit(solution)/shard_map/pack/pallas_call | solution.py:318
  6.1 8.8 %all-to-all-start = ((bf16[32,400,128]{2,1,0:T(8,128)(2,1)}), bf16[32,400,128]{2,1,0:T(8,128)(2,1)}, u32[]{:S(2)}, u32[]{:S(2)}) async-start(bf16[32,400,128]{2,1,0:T(8,128)(2,1)} %pack.1), calls=%async_computation | async-start | bytes 6553600 | tf_op jit(solution)/shard_map/all_to_all | solution.py:455
  15.1 2.1 %collective-permute-start = (bf16[4,2048]{1,0:T(4,128)(2,1)S(1)}, bf16[4,2048]{1,0:T(4,128)(2,1)S(1)}, u32[]{:S(2)}, u32[]{:S(2)}) collective-permute-start(bf16[4,2048]{1,0:T(4,128)(2,1)S(1)} %get-tuple-element.28), channel_id=1, source_target_pairs={{0,4},{4,8},{8,12},{12,16},{16,20},{20,24},{24,28},{28,32},{32,36}... | collective-permute-start | bytes 49160 | tf_op jit(solution)/shard_map/ppermute | solution.py:457
  17.2 1.3 %collective-permute-start.1 = (bf16[4,2048]{1,0:T(4,128)(2,1)S(1)}, bf16[4,2048]{1,0:T(4,128)(2,1)S(1)}, u32[]{:S(2)}, u32[]{:S(2)}) collective-permute-start(bf16[4,2048]{1,0:T(4,128)(2,1)S(1)} %get-tuple-element.29), channel_id=1, source_target_pairs={{4,0},{8,4},{12,8},{16,12},{20,16},{24,20},{28,24},{32,28},{36,32}... | collective-permute-start | bytes 49160 | tf_op jit(solution)/shard_map/ppermute | solution.py:458
  18.5 1.2 copy-done.3
  19.7 1.3 %gate.1 = bf16[256,2048]{1,0:T(8,128)(2,1)} custom-call(bf16[256,2048]{1,0:T(8,128)(2,1)S(1)} %copy-done.2, bf16[256,2048]{1,0:T(8,128)(2,1)S(1)} %copy-done.3), custom_call_target="tpu_custom_call" | custom-call | flops 3145728 | bytes 3145728 | tf_op jit(solution)/shard_map/gate/pallas_call | solution.py:318
  21.1 0.4 collective-permute-done.1.refs_6_
  21.4 36.9 %all-to-all-done.recv = bf16[32,400,128]{2,1,0:T(8,128)(2,1)} async-done(((bf16[32,400,128]{2,1,0:T(8,128)(2,1)}), bf16[32,400,128]{2,1,0:T(8,128)(2,1)}, u32[]{:S(2)}, u32[]{:S(2)}) %all-to-all-start) | async-done | bytes 3276832 | tf_op jit(solution)/shard_map/all_to_all | solution.py:455
  58.3 11.2 %spectral.1 = (bf16[32,144,128]{2,1,0:T(8,128)(2,1)}, bf16[32,128,128]{2,1,0:T(8,128)(2,1)}) custom-call(bf16[32,400,128]{2,1,0:T(8,128)(2,1)} %all-to-all-done.recv, bf16[512,256]{1,0:T(8,128)(2,1)} %constant.19.clone.refs_0_, bf16[2,256,256]{2,1,0:T(8,128)(2,1)} %constant.20.clone.refs_1_, bf16[2,256,256]{2,1,0:T(8,128)(2,1)} %constant.21.clone.refs_2_, ...), custom_call_target="tpu_custom_call" | custom-call | flops 5368709120 | bytes 7340032 | tf_op jit(solution)/shard_map/spectral/pallas_call | solution.py:208
  69.6 23.0 %all_to_all.15.refs_0_ = bf16[32,144,128]{2,1,0:T(8,128)(2,1)S(1)} all-to-all(bf16[32,144,128]{2,1,0:T(8,128)(2,1)} %get-tuple-element.32), channel_id=1, replica_groups=mesh['seq'=32,'chan'=4] {'seq'}, dimensions={0} | all-to-all | bytes 2359296 | tf_op jit(solution)/shard_map/all_to_all | solution.py:462
  92.6 4.7 %all-to-all-start.2 = ((bf16[32,128,128]{2,1,0:T(8,128)(2,1)}), bf16[32,128,128]{2,1,0:T(8,128)(2,1)}, u32[]{:S(2)}, u32[]{:S(2)}) async-start(bf16[32,128,128]{2,1,0:T(8,128)(2,1)} %get-tuple-element.46), calls=%async_computation.2 | async-start | bytes 2097152 | tf_op jit(solution)/shard_map/all_to_all | solution.py:464
  97.3 3.5 %taps.1 = f32[8,2048]{1,0:T(8,128)S(1)} custom-call(bf16[32,144,128]{2,1,0:T(8,128)(2,1)S(1)} %all_to_all.15.refs_0_, bf16[256,2048]{1,0:T(8,128)(2,1)S(1)} %copy-done, bf16[256,2048]{1,0:T(8,128)(2,1)S(1)} %copy-done.1, f32[3,2048]{1,0:T(4,128)S(1)} %copy-done.4, f32[3,2048]{1,0:T(4,128)S(1)} %copy-done.5, bf16[4,2048]{1,0:T(4,128)(2,1)S(1)} %collective-permute-done.refs_5_), custom_call_target="tpu_custom_call" | custom-call | flops 3342336 | bytes 3342336 | tf_op jit(solution)/shard_map/taps/pallas_call | solution.py:318
  101.0 1.6 %collective-permute-start.6 = (f32[8,128]{1,0:T(8,128)S(1)}, f32[8,128]{1,0:T(8,128)S(1)}, u32[]{:S(2)}, u32[]{:S(2)}) collective-permute-start(f32[8,128]{1,0:T(8,128)S(1)} %broadcast_in_dim.2), channel_id=1, source_target_pairs={{0,1},{1,0},{2,3},{3,2},{4,5},{5,4},{6,7},{7,6},{8,9},{9,8},{10,11... | collective-permute-start | bytes 12296 | tf_op jit(solution)/shard_map/ppermute | solution.py:430
  102.6 3.4 %collective-permute-start.3 = (f32[8,2048]{1,0:T(8,128)S(1)}, f32[8,2048]{1,0:T(8,128)S(1)}, u32[]{:S(2)}, u32[]{:S(2)}) collective-permute-start(f32[8,2048]{1,0:T(8,128)S(1)} %add.30), channel_id=1, source_target_pairs={{0,64},{4,68},{8,72},{12,76},{16,80},{20,84},{24,88},{28,92},{32,9... | collective-permute-start | bytes 196616 | tf_op jit(solution)/shard_map/ppermute | solution.py:435
  106.0 0.6 collective-permute-start.4
  106.6 2.6 %collective-permute-start.5 = (f32[8,2048]{1,0:T(8,128)S(1)}, f32[8,2048]{1,0:T(8,128)S(1)}, u32[]{:S(2)}, u32[]{:S(2)}) collective-permute-start(f32[8,2048]{1,0:T(8,128)S(1)} %add.30), channel_id=1, source_target_pairs={{0,96},{4,100},{8,104},{12,108},{16,112},{20,116},{24,120},{28,124... | collective-permute-start | bytes 196616 | tf_op jit(solution)/shard_map/ppermute | solution.py:435
  109.2 4.8 %inputs.1 = (bf16[256,2048]{1,0:T(8,128)(2,1)}, bf16[256,2048]{1,0:T(8,128)(2,1)}) custom-call(bf16[32,144,128]{2,1,0:T(8,128)(2,1)S(1)} %all_to_all.15.refs_0_, bf16[256,2048]{1,0:T(8,128)(2,1)S(1)} %copy-done, bf16[256,2048]{1,0:T(8,128)(2,1)S(1)} %copy-done.1, f32[3,2048]{1,0:T(4,128)S(1)} %copy-done.4, f32[3,2048]{1,0:T(4,128)S(1)} %copy-done.5, ...), custom_call_target="tpu_custom_call" | custom-call | flops 5373952 | bytes 5373952 | tf_op jit(solution)/shard_map/inputs/pallas_call | solution.py:318
  114.0 1.5 %collective-permute-done.4 = f32[8,2048]{1,0:T(8,128)S(1)} collective-permute-done((f32[8,2048]{1,0:T(8,128)S(1)}, f32[8,2048]{1,0:T(8,128)S(1)}, u32[]{:S(2)}, u32[]{:S(2)}) %collective-permute-start.4) | collective-permute-done | bytes 65568 | tf_op jit(solution)/shard_map/ppermute | solution.py:435
  115.6 1.4 %collective-permute-start.7 = (f32[8,2048]{1,0:T(8,128)S(1)}, f32[8,2048]{1,0:T(8,128)S(1)}, u32[]{:S(2)}, u32[]{:S(2)}) collective-permute-start(f32[8,2048]{1,0:T(8,128)S(1)} %add_add_fusion), channel_id=1, source_target_pairs={{0,8},{4,12},{8,0},{12,4},{16,24},{20,28},{24,16},{28,20},{32,40},... | collective-permute-start | bytes 196616 | tf_op jit(solution)/shard_map/ppermute | solution.py:430
  116.9 2.7 %collective-permute-start.8 = (f32[8,128]{1,0:T(8,128)S(1)}, f32[8,128]{1,0:T(8,128)S(1)}, u32[]{:S(2)}, u32[]{:S(2)}) collective-permute-start(f32[8,128]{1,0:T(8,128)S(1)} %broadcast_add_fusion), channel_id=1, source_target_pairs={{0,3},{1,2},{2,1},{3,0},{4,7},{5,6},{6,5},{7,4},{8,11},{9,10},{10,... | collective-permute-start | bytes 12296 | tf_op jit(solution)/shard_map/ppermute | solution.py:430
  119.9 2.6 %collective-permute-start.9 = (f32[8,2048]{1,0:T(8,128)S(1)}, f32[8,2048]{1,0:T(8,128)S(1)}, u32[]{:S(2)}, u32[]{:S(2)}) collective-permute-start(f32[8,2048]{1,0:T(8,128)S(1)} %add.35), channel_id=1, source_target_pairs={{0,24},{4,28},{8,16},{12,20},{16,8},{20,12},{24,0},{28,4},{32,56},... | collective-permute-start | bytes 196616 | tf_op jit(solution)/shard_map/ppermute | solution.py:430
  122.5 2.5 %clip.1 = f32[256,2048]{1,0:T(8,128)} custom-call(bf16[32,128,128]{2,1,0:T(8,128)(2,1)} %all-to-all-done.2.refs_0_, f32[8,128]{1,0:T(8,128)S(1)} %rsqrt_minimum_fusion.refs_1_), custom_call_target="tpu_custom_call" | custom-call | flops 3145728 | bytes 3145728 | tf_op jit(solution)/shard_map/clip/pallas_call | solution.py:318
  125.0 0.5 collective-permute-done.9
  125.5 0.6 fusion.2
  (31 shorter events, 0.7 us)
Async XLA Ops:
  6.1 8.9 %copy-start = (bf16[256,2048]{1,0:T(8,128)(2,1)S(1)}, bf16[256,2048]{1,0:T(8,128)(2,1)}, u32[]{:S(2)}) copy-start(bf16[256,2048]{1,0:T(8,128)(2,1)} %refs_1_.8) | copy-start | bytes 3145732
  6.1 8.9 %copy-start.1 = (bf16[256,2048]{1,0:T(8,128)(2,1)S(1)}, bf16[256,2048]{1,0:T(8,128)(2,1)}, u32[]{:S(2)}) copy-start(bf16[256,2048]{1,0:T(8,128)(2,1)} %refs_2_.6) | copy-start | bytes 3145732
  6.1 12.4 %copy-start.2 = (bf16[256,2048]{1,0:T(8,128)(2,1)S(1)}, bf16[256,2048]{1,0:T(8,128)(2,1)}, u32[]{:S(2)}) copy-start(bf16[256,2048]{1,0:T(8,128)(2,1)} %refs_0_.4) | copy-start | bytes 3145732
  6.1 52.2 %all-to-all-start = ((bf16[32,400,128]{2,1,0:T(8,128)(2,1)}), bf16[32,400,128]{2,1,0:T(8,128)(2,1)}, u32[]{:S(2)}, u32[]{:S(2)}) async-start(bf16[32,400,128]{2,1,0:T(8,128)(2,1)} %pack.1), calls=%async_computation | async-start | bytes 6553600 | tf_op jit(solution)/shard_map/all_to_all | solution.py:455
  15.1 6.0 %collective-permute-start = (bf16[4,2048]{1,0:T(4,128)(2,1)S(1)}, bf16[4,2048]{1,0:T(4,128)(2,1)S(1)}, u32[]{:S(2)}, u32[]{:S(2)}) collective-permute-start(bf16[4,2048]{1,0:T(4,128)(2,1)S(1)} %get-tuple-element.28), channel_id=1, source_target_pairs={{0,4},{4,8},{8,12},{12,16},{16,20},{20,24},{24,28},{28,32},{32,36}... | collective-permute-start | bytes 49160 | tf_op jit(solution)/shard_map/ppermute | solution.py:457
  17.2 4.2 %collective-permute-start.1 = (bf16[4,2048]{1,0:T(4,128)(2,1)S(1)}, bf16[4,2048]{1,0:T(4,128)(2,1)S(1)}, u32[]{:S(2)}, u32[]{:S(2)}) collective-permute-start(bf16[4,2048]{1,0:T(4,128)(2,1)S(1)} %get-tuple-element.29), channel_id=1, source_target_pairs={{4,0},{8,4},{12,8},{16,12},{20,16},{24,20},{28,24},{32,28},{36,32}... | collective-permute-start | bytes 49160 | tf_op jit(solution)/shard_map/ppermute | solution.py:458
  18.5 1.2 copy-start.3
  69.6 27.7 %copy-start.4 = (f32[3,2048]{1,0:T(4,128)S(1)}, f32[3,2048]{1,0:T(4,128)}, u32[]{:S(2)}) copy-start(f32[3,2048]{1,0:T(4,128)} %refs_3_.6) | copy-start | bytes 73732
  69.6 27.7 %copy-start.5 = (f32[3,2048]{1,0:T(4,128)S(1)}, f32[3,2048]{1,0:T(4,128)}, u32[]{:S(2)}) copy-start(f32[3,2048]{1,0:T(4,128)} %refs_4_.6) | copy-start | bytes 73732
  92.6 27.4 %all-to-all-start.2 = ((bf16[32,128,128]{2,1,0:T(8,128)(2,1)}), bf16[32,128,128]{2,1,0:T(8,128)(2,1)}, u32[]{:S(2)}, u32[]{:S(2)}) async-start(bf16[32,128,128]{2,1,0:T(8,128)(2,1)} %get-tuple-element.46), calls=%async_computation.2 | async-start | bytes 2097152 | tf_op jit(solution)/shard_map/all_to_all | solution.py:464
  100.8 1.8 %collective-permute-start.2 = (f32[8,2048]{1,0:T(8,128)S(1)}, f32[8,2048]{1,0:T(8,128)S(1)}, u32[]{:S(2)}, u32[]{:S(2)}) collective-permute-start(f32[8,2048]{1,0:T(8,128)S(1)} %taps.1), channel_id=1, source_target_pairs={{0,4},{4,0},{8,12},{12,8},{16,20},{20,16},{24,28},{28,24},{32,36},... | collective-permute-start | bytes 196616 | tf_op jit(solution)/shard_map/ppermute | solution.py:430
  101.0 8.2 %collective-permute-start.6 = (f32[8,128]{1,0:T(8,128)S(1)}, f32[8,128]{1,0:T(8,128)S(1)}, u32[]{:S(2)}, u32[]{:S(2)}) collective-permute-start(f32[8,128]{1,0:T(8,128)S(1)} %broadcast_in_dim.2), channel_id=1, source_target_pairs={{0,1},{1,0},{2,3},{3,2},{4,5},{5,4},{6,7},{7,6},{8,9},{9,8},{10,11... | collective-permute-start | bytes 12296 | tf_op jit(solution)/shard_map/ppermute | solution.py:430
  102.6 11.4 %collective-permute-start.3 = (f32[8,2048]{1,0:T(8,128)S(1)}, f32[8,2048]{1,0:T(8,128)S(1)}, u32[]{:S(2)}, u32[]{:S(2)}) collective-permute-start(f32[8,2048]{1,0:T(8,128)S(1)} %add.30), channel_id=1, source_target_pairs={{0,64},{4,68},{8,72},{12,76},{16,80},{20,84},{24,88},{28,92},{32,9... | collective-permute-start | bytes 196616 | tf_op jit(solution)/shard_map/ppermute | solution.py:435
  106.0 9.6 %collective-permute-start.4 = (f32[8,2048]{1,0:T(8,128)S(1)}, f32[8,2048]{1,0:T(8,128)S(1)}, u32[]{:S(2)}, u32[]{:S(2)}) collective-permute-start(f32[8,2048]{1,0:T(8,128)S(1)} %add.30), channel_id=1, source_target_pairs={{0,32},{4,36},{8,40},{12,44},{16,48},{20,52},{24,56},{28,60},{32,6... | collective-permute-start | bytes 196616 | tf_op jit(solution)/shard_map/ppermute | solution.py:435
  106.6 9.0 %collective-permute-start.5 = (f32[8,2048]{1,0:T(8,128)S(1)}, f32[8,2048]{1,0:T(8,128)S(1)}, u32[]{:S(2)}, u32[]{:S(2)}) collective-permute-start(f32[8,2048]{1,0:T(8,128)S(1)} %add.30), channel_id=1, source_target_pairs={{0,96},{4,100},{8,104},{12,108},{16,112},{20,116},{24,120},{28,124... | collective-permute-start | bytes 196616 | tf_op jit(solution)/shard_map/ppermute | solution.py:435
  115.6 4.3 %collective-permute-start.7 = (f32[8,2048]{1,0:T(8,128)S(1)}, f32[8,2048]{1,0:T(8,128)S(1)}, u32[]{:S(2)}, u32[]{:S(2)}) collective-permute-start(f32[8,2048]{1,0:T(8,128)S(1)} %add_add_fusion), channel_id=1, source_target_pairs={{0,8},{4,12},{8,0},{12,4},{16,24},{20,28},{24,16},{28,20},{32,40},... | collective-permute-start | bytes 196616 | tf_op jit(solution)/shard_map/ppermute | solution.py:430
  116.9 5.5 %collective-permute-start.8 = (f32[8,128]{1,0:T(8,128)S(1)}, f32[8,128]{1,0:T(8,128)S(1)}, u32[]{:S(2)}, u32[]{:S(2)}) collective-permute-start(f32[8,128]{1,0:T(8,128)S(1)} %broadcast_add_fusion), channel_id=1, source_target_pairs={{0,3},{1,2},{2,1},{3,0},{4,7},{5,6},{6,5},{7,4},{8,11},{9,10},{10,... | collective-permute-start | bytes 12296 | tf_op jit(solution)/shard_map/ppermute | solution.py:430
  119.9 5.6 %collective-permute-start.9 = (f32[8,2048]{1,0:T(8,128)S(1)}, f32[8,2048]{1,0:T(8,128)S(1)}, u32[]{:S(2)}, u32[]{:S(2)}) collective-permute-start(f32[8,2048]{1,0:T(8,128)S(1)} %add.35), channel_id=1, source_target_pairs={{0,24},{4,28},{8,16},{12,20},{16,8},{20,12},{24,0},{28,4},{32,56},... | collective-permute-start | bytes 196616 | tf_op jit(solution)/shard_map/ppermute | solution.py:430

commit v5 on v4

--- a/solution.py
+++ b/solution.py
@@ -457,8 +457,9 @@
     before = lax.ppermute(tails, "seq", [(i, i + 1) for i in range(parts - 1)])
     after = lax.ppermute(heads, "seq", [(i + 1, i) for i in range(parts - 1)])
     (gate_grad,) = stream(gate_body, "gate", (cotangent, conv_out), (), (block,), ((0, None),), 4, 16)
-    recv, gate_grad, before, after = lax.optimization_barrier((recv, gate_grad, before, after))
+    recv, gate_grad = lax.optimization_barrier((recv, gate_grad))
     gz_send, gh_send = spectral(recv, parts, rows)
+    gz_send, before, after = lax.optimization_barrier((gz_send, before, after))
     gz_recv = lax.all_to_all(gz_send, "seq", 0, 0)
     gz_recv, gh_send = lax.optimization_barrier((gz_recv, gh_send))
     gh_recv = lax.all_to_all(gh_send, "seq", 0, 0)

time: 127 us -> 127 us (level)
  transfers between devices with their start and end apart: 12 -> 12, of which waited for: 5 -> 4; matrix products, arithmetic and copies ran while one was open for 0% -> 0% of each run, Pallas kernels for 10% -> 18%
where the time goes in v5:
time: 127 us; the launch traced here: 126 us
  waiting for transfers between devices  39.6 us (31%)
  starting transfers between devices  31.9 us (25%)
  Pallas kernels  28.8 us (23%)
  blocking collectives  23 us (18%)
  local copies, waits for them, and re-layouts  1.93 us (2%)
    all_to_all x1, waiting for transfers between devices, shards(): recv = lax.all_to_all(send, 'seq', 0, 0)  37.3 us
    all_to_all x1, blocking collectives, shards(): gz_recv = lax.all_to_all(gz_send, 'seq', 0, 0)  23 us
    pallas_call x5, Pallas kernels, stream(): pl.pallas_call(kernel, in_specs=[anywhere] * (n_in + n_small), out_specs=...  17.6 us
    pallas_call x1, Pallas kernels, spectral(): pl.pallas_call(spectral_kernel, out_shape=(jax.ShapeDtypeStruct((parts, 2...  11.2 us
    all_to_all x1, starting transfers between devices, shards(): recv = lax.all_to_all(send, 'seq', 0, 0)  8.81 us
    ppermute x5, starting transfers between devices, tree_step(): lax.ppermute(x, axis, [(i, i ^ step) for i in range(lax.axis_size(axis))])  8.38 us
    ppermute x3, starting transfers between devices, quarter_sum(): lax.ppermute(x, axis, [(i, (i + n * size // 4) % size) for i in range(siz...  6.6 us
    all_to_all x1, starting transfers between devices, shards(): gh_recv = lax.all_to_all(gh_send, 'seq', 0, 0)  4.66 us
  transfers between devices with their start and end apart: 12, of which 4 were waited for; matrix products, arithmetic and copies ran while one was open for 0% of the time, Pallas kernels for 18%

profile of v5, /device:TPU:0, one launch (start us, length us, event | category | flops | bytes accessed | tf_op | source)
XLA Modules:
  0.0 126.2 jit_solution(12478895823850710652)
XLA Ops:
  0.6 5.5 %pack.1 = bf16[32,400,128]{2,1,0:T(8,128)(2,1)} custom-call(bf16[256,2048]{1,0:T(8,128)(2,1)} %refs_0_.4, bf16[256,2048]{1,0:T(8,128)(2,1)} %refs_1_.5, f32[256,2048]{1,0:T(8,128)} %refs_2_.4, bf16[256,2048]{1,0:T(8,128)(2,1)} %refs_1_.8, bf16[256,2048]{1,0:T(8,128)(2,1)} %refs_2_.6, f32[3,2048]{1,0:T(4,128)} %refs_3_.6, f32[3,2048]{1,0:T(4,128)} %refs_4_.6), custom_call_target="tpu_custom_call" | custom-call | flops 9568256 | bytes 9568256 | tf_op jit(solution)/shard_map/pack/pallas_call | solution.py:318
  6.1 8.8 %all-to-all-start = ((bf16[32,400,128]{2,1,0:T(8,128)(2,1)}), bf16[32,400,128]{2,1,0:T(8,128)(2,1)}, u32[]{:S(2)}, u32[]{:S(2)}) async-start(bf16[32,400,128]{2,1,0:T(8,128)(2,1)} %pack.1), calls=%async_computation | async-start | bytes 6553600 | tf_op jit(solution)/shard_map/all_to_all | solution.py:455
  15.1 2.1 %collective-permute-start = (bf16[4,2048]{1,0:T(4,128)(2,1)S(1)}, bf16[4,2048]{1,0:T(4,128)(2,1)S(1)}, u32[]{:S(2)}, u32[]{:S(2)}) collective-permute-start(bf16[4,2048]{1,0:T(4,128)(2,1)S(1)} %get-tuple-element.32), channel_id=1, source_target_pairs={{0,4},{4,8},{8,12},{12,16},{16,20},{20,24},{24,28},{28,32},{32,36}... | collective-permute-start | bytes 49160 | tf_op jit(solution)/shard_map/ppermute | solution.py:457
  17.2 1.3 %collective-permute-start.1 = (bf16[4,2048]{1,0:T(4,128)(2,1)S(1)}, bf16[4,2048]{1,0:T(4,128)(2,1)S(1)}, u32[]{:S(2)}, u32[]{:S(2)}) collective-permute-start(bf16[4,2048]{1,0:T(4,128)(2,1)S(1)} %get-tuple-element.33), channel_id=1, source_target_pairs={{4,0},{8,4},{12,8},{16,12},{20,16},{24,20},{28,24},{32,28},{36,32}... | collective-permute-start | bytes 49160 | tf_op jit(solution)/shard_map/ppermute | solution.py:458
  18.5 1.2 copy-done.3
  19.7 1.3 %gate.1 = bf16[256,2048]{1,0:T(8,128)(2,1)} custom-call(bf16[256,2048]{1,0:T(8,128)(2,1)S(1)} %copy-done.2, bf16[256,2048]{1,0:T(8,128)(2,1)S(1)} %copy-done.3), custom_call_target="tpu_custom_call" | custom-call | flops 3145728 | bytes 3145728 | tf_op jit(solution)/shard_map/gate/pallas_call | solution.py:318
  21.0 37.3 %all-to-all-done.recv = bf16[32,400,128]{2,1,0:T(8,128)(2,1)} async-done(((bf16[32,400,128]{2,1,0:T(8,128)(2,1)}), bf16[32,400,128]{2,1,0:T(8,128)(2,1)}, u32[]{:S(2)}, u32[]{:S(2)}) %all-to-all-start) | async-done | bytes 3276832 | tf_op jit(solution)/shard_map/all_to_all | solution.py:455
  58.3 11.2 %spectral.1 = (bf16[32,144,128]{2,1,0:T(8,128)(2,1)}, bf16[32,128,128]{2,1,0:T(8,128)(2,1)}) custom-call(bf16[32,400,128]{2,1,0:T(8,128)(2,1)} %all-to-all-done.recv, bf16[512,256]{1,0:T(8,128)(2,1)} %constant.19.clone.refs_0_, bf16[2,256,256]{2,1,0:T(8,128)(2,1)} %constant.20.clone.refs_1_, bf16[2,256,256]{2,1,0:T(8,128)(2,1)} %constant.21.clone.refs_2_, ...), custom_call_target="tpu_custom_call" | custom-call | flops 5368709120 | bytes 7340032 | tf_op jit(solution)/shard_map/spectral/pallas_call | solution.py:208
  69.6 23.0 %all_to_all.15.refs_0_ = bf16[32,144,128]{2,1,0:T(8,128)(2,1)S(1)} all-to-all(bf16[32,144,128]{2,1,0:T(8,128)(2,1)} %get-tuple-element.34), channel_id=1, replica_groups=mesh['seq'=32,'chan'=4] {'seq'}, dimensions={0} | all-to-all | bytes 2359296 | tf_op jit(solution)/shard_map/all_to_all | solution.py:463
  92.6 4.7 %all-to-all-start.2 = ((bf16[32,128,128]{2,1,0:T(8,128)(2,1)}), bf16[32,128,128]{2,1,0:T(8,128)(2,1)}, u32[]{:S(2)}, u32[]{:S(2)}) async-start(bf16[32,128,128]{2,1,0:T(8,128)(2,1)} %get-tuple-element.48), calls=%async_computation.2 | async-start | bytes 2097152 | tf_op jit(solution)/shard_map/all_to_all | solution.py:465
  97.3 3.5 %taps.1 = f32[8,2048]{1,0:T(8,128)S(1)} custom-call(bf16[32,144,128]{2,1,0:T(8,128)(2,1)S(1)} %all_to_all.15.refs_0_, bf16[256,2048]{1,0:T(8,128)(2,1)S(1)} %copy-done, bf16[256,2048]{1,0:T(8,128)(2,1)S(1)} %copy-done.1, f32[3,2048]{1,0:T(4,128)S(1)} %copy-done.4, f32[3,2048]{1,0:T(4,128)S(1)} %copy-done.5, bf16[4,2048]{1,0:T(4,128)(2,1)S(1)} %collective-permute-done.refs_5_), custom_call_target="tpu_custom_call" | custom-call | flops 3342336 | bytes 3342336 | tf_op jit(solution)/shard_map/taps/pallas_call | solution.py:318
  101.0 1.6 %collective-permute-start.6 = (f32[8,128]{1,0:T(8,128)S(1)}, f32[8,128]{1,0:T(8,128)S(1)}, u32[]{:S(2)}, u32[]{:S(2)}) collective-permute-start(f32[8,128]{1,0:T(8,128)S(1)} %broadcast_in_dim.2), channel_id=1, source_target_pairs={{0,1},{1,0},{2,3},{3,2},{4,5},{5,4},{6,7},{7,6},{8,9},{9,8},{10,11... | collective-permute-start | bytes 12296 | tf_op jit(solution)/shard_map/ppermute | solution.py:430
  102.6 3.4 %collective-permute-start.3 = (f32[8,2048]{1,0:T(8,128)S(1)}, f32[8,2048]{1,0:T(8,128)S(1)}, u32[]{:S(2)}, u32[]{:S(2)}) collective-permute-start(f32[8,2048]{1,0:T(8,128)S(1)} %add.30), channel_id=1, source_target_pairs={{0,64},{4,68},{8,72},{12,76},{16,80},{20,84},{24,88},{28,92},{32,9... | collective-permute-start | bytes 196616 | tf_op jit(solution)/shard_map/ppermute | solution.py:435
  106.0 0.6 collective-permute-start.4
  106.6 2.6 %collective-permute-start.5 = (f32[8,2048]{1,0:T(8,128)S(1)}, f32[8,2048]{1,0:T(8,128)S(1)}, u32[]{:S(2)}, u32[]{:S(2)}) collective-permute-start(f32[8,2048]{1,0:T(8,128)S(1)} %add.30), channel_id=1, source_target_pairs={{0,96},{4,100},{8,104},{12,108},{16,112},{20,116},{24,120},{28,124... | collective-permute-start | bytes 196616 | tf_op jit(solution)/shard_map/ppermute | solution.py:435
  109.2 4.8 %inputs.1 = (bf16[256,2048]{1,0:T(8,128)(2,1)}, bf16[256,2048]{1,0:T(8,128)(2,1)}) custom-call(bf16[32,144,128]{2,1,0:T(8,128)(2,1)S(1)} %all_to_all.15.refs_0_, bf16[256,2048]{1,0:T(8,128)(2,1)S(1)} %copy-done, bf16[256,2048]{1,0:T(8,128)(2,1)S(1)} %copy-done.1, f32[3,2048]{1,0:T(4,128)S(1)} %copy-done.4, f32[3,2048]{1,0:T(4,128)S(1)} %copy-done.5, ...), custom_call_target="tpu_custom_call" | custom-call | flops 5373952 | bytes 5373952 | tf_op jit(solution)/shard_map/inputs/pallas_call | solution.py:318
  114.0 1.5 %collective-permute-done.4 = f32[8,2048]{1,0:T(8,128)S(1)} collective-permute-done((f32[8,2048]{1,0:T(8,128)S(1)}, f32[8,2048]{1,0:T(8,128)S(1)}, u32[]{:S(2)}, u32[]{:S(2)}) %collective-permute-start.4) | collective-permute-done | bytes 65568 | tf_op jit(solution)/shard_map/ppermute | solution.py:435
  115.6 1.4 %collective-permute-start.7 = (f32[8,2048]{1,0:T(8,128)S(1)}, f32[8,2048]{1,0:T(8,128)S(1)}, u32[]{:S(2)}, u32[]{:S(2)}) collective-permute-start(f32[8,2048]{1,0:T(8,128)S(1)} %add_add_fusion), channel_id=1, source_target_pairs={{0,8},{4,12},{8,0},{12,4},{16,24},{20,28},{24,16},{28,20},{32,40},... | collective-permute-start | bytes 196616 | tf_op jit(solution)/shard_map/ppermute | solution.py:430
  117.0 2.7 %collective-permute-start.8 = (f32[8,128]{1,0:T(8,128)S(1)}, f32[8,128]{1,0:T(8,128)S(1)}, u32[]{:S(2)}, u32[]{:S(2)}) collective-permute-start(f32[8,128]{1,0:T(8,128)S(1)} %broadcast_add_fusion), channel_id=1, source_target_pairs={{0,3},{1,2},{2,1},{3,0},{4,7},{5,6},{6,5},{7,4},{8,11},{9,10},{10,... | collective-permute-start | bytes 12296 | tf_op jit(solution)/shard_map/ppermute | solution.py:430
  119.7 0.2 collective-permute-done.7
  119.9 2.6 %collective-permute-start.9 = (f32[8,2048]{1,0:T(8,128)S(1)}, f32[8,2048]{1,0:T(8,128)S(1)}, u32[]{:S(2)}, u32[]{:S(2)}) collective-permute-start(f32[8,2048]{1,0:T(8,128)S(1)} %add.35), channel_id=1, source_target_pairs={{0,24},{4,28},{8,16},{12,20},{16,8},{20,12},{24,0},{28,4},{32,56},... | collective-permute-start | bytes 196616 | tf_op jit(solution)/shard_map/ppermute | solution.py:430
  122.5 2.5 %clip.1 = f32[256,2048]{1,0:T(8,128)} custom-call(bf16[32,128,128]{2,1,0:T(8,128)(2,1)} %all-to-all-done.2.refs_0_, f32[8,128]{1,0:T(8,128)S(1)} %rsqrt_minimum_fusion.refs_1_), custom_call_target="tpu_custom_call" | custom-call | flops 3145728 | bytes 3145728 | tf_op jit(solution)/shard_map/clip/pallas_call | solution.py:318
  125.0 0.5 collective-permute-done.9
  125.5 0.6 fusion.2
  (31 shorter events, 0.4 us)
Async XLA Ops:
  6.1 8.9 %copy-start = (bf16[256,2048]{1,0:T(8,128)(2,1)S(1)}, bf16[256,2048]{1,0:T(8,128)(2,1)}, u32[]{:S(2)}) copy-start(bf16[256,2048]{1,0:T(8,128)(2,1)} %refs_1_.8) | copy-start | bytes 3145732
  6.1 8.9 %copy-start.1 = (bf16[256,2048]{1,0:T(8,128)(2,1)S(1)}, bf16[256,2048]{1,0:T(8,128)(2,1)}, u32[]{:S(2)}) copy-start(bf16[256,2048]{1,0:T(8,128)(2,1)} %refs_2_.6) | copy-start | bytes 3145732
  6.1 12.4 %copy-start.2 = (bf16[256,2048]{1,0:T(8,128)(2,1)S(1)}, bf16[256,2048]{1,0:T(8,128)(2,1)}, u32[]{:S(2)}) copy-start(bf16[256,2048]{1,0:T(8,128)(2,1)} %refs_0_.4) | copy-start | bytes 3145732
  6.1 52.2 %all-to-all-start = ((bf16[32,400,128]{2,1,0:T(8,128)(2,1)}), bf16[32,400,128]{2,1,0:T(8,128)(2,1)}, u32[]{:S(2)}, u32[]{:S(2)}) async-start(bf16[32,400,128]{2,1,0:T(8,128)(2,1)} %pack.1), calls=%async_computation | async-start | bytes 6553600 | tf_op jit(solution)/shard_map/all_to_all | solution.py:455
  15.1 54.5 %collective-permute-start = (bf16[4,2048]{1,0:T(4,128)(2,1)S(1)}, bf16[4,2048]{1,0:T(4,128)(2,1)S(1)}, u32[]{:S(2)}, u32[]{:S(2)}) collective-permute-start(bf16[4,2048]{1,0:T(4,128)(2,1)S(1)} %get-tuple-element.32), channel_id=1, source_target_pairs={{0,4},{4,8},{8,12},{12,16},{16,20},{20,24},{24,28},{28,32},{32,36}... | collective-permute-start | bytes 49160 | tf_op jit(solution)/shard_map/ppermute | solution.py:457
  17.2 52.4 %collective-permute-start.1 = (bf16[4,2048]{1,0:T(4,128)(2,1)S(1)}, bf16[4,2048]{1,0:T(4,128)(2,1)S(1)}, u32[]{:S(2)}, u32[]{:S(2)}) collective-permute-start(bf16[4,2048]{1,0:T(4,128)(2,1)S(1)} %get-tuple-element.33), channel_id=1, source_target_pairs={{4,0},{8,4},{12,8},{16,12},{20,16},{24,20},{28,24},{32,28},{36,32}... | collective-permute-start | bytes 49160 | tf_op jit(solution)/shard_map/ppermute | solution.py:458
  18.5 1.2 copy-start.3
  69.6 27.7 %copy-start.4 = (f32[3,2048]{1,0:T(4,128)S(1)}, f32[3,2048]{1,0:T(4,128)}, u32[]{:S(2)}) copy-start(f32[3,2048]{1,0:T(4,128)} %refs_3_.6) | copy-start | bytes 73732
  69.6 27.7 %copy-start.5 = (f32[3,2048]{1,0:T(4,128)S(1)}, f32[3,2048]{1,0:T(4,128)}, u32[]{:S(2)}) copy-start(f32[3,2048]{1,0:T(4,128)} %refs_4_.6) | copy-start | bytes 73732
  92.6 27.4 %all-to-all-start.2 = ((bf16[32,128,128]{2,1,0:T(8,128)(2,1)}), bf16[32,128,128]{2,1,0:T(8,128)(2,1)}, u32[]{:S(2)}, u32[]{:S(2)}) async-start(bf16[32,128,128]{2,1,0:T(8,128)(2,1)} %get-tuple-element.48), calls=%async_computation.2 | async-start | bytes 2097152 | tf_op jit(solution)/shard_map/all_to_all | solution.py:465
  100.8 1.8 %collective-permute-start.2 = (f32[8,2048]{1,0:T(8,128)S(1)}, f32[8,2048]{1,0:T(8,128)S(1)}, u32[]{:S(2)}, u32[]{:S(2)}) collective-permute-start(f32[8,2048]{1,0:T(8,128)S(1)} %taps.1), channel_id=1, source_target_pairs={{0,4},{4,0},{8,12},{12,8},{16,20},{20,16},{24,28},{28,24},{32,36},... | collective-permute-start | bytes 196616 | tf_op jit(solution)/shard_map/ppermute | solution.py:430
  101.0 8.2 %collective-permute-start.6 = (f32[8,128]{1,0:T(8,128)S(1)}, f32[8,128]{1,0:T(8,128)S(1)}, u32[]{:S(2)}, u32[]{:S(2)}) collective-permute-start(f32[8,128]{1,0:T(8,128)S(1)} %broadcast_in_dim.2), channel_id=1, source_target_pairs={{0,1},{1,0},{2,3},{3,2},{4,5},{5,4},{6,7},{7,6},{8,9},{9,8},{10,11... | collective-permute-start | bytes 12296 | tf_op jit(solution)/shard_map/ppermute | solution.py:430
  102.6 11.4 %collective-permute-start.3 = (f32[8,2048]{1,0:T(8,128)S(1)}, f32[8,2048]{1,0:T(8,128)S(1)}, u32[]{:S(2)}, u32[]{:S(2)}) collective-permute-start(f32[8,2048]{1,0:T(8,128)S(1)} %add.30), channel_id=1, source_target_pairs={{0,64},{4,68},{8,72},{12,76},{16,80},{20,84},{24,88},{28,92},{32,9... | collective-permute-start | bytes 196616 | tf_op jit(solution)/shard_map/ppermute | solution.py:435
  106.0 9.6 %collective-permute-start.4 = (f32[8,2048]{1,0:T(8,128)S(1)}, f32[8,2048]{1,0:T(8,128)S(1)}, u32[]{:S(2)}, u32[]{:S(2)}) collective-permute-start(f32[8,2048]{1,0:T(8,128)S(1)} %add.30), channel_id=1, source_target_pairs={{0,32},{4,36},{8,40},{12,44},{16,48},{20,52},{24,56},{28,60},{32,6... | collective-permute-start | bytes 196616 | tf_op jit(solution)/shard_map/ppermute | solution.py:435
  106.6 9.0 %collective-permute-start.5 = (f32[8,2048]{1,0:T(8,128)S(1)}, f32[8,2048]{1,0:T(8,128)S(1)}, u32[]{:S(2)}, u32[]{:S(2)}) collective-permute-start(f32[8,2048]{1,0:T(8,128)S(1)} %add.30), channel_id=1, source_target_pairs={{0,96},{4,100},{8,104},{12,108},{16,112},{20,116},{24,120},{28,124... | collective-permute-start | bytes 196616 | tf_op jit(solution)/shard_map/ppermute | solution.py:435
  115.6 4.3 %collective-permute-start.7 = (f32[8,2048]{1,0:T(8,128)S(1)}, f32[8,2048]{1,0:T(8,128)S(1)}, u32[]{:S(2)}, u32[]{:S(2)}) collective-permute-start(f32[8,2048]{1,0:T(8,128)S(1)} %add_add_fusion), channel_id=1, source_target_pairs={{0,8},{4,12},{8,0},{12,4},{16,24},{20,28},{24,16},{28,20},{32,40},... | collective-permute-start | bytes 196616 | tf_op jit(solution)/shard_map/ppermute | solution.py:430
  117.0 5.5 %collective-permute-start.8 = (f32[8,128]{1,0:T(8,128)S(1)}, f32[8,128]{1,0:T(8,128)S(1)}, u32[]{:S(2)}, u32[]{:S(2)}) collective-permute-start(f32[8,128]{1,0:T(8,128)S(1)} %broadcast_add_fusion), channel_id=1, source_target_pairs={{0,3},{1,2},{2,1},{3,0},{4,7},{5,6},{6,5},{7,4},{8,11},{9,10},{10,... | collective-permute-start | bytes 12296 | tf_op jit(solution)/shard_map/ppermute | solution.py:430
  119.9 5.6 %collective-permute-start.9 = (f32[8,2048]{1,0:T(8,128)S(1)}, f32[8,2048]{1,0:T(8,128)S(1)}, u32[]{:S(2)}, u32[]{:S(2)}) collective-permute-start(f32[8,2048]{1,0:T(8,128)S(1)} %add.35), channel_id=1, source_target_pairs={{0,24},{4,28},{8,16},{12,20},{16,8},{20,12},{24,0},{28,4},{32,56},... | collective-permute-start | bytes 196616 | tf_op jit(solution)/shard_map/ppermute | solution.py:430

commit v6 on v5

--- a/solution.py
+++ b/solution.py
@@ -106,17 +106,12 @@
     tables_in[0].wait()
     tables_in[4].wait()
 
-    @pl.loop(1, pieces + 1)
-    def _(n):
-        i = lax.rem(n, pieces)
-
-        @pl.when(i != 1)
-        def _():
+    for i in (1, 2, 0):
+        if i != 1:
             for copy in fetches(i):
                 copy.wait()
-
         for q in range(chans // 16):
-            forward(pl.multiple_of(chans * i + 16 * q, 16))
+            forward(chans * i + 16 * q)
 
     tables_in[1].wait()
     tables_in[2].wait()
@@ -164,6 +159,22 @@
         return pltpu.make_async_copy(scratch.at[:, at, :], target.at[:, at, :], out_sems.at[first])
 
     tables_in[3].wait()
+    for i in range(tiles):
+        grad = backward(16 * i)
+        for h in range(2):
+            row = chans * h + 16 * i
+            gz_v[:, row : row + 16, :] = grad[:, :, mid * h : mid * h + mid].astype(BF)
+            store(gz_out, gz_v, 2 * tiles + tiles * h + i, row).start()
+
+    for p in range(parts):
+        after = jnp.zeros((16, 128), F32)
+        if p + 1 < parts:
+            at = (p + 1) // 2 * 2
+            after = gz_v[at : at + 2, :chans, :].reshape(2 * chans, mid).T[:16].astype(F32)
+            if (p + 1) % 2:
+                after = swap_halves(after)
+        gz_v[p, 2 * chans : 2 * chans + 16, :] = after.astype(BF)
+
     squares = jnp.zeros((8, rows), F32)
     for i in range(tiles):
         grad = backward(chans + 16 * i)
@@ -172,26 +183,14 @@
             gh_v[:, row : row + 16, :] = grad[:, :, mid * h : mid * h + mid].astype(BF)
             store(gh_out, gh_v, tiles * h + i, row).start()
         squares += jnp.sum((grad * grad).reshape(parts * 2, 8, rows), axis=0)
-    for i in range(tiles):
-        grad = backward(16 * i)
-        for h in range(2):
-            row = chans * h + 16 * i
-            gz_v[:, row : row + 16, :] = grad[:, :, mid * h : mid * h + mid].astype(BF)
-            store(gz_out, gz_v, 2 * tiles + tiles * h + i, row).start()
 
     total = jnp.sum(jnp.sum(squares, axis=0, keepdims=True), axis=1, keepdims=True)
     coarse = total.astype(BF).astype(F32)
     fine = (total - coarse).astype(BF).astype(F32)
     row = lax.broadcasted_iota(jnp.int32, (16, 128), 0)
     sums = jnp.where(row == 2, coarse, jnp.where(row == 3, fine, 0.0))
-    for p in range(parts):
-        after = jnp.zeros((16, 128), F32)
-        if p + 1 < parts:
-            at = (p + 1) // 2 * 2
-            after = gz_v[at : at + 2, :chans, :].reshape(2 * chans, mid).T[:16].astype(F32)
-            if (p + 1) % 2:
-                after = swap_halves(after)
-        gz_v[p, 2 * chans : 2 * chans + 16, :] = jnp.where(row < 2, after, sums).astype(BF)
+    edges = gz_v[:, 2 * chans : 2 * chans + 16, :].astype(F32)
+    gz_v[:, 2 * chans : 2 * chans + 16, :] = jnp.where(row[None] < 2, edges, sums[None]).astype(BF)
     store(gz_out, gz_v, 4 * tiles, 2 * chans).start()
     for n in range(2 * tiles):
         store(gh_out, gh_v, n, 16 * n).wait()

time: 127 us -> 126 us (level)
  no operation moved by 1% of the time
where the time goes in v6:
time: 126 us
  waiting for transfers between devices  39.3 us (31%)
  starting transfers between devices  32.1 us (25%)
  Pallas kernels  28.4 us (23%)
  blocking collectives  23 us (18%)
  local copies, waits for them, and re-layouts  1.93 us (2%)
    all_to_all x1, waiting for transfers between devices, shards(): recv = lax.all_to_all(send, 'seq', 0, 0)  37.3 us
    all_to_all x1, blocking collectives, shards(): gz_recv = lax.all_to_all(gz_send, 'seq', 0, 0)  23 us
    pallas_call x5, Pallas kernels, stream(): pl.pallas_call(kernel, in_specs=[anywhere] * (n_in + n_small), out_specs=...  17.6 us
    pallas_call x1, Pallas kernels, spectral(): pl.pallas_call(spectral_kernel, out_shape=(jax.ShapeDtypeStruct((parts, 2...  10.9 us
    all_to_all x1, starting transfers between devices, shards(): recv = lax.all_to_all(send, 'seq', 0, 0)  8.81 us
    ppermute x5, starting transfers between devices, tree_step(): lax.ppermute(x, axis, [(i, i ^ step) for i in range(lax.axis_size(axis))])  8.6 us
    ppermute x3, starting transfers between devices, quarter_sum(): lax.ppermute(x, axis, [(i, (i + n * size // 4) % size) for i in range(siz...  6.6 us
    all_to_all x1, starting transfers between devices, shards(): gh_recv = lax.all_to_all(gh_send, 'seq', 0, 0)  4.66 us
  transfers between devices with their start and end apart: 12, of which 4 were waited for; matrix products, arithmetic and copies ran while one was open for 0% of the time, Pallas kernels for 18%

profile of v6, /device:TPU:0, one launch (start us, length us, event | category | flops | bytes accessed | tf_op | source)
XLA Modules:
  0.0 125.8 jit_solution(2170281325001700911)
XLA Ops:
  0.6 5.5 %pack.1 = bf16[32,400,128]{2,1,0:T(8,128)(2,1)} custom-call(bf16[256,2048]{1,0:T(8,128)(2,1)} %refs_0_.4, bf16[256,2048]{1,0:T(8,128)(2,1)} %refs_1_.5, f32[256,2048]{1,0:T(8,128)} %refs_2_.4, bf16[256,2048]{1,0:T(8,128)(2,1)} %refs_1_.8, bf16[256,2048]{1,0:T(8,128)(2,1)} %refs_2_.6, f32[3,2048]{1,0:T(4,128)} %refs_3_.6, f32[3,2048]{1,0:T(4,128)} %refs_4_.6), custom_call_target="tpu_custom_call" | custom-call | flops 9568256 | bytes 9568256 | tf_op jit(solution)/shard_map/pack/pallas_call | solution.py:317
  6.1 8.8 %all-to-all-start = ((bf16[32,400,128]{2,1,0:T(8,128)(2,1)}), bf16[32,400,128]{2,1,0:T(8,128)(2,1)}, u32[]{:S(2)}, u32[]{:S(2)}) async-start(bf16[32,400,128]{2,1,0:T(8,128)(2,1)} %pack.1), calls=%async_computation | async-start | bytes 6553600 | tf_op jit(solution)/shard_map/all_to_all | solution.py:454
  15.1 2.1 %collective-permute-start = (bf16[4,2048]{1,0:T(4,128)(2,1)S(1)}, bf16[4,2048]{1,0:T(4,128)(2,1)S(1)}, u32[]{:S(2)}, u32[]{:S(2)}) collective-permute-start(bf16[4,2048]{1,0:T(4,128)(2,1)S(1)} %get-tuple-element.32), channel_id=1, source_target_pairs={{0,4},{4,8},{8,12},{12,16},{16,20},{20,24},{24,28},{28,32},{32,36}... | collective-permute-start | bytes 49160 | tf_op jit(solution)/shard_map/ppermute | solution.py:456
  17.2 1.3 %collective-permute-start.1 = (bf16[4,2048]{1,0:T(4,128)(2,1)S(1)}, bf16[4,2048]{1,0:T(4,128)(2,1)S(1)}, u32[]{:S(2)}, u32[]{:S(2)}) collective-permute-start(bf16[4,2048]{1,0:T(4,128)(2,1)S(1)} %get-tuple-element.33), channel_id=1, source_target_pairs={{4,0},{8,4},{12,8},{16,12},{20,16},{24,20},{28,24},{32,28},{36,32}... | collective-permute-start | bytes 49160 | tf_op jit(solution)/shard_map/ppermute | solution.py:457
  18.5 1.2 copy-done.3
  19.7 1.3 %gate.1 = bf16[256,2048]{1,0:T(8,128)(2,1)} custom-call(bf16[256,2048]{1,0:T(8,128)(2,1)S(1)} %copy-done.2, bf16[256,2048]{1,0:T(8,128)(2,1)S(1)} %copy-done.3), custom_call_target="tpu_custom_call" | custom-call | flops 3145728 | bytes 3145728 | tf_op jit(solution)/shard_map/gate/pallas_call | solution.py:317
  21.0 37.3 %all-to-all-done.recv = bf16[32,400,128]{2,1,0:T(8,128)(2,1)} async-done(((bf16[32,400,128]{2,1,0:T(8,128)(2,1)}), bf16[32,400,128]{2,1,0:T(8,128)(2,1)}, u32[]{:S(2)}, u32[]{:S(2)}) %all-to-all-start) | async-done | bytes 3276832 | tf_op jit(solution)/shard_map/all_to_all | solution.py:454
  58.3 10.9 %spectral.1 = (bf16[32,144,128]{2,1,0:T(8,128)(2,1)}, bf16[32,128,128]{2,1,0:T(8,128)(2,1)}) custom-call(bf16[32,400,128]{2,1,0:T(8,128)(2,1)} %all-to-all-done.recv, bf16[512,256]{1,0:T(8,128)(2,1)} %constant.19.clone.refs_0_, bf16[2,256,256]{2,1,0:T(8,128)(2,1)} %constant.20.clone.refs_1_, bf16[2,256,256]{2,1,0:T(8,128)(2,1)} %constant.21.clone.refs_2_, ...), custom_call_target="tpu_custom_call" | custom-call | flops 5368709120 | bytes 7340032 | tf_op jit(solution)/shard_map/spectral/pallas_call | solution.py:207
  69.2 23.0 %all_to_all.15.refs_0_ = bf16[32,144,128]{2,1,0:T(8,128)(2,1)S(1)} all-to-all(bf16[32,144,128]{2,1,0:T(8,128)(2,1)} %get-tuple-element.34), channel_id=1, replica_groups=mesh['seq'=32,'chan'=4] {'seq'}, dimensions={0} | all-to-all | bytes 2359296 | tf_op jit(solution)/shard_map/all_to_all | solution.py:462
  92.2 4.7 %all-to-all-start.2 = ((bf16[32,128,128]{2,1,0:T(8,128)(2,1)}), bf16[32,128,128]{2,1,0:T(8,128)(2,1)}, u32[]{:S(2)}, u32[]{:S(2)}) async-start(bf16[32,128,128]{2,1,0:T(8,128)(2,1)} %get-tuple-element.48), calls=%async_computation.2 | async-start | bytes 2097152 | tf_op jit(solution)/shard_map/all_to_all | solution.py:464
  96.9 3.5 %taps.1 = f32[8,2048]{1,0:T(8,128)S(1)} custom-call(bf16[32,144,128]{2,1,0:T(8,128)(2,1)S(1)} %all_to_all.15.refs_0_, bf16[256,2048]{1,0:T(8,128)(2,1)S(1)} %copy-done, bf16[256,2048]{1,0:T(8,128)(2,1)S(1)} %copy-done.1, f32[3,2048]{1,0:T(4,128)S(1)} %copy-done.4, f32[3,2048]{1,0:T(4,128)S(1)} %copy-done.5, bf16[4,2048]{1,0:T(4,128)(2,1)S(1)} %collective-permute-done.refs_5_), custom_call_target="tpu_custom_call" | custom-call | flops 3342336 | bytes 3342336 | tf_op jit(solution)/shard_map/taps/pallas_call | solution.py:317
  100.4 0.3 collective-permute-start.2
  100.8 1.6 %collective-permute-start.6 = (f32[8,128]{1,0:T(8,128)S(1)}, f32[8,128]{1,0:T(8,128)S(1)}, u32[]{:S(2)}, u32[]{:S(2)}) collective-permute-start(f32[8,128]{1,0:T(8,128)S(1)} %broadcast_in_dim.2), channel_id=1, source_target_pairs={{0,1},{1,0},{2,3},{3,2},{4,5},{5,4},{6,7},{7,6},{8,9},{9,8},{10,11... | collective-permute-start | bytes 12296 | tf_op jit(solution)/shard_map/ppermute | solution.py:429
  102.4 3.4 %collective-permute-start.3 = (f32[8,2048]{1,0:T(8,128)S(1)}, f32[8,2048]{1,0:T(8,128)S(1)}, u32[]{:S(2)}, u32[]{:S(2)}) collective-permute-start(f32[8,2048]{1,0:T(8,128)S(1)} %add.30), channel_id=1, source_target_pairs={{0,64},{4,68},{8,72},{12,76},{16,80},{20,84},{24,88},{28,92},{32,9... | collective-permute-start | bytes 196616 | tf_op jit(solution)/shard_map/ppermute | solution.py:434
  105.8 0.6 collective-permute-start.4
  106.4 2.6 %collective-permute-start.5 = (f32[8,2048]{1,0:T(8,128)S(1)}, f32[8,2048]{1,0:T(8,128)S(1)}, u32[]{:S(2)}, u32[]{:S(2)}) collective-permute-start(f32[8,2048]{1,0:T(8,128)S(1)} %add.30), channel_id=1, source_target_pairs={{0,96},{4,100},{8,104},{12,108},{16,112},{20,116},{24,120},{28,124... | collective-permute-start | bytes 196616 | tf_op jit(solution)/shard_map/ppermute | solution.py:434
  109.0 4.8 %inputs.1 = (bf16[256,2048]{1,0:T(8,128)(2,1)}, bf16[256,2048]{1,0:T(8,128)(2,1)}) custom-call(bf16[32,144,128]{2,1,0:T(8,128)(2,1)S(1)} %all_to_all.15.refs_0_, bf16[256,2048]{1,0:T(8,128)(2,1)S(1)} %copy-done, bf16[256,2048]{1,0:T(8,128)(2,1)S(1)} %copy-done.1, f32[3,2048]{1,0:T(4,128)S(1)} %copy-done.4, f32[3,2048]{1,0:T(4,128)S(1)} %copy-done.5, ...), custom_call_target="tpu_custom_call" | custom-call | flops 5373952 | bytes 5373952 | tf_op jit(solution)/shard_map/inputs/pallas_call | solution.py:317
  113.8 1.4 %collective-permute-done.4 = f32[8,2048]{1,0:T(8,128)S(1)} collective-permute-done((f32[8,2048]{1,0:T(8,128)S(1)}, f32[8,2048]{1,0:T(8,128)S(1)}, u32[]{:S(2)}, u32[]{:S(2)}) %collective-permute-start.4) | collective-permute-done | bytes 65568 | tf_op jit(solution)/shard_map/ppermute | solution.py:434
  115.2 1.4 %collective-permute-start.7 = (f32[8,2048]{1,0:T(8,128)S(1)}, f32[8,2048]{1,0:T(8,128)S(1)}, u32[]{:S(2)}, u32[]{:S(2)}) collective-permute-start(f32[8,2048]{1,0:T(8,128)S(1)} %add_add_fusion), channel_id=1, source_target_pairs={{0,8},{4,12},{8,0},{12,4},{16,24},{20,28},{24,16},{28,20},{32,40},... | collective-permute-start | bytes 196616 | tf_op jit(solution)/shard_map/ppermute | solution.py:429
  116.6 2.8 %collective-permute-start.8 = (f32[8,128]{1,0:T(8,128)S(1)}, f32[8,128]{1,0:T(8,128)S(1)}, u32[]{:S(2)}, u32[]{:S(2)}) collective-permute-start(f32[8,128]{1,0:T(8,128)S(1)} %broadcast_add_fusion), channel_id=1, source_target_pairs={{0,3},{1,2},{2,1},{3,0},{4,7},{5,6},{6,5},{7,4},{8,11},{9,10},{10,... | collective-permute-start | bytes 12296 | tf_op jit(solution)/shard_map/ppermute | solution.py:429
  119.6 2.6 %collective-permute-start.9 = (f32[8,2048]{1,0:T(8,128)S(1)}, f32[8,2048]{1,0:T(8,128)S(1)}, u32[]{:S(2)}, u32[]{:S(2)}) collective-permute-start(f32[8,2048]{1,0:T(8,128)S(1)} %add.35), channel_id=1, source_target_pairs={{0,24},{4,28},{8,16},{12,20},{16,8},{20,12},{24,0},{28,4},{32,56},... | collective-permute-start | bytes 196616 | tf_op jit(solution)/shard_map/ppermute | solution.py:429
  122.1 2.5 %clip.1 = f32[256,2048]{1,0:T(8,128)} custom-call(bf16[32,128,128]{2,1,0:T(8,128)(2,1)} %all-to-all-done.2.refs_0_, f32[8,128]{1,0:T(8,128)S(1)} %rsqrt_minimum_fusion.refs_1_), custom_call_target="tpu_custom_call" | custom-call | flops 3145728 | bytes 3145728 | tf_op jit(solution)/shard_map/clip/pallas_call | solution.py:317
  124.6 0.5 collective-permute-done.9
  125.1 0.6 fusion.2
  (31 shorter events, 0.5 us)
Async XLA Ops:
  6.1 8.9 %copy-start = (bf16[256,2048]{1,0:T(8,128)(2,1)S(1)}, bf16[256,2048]{1,0:T(8,128)(2,1)}, u32[]{:S(2)}) copy-start(bf16[256,2048]{1,0:T(8,128)(2,1)} %refs_1_.8) | copy-start | bytes 3145732
  6.1 8.9 %copy-start.1 = (bf16[256,2048]{1,0:T(8,128)(2,1)S(1)}, bf16[256,2048]{1,0:T(8,128)(2,1)}, u32[]{:S(2)}) copy-start(bf16[256,2048]{1,0:T(8,128)(2,1)} %refs_2_.6) | copy-start | bytes 3145732
  6.1 12.4 %copy-start.2 = (bf16[256,2048]{1,0:T(8,128)(2,1)S(1)}, bf16[256,2048]{1,0:T(8,128)(2,1)}, u32[]{:S(2)}) copy-start(bf16[256,2048]{1,0:T(8,128)(2,1)} %refs_0_.4) | copy-start | bytes 3145732
  6.1 52.2 %all-to-all-start = ((bf16[32,400,128]{2,1,0:T(8,128)(2,1)}), bf16[32,400,128]{2,1,0:T(8,128)(2,1)}, u32[]{:S(2)}, u32[]{:S(2)}) async-start(bf16[32,400,128]{2,1,0:T(8,128)(2,1)} %pack.1), calls=%async_computation | async-start | bytes 6553600 | tf_op jit(solution)/shard_map/all_to_all | solution.py:454
  15.1 54.1 %collective-permute-start = (bf16[4,2048]{1,0:T(4,128)(2,1)S(1)}, bf16[4,2048]{1,0:T(4,128)(2,1)S(1)}, u32[]{:S(2)}, u32[]{:S(2)}) collective-permute-start(bf16[4,2048]{1,0:T(4,128)(2,1)S(1)} %get-tuple-element.32), channel_id=1, source_target_pairs={{0,4},{4,8},{8,12},{12,16},{16,20},{20,24},{24,28},{28,32},{32,36}... | collective-permute-start | bytes 49160 | tf_op jit(solution)/shard_map/ppermute | solution.py:456
  17.2 52.0 %collective-permute-start.1 = (bf16[4,2048]{1,0:T(4,128)(2,1)S(1)}, bf16[4,2048]{1,0:T(4,128)(2,1)S(1)}, u32[]{:S(2)}, u32[]{:S(2)}) collective-permute-start(bf16[4,2048]{1,0:T(4,128)(2,1)S(1)} %get-tuple-element.33), channel_id=1, source_target_pairs={{4,0},{8,4},{12,8},{16,12},{20,16},{24,20},{28,24},{32,28},{36,32}... | collective-permute-start | bytes 49160 | tf_op jit(solution)/shard_map/ppermute | solution.py:457
  18.5 1.2 copy-start.3
  69.2 27.7 %copy-start.4 = (f32[3,2048]{1,0:T(4,128)S(1)}, f32[3,2048]{1,0:T(4,128)}, u32[]{:S(2)}) copy-start(f32[3,2048]{1,0:T(4,128)} %refs_3_.6) | copy-start | bytes 73732
  69.2 27.7 %copy-start.5 = (f32[3,2048]{1,0:T(4,128)S(1)}, f32[3,2048]{1,0:T(4,128)}, u32[]{:S(2)}) copy-start(f32[3,2048]{1,0:T(4,128)} %refs_4_.6) | copy-start | bytes 73732
  92.2 27.4 %all-to-all-start.2 = ((bf16[32,128,128]{2,1,0:T(8,128)(2,1)}), bf16[32,128,128]{2,1,0:T(8,128)(2,1)}, u32[]{:S(2)}, u32[]{:S(2)}) async-start(bf16[32,128,128]{2,1,0:T(8,128)(2,1)} %get-tuple-element.48), calls=%async_computation.2 | async-start | bytes 2097152 | tf_op jit(solution)/shard_map/all_to_all | solution.py:464
  100.4 2.0 %collective-permute-start.2 = (f32[8,2048]{1,0:T(8,128)S(1)}, f32[8,2048]{1,0:T(8,128)S(1)}, u32[]{:S(2)}, u32[]{:S(2)}) collective-permute-start(f32[8,2048]{1,0:T(8,128)S(1)} %taps.1), channel_id=1, source_target_pairs={{0,4},{4,0},{8,12},{12,8},{16,20},{20,16},{24,28},{28,24},{32,36},... | collective-permute-start | bytes 196616 | tf_op jit(solution)/shard_map/ppermute | solution.py:429
  100.8 8.2 %collective-permute-start.6 = (f32[8,128]{1,0:T(8,128)S(1)}, f32[8,128]{1,0:T(8,128)S(1)}, u32[]{:S(2)}, u32[]{:S(2)}) collective-permute-start(f32[8,128]{1,0:T(8,128)S(1)} %broadcast_in_dim.2), channel_id=1, source_target_pairs={{0,1},{1,0},{2,3},{3,2},{4,5},{5,4},{6,7},{7,6},{8,9},{9,8},{10,11... | collective-permute-start | bytes 12296 | tf_op jit(solution)/shard_map/ppermute | solution.py:429
  102.4 11.4 %collective-permute-start.3 = (f32[8,2048]{1,0:T(8,128)S(1)}, f32[8,2048]{1,0:T(8,128)S(1)}, u32[]{:S(2)}, u32[]{:S(2)}) collective-permute-start(f32[8,2048]{1,0:T(8,128)S(1)} %add.30), channel_id=1, source_target_pairs={{0,64},{4,68},{8,72},{12,76},{16,80},{20,84},{24,88},{28,92},{32,9... | collective-permute-start | bytes 196616 | tf_op jit(solution)/shard_map/ppermute | solution.py:434
  105.8 9.4 %collective-permute-start.4 = (f32[8,2048]{1,0:T(8,128)S(1)}, f32[8,2048]{1,0:T(8,128)S(1)}, u32[]{:S(2)}, u32[]{:S(2)}) collective-permute-start(f32[8,2048]{1,0:T(8,128)S(1)} %add.30), channel_id=1, source_target_pairs={{0,32},{4,36},{8,40},{12,44},{16,48},{20,52},{24,56},{28,60},{32,6... | collective-permute-start | bytes 196616 | tf_op jit(solution)/shard_map/ppermute | solution.py:434
  106.4 8.8 %collective-permute-start.5 = (f32[8,2048]{1,0:T(8,128)S(1)}, f32[8,2048]{1,0:T(8,128)S(1)}, u32[]{:S(2)}, u32[]{:S(2)}) collective-permute-start(f32[8,2048]{1,0:T(8,128)S(1)} %add.30), channel_id=1, source_target_pairs={{0,96},{4,100},{8,104},{12,108},{16,112},{20,116},{24,120},{28,124... | collective-permute-start | bytes 196616 | tf_op jit(solution)/shard_map/ppermute | solution.py:434
  115.2 4.3 %collective-permute-start.7 = (f32[8,2048]{1,0:T(8,128)S(1)}, f32[8,2048]{1,0:T(8,128)S(1)}, u32[]{:S(2)}, u32[]{:S(2)}) collective-permute-start(f32[8,2048]{1,0:T(8,128)S(1)} %add_add_fusion), channel_id=1, source_target_pairs={{0,8},{4,12},{8,0},{12,4},{16,24},{20,28},{24,16},{28,20},{32,40},... | collective-permute-start | bytes 196616 | tf_op jit(solution)/shard_map/ppermute | solution.py:429
  116.6 5.5 %collective-permute-start.8 = (f32[8,128]{1,0:T(8,128)S(1)}, f32[8,128]{1,0:T(8,128)S(1)}, u32[]{:S(2)}, u32[]{:S(2)}) collective-permute-start(f32[8,128]{1,0:T(8,128)S(1)} %broadcast_add_fusion), channel_id=1, source_target_pairs={{0,3},{1,2},{2,1},{3,0},{4,7},{5,6},{6,5},{7,4},{8,11},{9,10},{10,... | collective-permute-start | bytes 12296 | tf_op jit(solution)/shard_map/ppermute | solution.py:429
  119.6 5.6 %collective-permute-start.9 = (f32[8,2048]{1,0:T(8,128)S(1)}, f32[8,2048]{1,0:T(8,128)S(1)}, u32[]{:S(2)}, u32[]{:S(2)}) collective-permute-start(f32[8,2048]{1,0:T(8,128)S(1)} %add.35), channel_id=1, source_target_pairs={{0,24},{4,28},{8,16},{12,20},{16,8},{20,12},{24,0},{28,4},{32,56},... | collective-permute-start | bytes 196616 | tf_op jit(solution)/shard_map/ppermute | solution.py:429
